TPU v7x, 32 devices: a whole 2x2x4 slice. The times are simulated.
32 devices in a mesh: dp: 16 (over z, y, core), grp: 2 (over x).
Axes of the slice: x: 2, y: 2, z: 4, core: 2. Of those that a mesh axis runs over, the one named last changes fastest.
Arguments:
- feature_maps: bfloat16 [2, 32, 56, 3584], P(None, ('dp', 'grp')), may hold values from -200 to 200, as said below
- output_grads: bfloat16 [2, 32, 56, 3584], P(None, ('dp', 'grp')), may hold values from -200 to 200, as said below
Outputs:
- precond: float32 [2, 64, 576], replicated
Inputs may be any that keep to these rules, and one draw needn't show every extreme that they name: `feature_maps`: real values. `output_grads`: real values.
All inputs are finite; a program needn't handle non-finite values.
Results may differ from a plain program's by a relative error of at most 0.0003.
Values sent between devices are 32-bit elements; how exact they have to be, the bound alone decides.
No kernel may reach another device: no remote copies, remote signals or barrier semaphores. Data moves between devices by JAX's collectives and lax.ppermute only.
A program may use at most 128 MiB of HBM per device.

v0:
```python
import jax
import jax.numpy as jnp
from jax import lax
from jax.sharding import PartitionSpec as P

C = 64
MAP_W = 56
NS_ITERS = 2


damping_factor = 0.1


def patch_rows(feature):
    height = feature.shape[0]
    cube = feature.reshape(height, MAP_W, C)
    padded = jnp.pad(cube, ((1, 1), (1, 1), (0, 0)))
    pieces = [
        padded[row_tap : row_tap + height, col_tap : col_tap + MAP_W, :]
        for row_tap in range(3)
        for col_tap in range(3)
    ]
    return jnp.concatenate(pieces, axis=-1).reshape(height * MAP_W, 9 * C)


def damped(factor):
    size_n = factor.shape[-1]
    identity_mat = jnp.eye(size_n, dtype=jnp.float32)
    return factor + damping_factor * jnp.trace(factor) / size_n * identity_mat


def newton_inverse(matrix):
    size_n = matrix.shape[-1]
    identity_mat = jnp.eye(size_n, dtype=jnp.float32)
    current = identity_mat / jnp.sqrt(jnp.sum(matrix * matrix))
    for sweep in range(NS_ITERS):
        product = jnp.dot(matrix, current, precision=lax.Precision.HIGHEST)
        current = jnp.dot(current, 2.0 * identity_mat - product, precision=lax.Precision.HIGHEST)
    return current


def precondition(cov_a, cov_g, grad_w):
    inverse_a = newton_inverse(damped(cov_a))
    inverse_g = newton_inverse(damped(cov_g))
    left = jnp.dot(inverse_g, grad_w, precision=lax.Precision.HIGHEST)
    return jnp.dot(left, inverse_a, precision=lax.Precision.HIGHEST)


def shards(feature_maps, output_grads):
    levels = feature_maps.shape[0]
    contract = (((0,), (0,)), ((), ()))
    partial_a = []
    partial_g = []
    partial_w = []
    for layer_index in range(levels):
        patches = patch_rows(feature_maps[layer_index, 0])
        grads = output_grads[layer_index, 0].reshape(-1, C)
        partial_a.append(
            lax.dot_general(patches, patches, contract, preferred_element_type=jnp.float32)
        )
        partial_g.append(
            lax.dot_general(grads, grads, contract, preferred_element_type=jnp.float32)
        )
        partial_w.append(
            lax.dot_general(grads, patches, contract, preferred_element_type=jnp.float32)
        )
    local_rows = feature_maps.shape[2] * MAP_W
    total_rows = local_rows * feature_maps.shape[1] * lax.axis_size("dp") * lax.axis_size("grp")
    stack_a = jnp.stack(partial_a)
    stack_g = jnp.stack(partial_g)
    stack_w = jnp.stack(partial_w)
    summed_first, summed_g, summed_w = lax.psum((stack_a, stack_g, stack_w), ("dp", "grp"))
    owned_levels = summed_g.shape[0]
    scale = 1.0 / total_rows
    cov_a = summed_first * scale
    cov_g = summed_g * scale
    grad_w = summed_w * scale
    results = jnp.stack(
        [precondition(cov_a[index], cov_g[index], grad_w[index]) for index in range(owned_levels)]
    )
    return results


def solution(mesh):
    placed = (P(None, ("dp", "grp"), None, None), P(None, ("dp", "grp"), None, None))
    return jax.shard_map(shards, mesh=mesh, in_specs=placed, out_specs=P(), check_vma=False)
```

profile of v0, /device:TPU:0, one launch (start us, length us, event | category | flops | bytes accessed | tf_op | source)
XLA Modules:
  0.0 277.1 jit_solution(12843781139318456501)
XLA Ops:
  6.5 1.2 fusion.72
  7.7 0.5 reshape_squeeze.14
  8.2 1.3 concatenate.52
  9.5 0.4 reshape_squeeze.15
  10.0 1.4 concatenate.62
  11.4 1.9 fusion.73
  13.3 0.4 reshape_squeeze.12
  13.7 1.5 reshape_squeeze.13
  15.2 3.9 %pad_slice_fusion = (bf16[56,56,64]{2,1,0:T(8,128)(2,1)}, bf16[56,56,64]{2,1,0:T(8,128)(2,1)}, bf16[56,56,64]{2,1,0:T(8,128)(2,1)}, bf16[56,56,64]{2,1,0:T(8,128...) fusion(bf16[56,56,64]{2,1,0:T(8,128)(2,1)S(1)} %reshape_squeeze.15), kind=kLoop, calls=%fused_computation.57 | loop fusion | bytes 3612672 | tf_op jit(solution)/shard_map/slice | solution.py:19
  19.1 9.3 %concatenate.69 = bf16[56,56,576]{2,1,0:T(8,128)(2,1)} concatenate(bf16[56,56,64]{2,1,0:T(8,128)(2,1)} %get-tuple-element.32, bf16[56,56,64]{2,1,0:T(8,128)(2,1)} %get-tuple-element.26, bf16[56,56,64]{2,1,0:T(8,128)(2,1)} %get-tuple-element.27, bf16[56,56,64]{2,1,0:T(8,128)(2,1)} %get-tuple-element.28, bf16[56,56,64]{2,1,0:T(8,128)(2,1)S(1)} %reshape_squeeze.15, ...), dimensions={2} | concatenate | bytes 7225344 | tf_op jit(solution)/shard_map/concatenate | solution.py:23
  28.4 7.6 %convolution_bitcast_fusion = f32[1,576,576]{2,1,0:T(8,128)} fusion(bf16[56,56,576]{2,1,0:T(8,128)(2,1)} %concatenate.69), kind=kOutput, calls=%fused_computation.25 | convolution fusion | flops 2080899072 | bytes 4939776 | tf_op jit(solution)/shard_map/dot_general | solution.py:59
  36.0 3.3 %pad_slice_fusion.8 = (bf16[56,56,64]{2,1,0:T(8,128)(2,1)S(1)}, bf16[56,56,64]{2,1,0:T(8,128)(2,1)}, bf16[56,56,64]{2,1,0:T(8,128)(2,1)}, bf16[56,56,64]{2,1,0:T...) fusion(bf16[56,56,64]{2,1,0:T(8,128)(2,1)S(1)} %reshape_squeeze.14), kind=kLoop, calls=%fused_computation.65 | loop fusion | bytes 3612672 | tf_op jit(solution)/shard_map/slice | solution.py:19
  39.3 0.9 copy-done.2
  40.2 9.2 %concatenate.68 = bf16[56,56,576]{2,1,0:T(8,128)(2,1)} concatenate(bf16[56,56,64]{2,1,0:T(8,128)(2,1)} %get-tuple-element.22, bf16[56,56,64]{2,1,0:T(8,128)(2,1)} %get-tuple-element.16, bf16[56,56,64]{2,1,0:T(8,128)(2,1)} %get-tuple-element.17, bf16[56,56,64]{2,1,0:T(8,128)(2,1)} %get-tuple-element.18, bf16[56,56,64]{2,1,0:T(8,128)(2,1)S(1)} %reshape_squeeze.14, ...), dimensions={2} | concatenate | bytes 7225344 | tf_op jit(solution)/shard_map/concatenate | solution.py:23
  49.3 7.8 %convolution_bitcast_fusion.1 = f32[1,576,576]{2,1,0:T(8,128)} fusion(bf16[56,56,576]{2,1,0:T(8,128)(2,1)} %concatenate.68), kind=kOutput, calls=%fused_computation.26 | convolution fusion | flops 2080899072 | bytes 4939776 | tf_op jit(solution)/shard_map/dot_general | solution.py:59
  57.2 9.2 %concatenate.67 = bf16[3136,576]{1,0:T(8,128)(2,1)} concatenate(bf16[3136,64]{1,0:T(8,128)(2,1)} %bitcast.135, bf16[3136,64]{1,0:T(8,128)(2,1)S(1)} %bitcast.129, bf16[3136,64]{1,0:T(8,128)(2,1)} %bitcast.130, bf16[3136,64]{1,0:T(8,128)(2,1)} %bitcast.131, bf16[3136,64]{1,0:T(8,128)(2,1)} %concatenate.62, bf16[3136,64]{1,0:T(8,128)(2,1)} %bitcast.132, ...), dimensions={1} | concatenate | bytes 7225344 | tf_op jit(solution)/shard_map/concatenate | solution.py:23
  66.3 3.0 %convolution_bitcast_fusion.2 = f32[1,64,576]{2,1,0:T(8,128)S(1)} fusion(bf16[3136,576]{1,0:T(8,128)(2,1)} %concatenate.67, bf16[3136,64]{1,0:T(8,128)(2,1)S(1)} %reshape_squeeze.13), kind=kOutput, calls=%fused_computation.27 | convolution fusion | flops 231211008 | bytes 4161536 | tf_op jit(solution)/shard_map/dot_general | solution.py:65
  69.4 9.2 %concatenate.57 = bf16[3136,576]{1,0:T(8,128)(2,1)} concatenate(bf16[3136,64]{1,0:T(8,128)(2,1)} %bitcast.143, bf16[3136,64]{1,0:T(8,128)(2,1)S(1)} %bitcast.137, bf16[3136,64]{1,0:T(8,128)(2,1)} %bitcast.138, bf16[3136,64]{1,0:T(8,128)(2,1)} %bitcast.139, bf16[3136,64]{1,0:T(8,128)(2,1)} %concatenate.52, bf16[3136,64]{1,0:T(8,128)(2,1)} %bitcast.140, ...), dimensions={1} | concatenate | bytes 7225344 | tf_op jit(solution)/shard_map/concatenate | solution.py:23
  78.6 3.1 %convolution_bitcast_fusion.3 = f32[1,64,576]{2,1,0:T(8,128)S(1)} fusion(bf16[3136,576]{1,0:T(8,128)(2,1)} %concatenate.57, bf16[3136,64]{1,0:T(8,128)(2,1)S(1)} %reshape_squeeze.12), kind=kOutput, calls=%fused_computation.28 | convolution fusion | flops 231211008 | bytes 4161536 | tf_op jit(solution)/shard_map/dot_general | solution.py:65
  81.6 0.7 pad_maximum_fusion.1
  82.4 1.8 pad_maximum_fusion
  84.2 0.4 convolution_bitcast_fusion.7
  84.6 0.4 convolution_bitcast_fusion.6
  85.0 42.9 %psum.21 = f32[2,64,64]{2,1,0:T(8,128)S(1)} all-reduce(f32[2,64,64]{2,1,0:T(8,128)S(1)} %pad_maximum_fusion.3), channel_id=1, replica_groups=mesh['dp'=16,'grp'=2] {'dp','grp'}, use_global_device_ids=true, to_apply=%region_0.1 | all-reduce | flops 8192 | bytes 65536 | tf_op jit(solution)/shard_map/psum | solution.py:72
  128.0 0.7 select_reduce_fusion.3
  129.9 0.7 multiply_reduce_fusion.3
  132.0 0.2 convolution_subtract_fusion.3
  132.3 0.2 convolution_subtract_fusion.1
  132.6 0.2 convolution_subtract_fusion.2
  133.0 0.2 convolution_subtract_fusion
  133.3 92.3 %all-reduce.5.cloned.1.call-done = (f32[2,64,576]{2,1,0:T(8,128)}, f32[2,576,576]{2,1,0:T(8,128)}) async-done(((f32[2,64,576]{2,1,0:T(8,128)}, f32[2,576,576]{2,1,0:T(8,128)}), (f32[2,64,576]{2,1,0:T(8,128)}, f32[2,576,576]{2,1,0:T(8,128)})) %all-reduce.5.cloned.1.call-update) | async-done | bytes 2949136 | tf_op jit(solution)/shard_map/psum | solution.py:72
  225.7 1.0 broadcast_multiply_fusion.1
  226.7 0.3 fusion.34
  227.0 0.3 fusion.35
  227.3 2.1 broadcast_multiply_fusion
  229.4 0.8 select_reduce_fusion.1
  231.5 1.1 multiply_reduce_fusion.1
  234.0 3.7 %select_subtract_fusion.3 = f32[576,576]{1,0:T(8,128)S(1)} fusion(f32[2,576,576]{2,1,0:T(8,128)S(1)} %broadcast_multiply_fusion, f32[]{:T(128)S(6)} %sqrt.13, f32[]{:T(128)S(6)} %div.39), kind=kOutput, calls=%fused_computation.4 | convolution fusion | flops 2295889920 | bytes 2801672 | tf_op jit(solution)/shard_map/dot_general | solution.py:37
  237.7 4.1 %fusion.4 = f32[576,576]{1,0:T(8,128)S(1)} fusion(f32[576,576]{1,0:T(8,128)S(1)} %select_subtract_fusion.3, f32[]{:T(128)S(6)} %sqrt.13), kind=kOutput, calls=%fused_computation.9 | convolution fusion | flops 2293899264 | bytes 2654212 | tf_op jit(solution)/shard_map/dot_general | solution.py:38
  241.8 4.4 %fusion.14 = f32[576,576]{1,0:T(8,128)S(1)} fusion(f32[576,576]{1,0:T(8,128)S(1)} %fusion.4, f32[2,576,576]{2,1,0:T(8,128)S(1)} %broadcast_multiply_fusion, f32[]{:T(128)S(6)} %div.39), kind=kOutput, calls=%fused_computation.37 | convolution fusion | flops 2294231040 | bytes 4276228 | tf_op jit(solution)/shard_map/dot_general | solution.py:37
  246.3 4.3 %fusion.12 = f32[576,576]{1,0:T(8,128)S(1)} fusion(f32[576,576]{1,0:T(8,128)S(1)} %fusion.4, f32[576,576]{1,0:T(8,128)S(1)} %fusion.14), kind=kOutput, calls=%fused_computation.13 | convolution fusion | flops 2294231040 | bytes 3981312 | tf_op jit(solution)/shard_map/dot_general | solution.py:38
  250.6 3.7 %select_subtract_fusion.1 = f32[576,576]{1,0:T(8,128)S(1)} fusion(f32[2,576,576]{2,1,0:T(8,128)S(1)} %broadcast_multiply_fusion, f32[]{:T(128)S(6)} %sqrt.15, f32[]{:T(128)S(6)} %div.45), kind=kOutput, calls=%fused_computation.2 | convolution fusion | flops 2295889920 | bytes 2801672 | tf_op jit(solution)/shard_map/dot_general | solution.py:37
  254.3 4.4 %fusion = f32[576,576]{1,0:T(8,128)S(1)} fusion(f32[576,576]{1,0:T(8,128)S(1)} %select_subtract_fusion.1, f32[]{:T(128)S(6)} %sqrt.15), kind=kOutput, calls=%fused_computation.5 | convolution fusion | flops 2293899264 | bytes 2654212 | tf_op jit(solution)/shard_map/dot_general | solution.py:38
  258.6 4.2 %fusion.15 = f32[576,576]{1,0:T(8,128)S(1)} fusion(f32[576,576]{1,0:T(8,128)S(1)} %fusion, f32[2,576,576]{2,1,0:T(8,128)S(1)} %broadcast_multiply_fusion, f32[]{:T(128)S(6)} %div.45), kind=kOutput, calls=%fused_computation.38 | convolution fusion | flops 2294231040 | bytes 4276228 | tf_op jit(solution)/shard_map/dot_general | solution.py:37
  262.9 4.3 %fusion.13 = f32[576,576]{1,0:T(8,128)S(1)} fusion(f32[576,576]{1,0:T(8,128)S(1)} %fusion, f32[576,576]{1,0:T(8,128)S(1)} %fusion.15), kind=kOutput, calls=%fused_computation.14 | convolution fusion | flops 2294231040 | bytes 3981312 | tf_op jit(solution)/shard_map/dot_general | solution.py:38
  267.1 1.0 convolution_bitcast_fusion.5
  268.1 1.0 convolution_bitcast_fusion.4
  269.1 0.7 pad_maximum_fusion.2
  (21 shorter events, 0.7 us)
Async XLA Ops:
  6.5 219.1 %all-reduce.5.cloned.1.call-start = ((), (), s32[]{:S(2)}) async-start(), calls=%async_computation | async-start | bytes 6553600 | tf_op jit(solution)/shard_map/psum | solution.py:72
  39.3 0.9 copy-start.2
  49.3 7.8 %copy-start = (bf16[56,56,64]{2,1,0:T(8,128)(2,1)S(1)}, bf16[56,56,64]{2,1,0:T(8,128)(2,1)}, u32[]{:S(2)}) copy-start(bf16[56,56,64]{2,1,0:T(8,128)(2,1)} %get-tuple-element.25) | copy-start | bytes 1204228
  49.3 7.8 %copy-start.1 = (bf16[56,56,64]{2,1,0:T(8,128)(2,1)S(1)}, bf16[56,56,64]{2,1,0:T(8,128)(2,1)}, u32[]{:S(2)}) copy-start(bf16[56,56,64]{2,1,0:T(8,128)(2,1)} %get-tuple-element.26) | copy-start | bytes 1204228
  66.3 3.0 %copy-start.3 = (bf16[56,56,64]{2,1,0:T(8,128)(2,1)S(1)}, bf16[56,56,64]{2,1,0:T(8,128)(2,1)}, u32[]{:S(2)}) copy-start(bf16[56,56,64]{2,1,0:T(8,128)(2,1)} %copy-done.2) | copy-start | bytes 1204228
  66.3 3.1 %copy-start.4 = (bf16[56,56,64]{2,1,0:T(8,128)(2,1)S(1)}, bf16[56,56,64]{2,1,0:T(8,128)(2,1)}, u32[]{:S(2)}) copy-start(bf16[56,56,64]{2,1,0:T(8,128)(2,1)} %get-tuple-element.16) | copy-start | bytes 1204228
  78.6 3.8 %copy-start.5 = (f32[1,576,576]{2,1,0:T(8,128)S(1)}, f32[1,576,576]{2,1,0:T(8,128)}, u32[]{:S(2)}) copy-start(f32[1,576,576]{2,1,0:T(8,128)} %convolution_bitcast_fusion) | copy-start | bytes 3981316
  78.6 3.8 %copy-start.6 = (f32[1,576,576]{2,1,0:T(8,128)S(1)}, f32[1,576,576]{2,1,0:T(8,128)}, u32[]{:S(2)}) copy-start(f32[1,576,576]{2,1,0:T(8,128)} %convolution_bitcast_fusion.1) | copy-start | bytes 3981316
Sparse Core Ops, SparseCore 0:
  84.4 141.2 all-reduce.4
where the time goes:
time: 282 us; the launch traced here: 277 us
  waiting for transfers between devices  92.4 us (33%)
  matrix products  59.2 us (21%)
  local copies, waits for them, and re-layouts  53.5 us (19%)
  blocking collectives  42.9 us (15%)
  between operations  19.5 us (7%)
  other arithmetic  9.69 us (3%)
    psum x1, waiting for transfers between devices, shards(): lax.psum((stack_a, stack_g, stack_w), ('dp', 'grp'))  92.3 us
    psum x1, blocking collectives, shards(): lax.psum((stack_a, stack_g, stack_w), ('dp', 'grp'))  42.9 us
    concatenate x6, local copies, waits for them, and re-layouts, patch_rows(): return jnp.concatenate(pieces, axis=-1).reshape(height * MAP_W, 9 * C)  39.5 us
    dot_general x8, matrix products, newton_inverse(): jnp.dot(current, 2.0 * identity_mat - product, precision=lax.Precision.HI...  17.6 us
    dot_general x8, matrix products, newton_inverse(): product = jnp.dot(matrix, current, precision=lax.Precision.HIGHEST)  16.7 us
    dot_general x2, matrix products, shards(): lax.dot_general(patches, patches, contract, preferred_element_type=jnp.fl...  15.5 us
    slice x2, local copies, waits for them, and re-layouts, patch_rows(): padded[row_tap:row_tap + height, col_tap:col_tap + MAP_W, :]  7.15 us
    dot_general x2, matrix products, shards(): lax.dot_general(grads, patches, contract, preferred_element_type=jnp.floa...  6.09 us
  transfers between devices with their start and end apart: 1, of which 1 were waited for; matrix products, arithmetic and copies ran while one was open for 1% of the time, Pallas kernels for 0%

commit v1 on v0

v1 whole, which is shorter than its diff:
```python
import functools

import jax
import jax.numpy as jnp
import numpy as np
from jax import lax
from jax.experimental import pallas as pl
from jax.experimental.pallas import tpu as pltpu
from jax.sharding import PartitionSpec as P

C = 64
TAPS = 9
PAIR = 2 * C
ROW = 64
NPAIR = 20
QUART = 5
DAMP = 0.1
F32 = jnp.float32
BF16 = jnp.bfloat16

PAIRS = (
    "x1m", "x1z", "cc1", "x2m", "x2z",
    "cc2", "x22", "x0z", "cc0", "r0z",
    "r1z", "k0", "k1", "w0z", "w1z",
    "w2z", "h0", "h1", "h2", "gg",
)
PLACE = {name: index for index, name in enumerate(PAIRS)}


def contract0(a, b):
    return lax.dot_general(a, b, (((0,), (0,)), ((), ())), preferred_element_type=F32)


def chip_place():
    dp = lax.axis_index("dp")
    core = lax.rem(dp, 2)
    second = lax.rem(dp // 2, 2)
    first = lax.axis_index("grp")
    return core, first, second


def slot_of(quarter, layer, first, second):
    mine_first = first ^ (quarter // 2)
    mine_second = second ^ (quarter % 2)
    major = jnp.where(layer == 0, mine_first, mine_second)
    minor = jnp.where(layer == 0, mine_second, mine_first)
    return 2 * major + minor


def local_kernel(height, width, x_hbm, g_hbm, send_ref, keep_ref, xbuf, gbuf, shifted, lhs_t, edges, sems):
    core, first, second = chip_place()
    wp = width // 2
    rows = wp * ROW
    layers = [1 - core, core]
    copies = []
    for i in range(2):
        copies.append(
            (
                pltpu.make_async_copy(x_hbm.at[layers[i], 0], xbuf.at[i], sems.at[2 * i]),
                pltpu.make_async_copy(g_hbm.at[layers[i], 0], gbuf.at[i], sems.at[2 * i + 1]),
            )
        )
    for pair in copies:
        for one in pair:
            one.start()
    for d in range(4):
        shifted[d, 0:ROW, :] = jnp.zeros((ROW, PAIR), BF16)
        shifted[d, ROW + rows : 2 * ROW + rows, :] = jnp.zeros((ROW, PAIR), BF16)
    edges[...] = jnp.zeros_like(edges)
    low = lax.broadcasted_iota(jnp.int32, (ROW, PAIR), 1) < C
    pad = jnp.zeros((ROW - height, PAIR), F32)
    n_edge = edges.shape[1] - 16

    for i in range(2):
        layer = layers[i]
        copies[i][0].wait()
        copies[i][1].wait()
        for pair in range(wp // 2):
            tiles_x = []
            tiles_g = []
            for half in range(2):
                j = 2 * pair + half
                block = jnp.concatenate([xbuf[i, :, j * PAIR : (j + 1) * PAIR].astype(F32), pad], axis=0)
                at = ROW + j * ROW
                edges[0, 8 + j : 9 + j, :] = block[0:1, :]
                edges[1, 8 + j : 9 + j, :] = block[height - 1 : height, :]
                shifted[0, at : at + ROW, :] = pltpu.roll(block, 1, 0).astype(BF16)
                shifted[1, at : at + ROW, :] = block.astype(BF16)
                shifted[2, at : at + ROW, :] = pltpu.roll(block, ROW - 1, 0).astype(BF16)
                shifted[3, at : at + ROW, :] = pltpu.roll(block, ROW - 2, 0).astype(BF16)
                tiles_x.append(block)
                tiles_g.append(jnp.concatenate([gbuf[i, :, j * PAIR : (j + 1) * PAIR].astype(F32), pad], axis=0))
            lanes = slice(pair * PAIR, (pair + 1) * PAIR)
            lhs_t[0:PAIR, lanes] = jnp.concatenate(tiles_x, axis=0).T.astype(BF16)
            lhs_t[PAIR : 2 * PAIR, lanes] = jnp.concatenate(tiles_g, axis=0).T.astype(BF16)

        def product(d, s, part):
            left = lhs_t[...] if part is None else lhs_t[part * PAIR : (part + 1) * PAIR, :]
            right = [shifted[d, (1 + one) * ROW : (1 + one) * ROW + rows, :] for one in s]
            right = right[0] if len(right) == 1 else jnp.concatenate(right, axis=1)
            full = jnp.dot(left, right, preferred_element_type=F32)
            return [full[:, k * PAIR : (k + 1) * PAIR] for k in range(len(s))]

        def table(at_s, base, s):
            upper = at_s[s][base : base + C, :]
            here = pltpu.roll(at_s[s][base + C : base + PAIR, :], C, 1)
            if s + 1 not in at_s:
                return upper + here
            after = pltpu.roll(at_s[s + 1][base + C : base + PAIR, :], C, 1)
            return upper + jnp.where(low, here, after)

        def odd(at_s, base, s):
            return at_s[s][base : base + C, :] + pltpu.roll(at_s[s + 1][base + C : base + PAIR, :], C, 1)

        def store(name, value):
            index = PLACE[name]
            slot = slot_of(index // QUART, layer, first, second)
            (send_ref if i == 0 else keep_ref)[slot, index % QUART] = value

        p = product(0, (-1, 0), 1) + product(0, (1,), 1)
        at_s = dict(zip((-1, 0, 1), p))
        store("w0z", table(at_s, 0, 0))
        w0 = odd(at_s, 0, -1)
        p = product(1, (-1, 0), None) + product(1, (1,), None)
        at_s = dict(zip((-1, 0, 1), p))
        store("x0z", table(at_s, 0, 0))
        store("h0", jnp.where(low, table(at_s, 0, 1), w0))
        store("w1z", table(at_s, PAIR, 0))
        w1 = odd(at_s, PAIR, -1)
        p = product(2, (-1, 0), None) + product(2, (1,), None)
        at_s = dict(zip((-1, 0, 1), p))
        store("x1m", table(at_s, 0, -1))
        store("x1z", table(at_s, 0, 0))
        x12 = table(at_s, 0, 1)
        store("w2z", table(at_s, PAIR, 0))
        w2 = odd(at_s, PAIR, -1)
        p = product(3, (-1, 0), 0) + product(3, (1,), 0)
        at_s = dict(zip((-1, 0, 1), p))
        store("x2m", table(at_s, 0, -1))
        store("x2z", table(at_s, 0, 0))
        store("x22", jnp.where(low, x12, pltpu.roll(table(at_s, 0, 1), C, 1)))
        gl = lhs_t[PAIR : 2 * PAIR, :]
        gg = lax.dot_general(gl, gl, (((1,), (1,)), ((), ())), preferred_element_type=F32)
        store("gg", gg[0:C, :] + pltpu.roll(gg[C:PAIR, :], C, 1))
        fl = [
            jnp.where(
                low,
                shifted[d, ROW : 2 * ROW, :].astype(F32),
                shifted[d, rows : ROW + rows, :].astype(F32),
            ).astype(BF16)
            for d in (1, 2, 3)
        ]
        for d, name in enumerate(("cc0", "cc1", "cc2")):
            q = contract0(fl[0], fl[d])
            store(name, jnp.where(low, q[0:C, :], q[C:PAIR, :]))
        line = lax.broadcasted_iota(jnp.int32, (n_edge, PAIR), 0)
        lane = lax.broadcasted_iota(jnp.int32, (n_edge, PAIR), 1)
        corner = ((line == 0) & (lane < C)) | ((line == wp - 1) & (lane >= C))
        halves = []
        for e in range(2):
            zero = edges[e, 8 : 8 + n_edge, :]
            here = zero.astype(BF16)
            after = edges[e, 9 : 9 + n_edge, :].astype(BF16)
            at_s = {0: contract0(here, here), 1: contract0(here, after)}
            store(("r0z", "r1z")[e], table(at_s, 0, 0))
            halves.append(table(at_s, 0, 1))
            only = jnp.where(corner, zero, 0.0).astype(BF16)
            q = contract0(only, only)
            store(("k0", "k1")[e], jnp.where(low, q[0:C, :], q[C:PAIR, :]))
        store("h1", jnp.where(low, halves[0], w1))
        store("h2", jnp.where(low, halves[1], w2))


def local_sums(feature_maps, output_grads):
    height = feature_maps.shape[2]
    width = feature_maps.shape[3] // C
    wp = width // 2
    shape = jax.ShapeDtypeStruct((4, QUART, C, PAIR), F32)
    n_edge = (wp + 15) // 16 * 16
    return pl.pallas_call(
        functools.partial(local_kernel, height, width),
        out_shape=(shape, shape),
        in_specs=[pl.BlockSpec(memory_space=pl.ANY)] * 2,
        out_specs=(pl.BlockSpec(memory_space=pltpu.VMEM),) * 2,
        scratch_shapes=[
            pltpu.VMEM((2, height, width * C), BF16),
            pltpu.VMEM((2, height, width * C), BF16),
            pltpu.VMEM((4, (wp + 2) * ROW, PAIR), BF16),
            pltpu.VMEM((2 * PAIR, wp * ROW), BF16),
            pltpu.VMEM((2, n_edge + 16, PAIR), F32),
            pltpu.SemaphoreType.DMA((4,)),
        ],
        compiler_params=pltpu.CompilerParams(vmem_limit_bytes=40 * 2**20),
    )(feature_maps, output_grads)


def split(a):
    high = a.astype(BF16)
    return high, (a - high.astype(F32)).astype(BF16)


def dot3(a, b):
    ah, al = split(a)
    bh, bl = split(b)
    dot = functools.partial(jnp.dot, preferred_element_type=F32)
    return dot(ah, bh) + (dot(ah, bl) + dot(al, bh))


def normalized(m):
    n = m.shape[0]
    diag = lax.broadcasted_iota(jnp.int32, (n, n), 0) == lax.broadcasted_iota(jnp.int32, (n, n), 1)
    trace = jnp.sum(jnp.where(diag, m, 0.0))
    m = m + jnp.where(diag, DAMP * trace / n, 0.0)
    inv = lax.rsqrt(jnp.sum(m * m))
    return jnp.where(diag, 1.0, 0.0) - m * inv, inv


def final_kernel(total_rows, near_ref, far_ref, out_ref, quarters, m_ref, e_hi, e_lo):
    core, first, second = chip_place()
    quarters[0:2] = near_ref[...]
    quarters[2:4] = far_ref[...]

    def load(name):
        index = PLACE[name]
        both = quarters[slot_of(index // QUART, core, first, second), index % QUART]
        return both[:, 0:C], both[:, C:PAIR]

    x0 = dict(zip((0, 1), load("x0z")))
    h0, w00 = load("h0")
    x0[2] = h0
    row0 = dict(zip((0, 1), load("r0z")))
    row0[2], w10 = load("h1")
    row1 = dict(zip((0, 1), load("r1z")))
    row1[2], w20 = load("h2")
    col0 = {}
    col1 = {}
    col0[0], col1[0] = load("cc0")
    corner = load("k0") + load("k1")
    down = {}
    for dr in (1, 2):
        down[dr, -2], down[dr, -1] = load("x%dm" % dr)
        down[dr, 0], down[dr, 1] = load("x%dz" % dr)
        col0[dr], col1[dr] = load("cc%d" % dr)
    down[1, 2], down[2, 2] = load("x22")

    def put(t, u, block):
        m_ref[t * C : (t + 1) * C, u * C : (u + 1) * C] = block

    def put_all(taps, block):
        for t, u in taps:
            put(t, u, block)
        flipped = block.T
        for t, u in taps:
            put(u, t, flipped)

    for a in range(3):
        line = {}
        for dc in range(3):
            line[dc] = x0[dc] - row1[dc] if a == 0 else (x0[dc] - row0[dc] if a == 2 else x0[dc])
        for b in range(3):
            block = line[0]
            if b == 0:
                block = block - col1[0]
                if a == 0:
                    block = block + corner[3]
                if a == 2:
                    block = block + corner[1]
            if b == 2:
                block = block - col0[0]
                if a == 0:
                    block = block + corner[2]
                if a == 2:
                    block = block + corner[0]
            put(3 * a + b, 3 * a + b, block)
        put_all([(3 * a, 3 * a + 1), (3 * a + 1, 3 * a + 2)], line[1])
        put_all([(3 * a, 3 * a + 2)], line[2])
    for dr in (1, 2):
        starts = range(3 - dr)
        for b in range(3):
            block = down[dr, 0]
            if b == 0:
                block = block - col1[dr]
            if b == 2:
                block = block - col0[dr]
            put_all([(3 * a + b, 3 * (a + dr) + b) for a in starts], block)
        for dc in (-2, -1, 1, 2):
            taps = [(3 * a + b, 3 * (a + dr) + b + dc) for a in starts for b in range(3) if 0 <= b + dc < 3]
            put_all(taps, down[dr, dc])

    e, inv_a = normalized(m_ref[...])
    hi, lo = split(e)
    e_hi[...] = hi
    e_lo[...] = lo
    g, _ = load("gg")
    eg, inv_g = normalized(g)
    eg2 = dot3(eg, eg)
    pg = eg + dot3(eg, eg2) + eg2
    w0 = load("w0z")
    w1 = load("w1z")
    w2 = load("w2z")
    w = jnp.concatenate([w00, w0[0], w0[1], w10, w1[0], w1[1], w20, w2[0], w2[1]], axis=1)
    w = w + dot3(pg, w)
    v = w.T * (inv_a * inv_g * total_rows)

    def apply(v):
        vh, vl = split(v)
        both = jnp.dot(e_hi[...], jnp.concatenate([vh, vl], axis=1), preferred_element_type=F32)
        return both[:, 0:C] + (both[:, C:PAIR] + jnp.dot(e_lo[...], vh, preferred_element_type=F32))

    v = v + apply(v)
    v = v + apply(apply(v))
    out_ref[...] = v.T


def precondition(near, far, total_rows):
    n = TAPS * C
    return pl.pallas_call(
        functools.partial(final_kernel, float(total_rows)),
        out_shape=jax.ShapeDtypeStruct((C, n), F32),
        in_specs=[pl.BlockSpec(memory_space=pltpu.VMEM)] * 2,
        out_specs=pl.BlockSpec(memory_space=pltpu.VMEM),
        scratch_shapes=[
            pltpu.VMEM((4, QUART, C, PAIR), F32),
            pltpu.VMEM((n, n), F32),
            pltpu.VMEM((n, n), BF16),
            pltpu.VMEM((n, n), BF16),
        ],
        compiler_params=pltpu.CompilerParams(vmem_limit_bytes=40 * 2**20),
    )(near, far)


def stages(n_dp, n_grp):
    n = n_dp * n_grp
    core_bit = n_grp
    halvings = [1, 2 * n_grp]
    rest = []
    bit = 4 * n_grp
    while bit < n:
        rest.append(bit)
        bit *= 2
    orders = (halvings + rest, halvings[::-1] + rest[::-1])
    pairing = []
    for k in range(len(orders[0])):
        pairing.append([(i, i ^ orders[1 if i & core_bit else 0][k]) for i in range(n)])
    return [(i, i ^ core_bit) for i in range(n)], pairing


def shards(feature_maps, output_grads):
    n_dp, n_grp = lax.axis_size("dp"), lax.axis_size("grp")
    cores, pairing = stages(n_dp, n_grp)
    swap = lambda a, p: lax.ppermute(a, ("dp", "grp"), p)
    total_rows = feature_maps.shape[2] * feature_maps.shape[3] // C * feature_maps.shape[1] * n_dp * n_grp
    send, keep = local_sums(feature_maps, output_grads)
    got = swap(send, cores)
    got_far = swap(keep[2:4] + got[2:4], pairing[0])
    got_next = swap(keep[1] + got[1] + got_far[1], pairing[1])
    own = keep[0] + got[0] + got_far[0] + got_next
    for p in pairing[2:]:
        own = own + swap(own, p)
    near = jnp.stack([own, swap(own, pairing[1])])
    far = swap(near, pairing[0])
    mine = precondition(near, far, total_rows)
    other = swap(mine, cores)
    core = lax.rem(lax.axis_index("dp"), 2)
    return jnp.where(core == 0, jnp.stack([mine, other]), jnp.stack([other, mine]))


def solution(mesh):
    placed = (P(None, ("dp", "grp"), None, None), P(None, ("dp", "grp"), None, None))
    return jax.shard_map(shards, mesh=mesh, in_specs=placed, out_specs=P(), check_vma=False)
```

time: 282 us -> 57.5 us (0.20)
  the two profiles are of different devices: /device:TPU:0 before, /device:TPU:25 now
where the time goes in v1:
time: 57.5 us; the launch traced here: 57.3 us
  waiting for transfers between devices  31.6 us (55%)
  starting transfers between devices  13.2 us (23%)
  Pallas kernels  9.32 us (16%)
  local copies, waits for them, and re-layouts  2.28 us (4%)
  other arithmetic  0.93 us (2%)
    ppermute x8, waiting for transfers between devices, shards(): swap = lambda a, p: lax.ppermute(a, ('dp', 'grp'), p)  31.6 us
    ppermute x8, starting transfers between devices, shards(): swap = lambda a, p: lax.ppermute(a, ('dp', 'grp'), p)  13.2 us
    pallas_call x1, Pallas kernels, local_sums(): pl.pallas_call(functools.partial(local_kernel, height, width), out_shape=...  4.83 us
    pallas_call x1, Pallas kernels, precondition(): pl.pallas_call(functools.partial(final_kernel, float(total_rows)), out_sh...  4.49 us
    unnamed x4, local copies, waits for them, and re-layouts  2.28 us
  transfers between devices with their start and end apart: 8, of which 8 were waited for; matrix products, arithmetic and copies ran while one was open for 0% of the time, Pallas kernels for 0%

profile of v1, /device:TPU:25, one launch (start us, length us, event | category | flops | bytes accessed | tf_op | source)
XLA Modules:
  0.0 57.3 jit_solution(13683620953437298614)
XLA Ops:
  0.0 0.0 copy-start
  0.0 1.1 %copy-done = bf16[2,1,56,3584]{3,2,1,0:T(8,128)(2,1)S(1)} copy-done((bf16[2,1,56,3584]{3,2,1,0:T(8,128)(2,1)S(1)}, bf16[2,1,56,3584]{3,2,1,0:T(8,128)(2,1)}, u32[]{:S(2)}) %copy-start) | copy-done | bytes 802840
  1.1 0.0 copy-start.1
  1.1 1.1 %copy-done.1 = bf16[2,1,56,3584]{3,2,1,0:T(8,128)(2,1)S(1)} copy-done((bf16[2,1,56,3584]{3,2,1,0:T(8,128)(2,1)S(1)}, bf16[2,1,56,3584]{3,2,1,0:T(8,128)(2,1)}, u32[]{:S(2)}) %copy-start.1) | copy-done | bytes 802840
  2.3 4.8 %shard_map.28 = (f32[4,5,64,128]{3,2,1,0:T(8,128)S(1)}, f32[4,5,64,128]{3,2,1,0:T(8,128)S(1)}) custom-call(bf16[2,1,56,3584]{3,2,1,0:T(8,128)(2,1)S(1)} %copy-done, bf16[2,1,56,3584]{3,2,1,0:T(8,128)(2,1)S(1)} %copy-done.1), custom_call_target="tpu_custom_call" | custom-call | tf_op jit(solution)/shard_map/pallas_call | solution.py:180
  7.1 0.7 %collective-permute-start = (f32[4,5,64,128]{3,2,1,0:T(8,128)S(1)}, f32[4,5,64,128]{3,2,1,0:T(8,128)S(1)}, u32[]{:S(2)}, u32[]{:S(2)}) collective-permute-start(f32[4,5,64,128]{3,2,1,0:T(8,128)S(1)} %get-tuple-element.8), channel_id=1, source_target_pairs={{0,2},{1,3},{2,0},{3,1},{4,6},{5,7},{6,4},{7,5},{8,10},{9,11},{10,... | collective-permute-start | bytes 1966088 | tf_op jit(solution)/shard_map/ppermute | solution.py:351
  7.9 1.7 %collective-permute-done = f32[4,5,64,128]{3,2,1,0:T(8,128)S(1)} collective-permute-done((f32[4,5,64,128]{3,2,1,0:T(8,128)S(1)}, f32[4,5,64,128]{3,2,1,0:T(8,128)S(1)}, u32[]{:S(2)}, u32[]{:S(2)}) %collective-permute-start) | collective-permute-done | bytes 655392 | tf_op jit(solution)/shard_map/ppermute | solution.py:351
  9.6 1.3 %collective-permute-start.1 = (f32[2,5,64,128]{3,2,1,0:T(8,128)S(1)}, f32[2,5,64,128]{3,2,1,0:T(8,128)S(1)}, u32[]{:S(2)}, u32[]{:S(2)}) collective-permute-start(f32[2,5,64,128]{3,2,1,0:T(8,128)S(1)} %slice_add_fusion), channel_id=1, source_target_pairs={{0,1},{1,0},{2,6},{3,7},{4,5},{5,4},{6,2},{7,3},{8,9},{9,8},{10,14... | collective-permute-start | bytes 983048 | tf_op jit(solution)/shard_map/ppermute | solution.py:351
  10.9 5.0 %collective-permute-done.1 = f32[2,5,64,128]{3,2,1,0:T(8,128)S(1)} collective-permute-done((f32[2,5,64,128]{3,2,1,0:T(8,128)S(1)}, f32[2,5,64,128]{3,2,1,0:T(8,128)S(1)}, u32[]{:S(2)}, u32[]{:S(2)}) %collective-permute-start.1) | collective-permute-done | bytes 327712 | tf_op jit(solution)/shard_map/ppermute | solution.py:351
  15.9 1.3 %collective-permute-start.2 = (f32[5,64,128]{2,1,0:T(8,128)S(1)}, f32[5,64,128]{2,1,0:T(8,128)S(1)}, u32[]{:S(2)}, u32[]{:S(2)}) collective-permute-start(f32[5,64,128]{2,1,0:T(8,128)S(1)} %fusion), channel_id=1, source_target_pairs={{0,4},{1,5},{2,3},{3,2},{4,0},{5,1},{6,7},{7,6},{8,12},{9,13},{10,... | collective-permute-start | bytes 491528 | tf_op jit(solution)/shard_map/ppermute | solution.py:351
  17.2 3.3 %collective-permute-done.2 = f32[5,64,128]{2,1,0:T(8,128)S(1)} collective-permute-done((f32[5,64,128]{2,1,0:T(8,128)S(1)}, f32[5,64,128]{2,1,0:T(8,128)S(1)}, u32[]{:S(2)}, u32[]{:S(2)}) %collective-permute-start.2) | collective-permute-done | bytes 163872 | tf_op jit(solution)/shard_map/ppermute | solution.py:351
  20.5 0.1 collective-permute-start.3
  20.6 6.8 %collective-permute-done.3 = f32[5,64,128]{2,1,0:T(8,128)S(1)} collective-permute-done((f32[5,64,128]{2,1,0:T(8,128)S(1)}, f32[5,64,128]{2,1,0:T(8,128)S(1)}, u32[]{:S(2)}, u32[]{:S(2)}) %collective-permute-start.3) | collective-permute-done | bytes 163872 | tf_op jit(solution)/shard_map/ppermute | solution.py:351
  27.4 0.1 collective-permute-start.4
  27.5 4.2 %collective-permute-done.4 = f32[5,64,128]{2,1,0:T(8,128)S(1)} collective-permute-done((f32[5,64,128]{2,1,0:T(8,128)S(1)}, f32[5,64,128]{2,1,0:T(8,128)S(1)}, u32[]{:S(2)}, u32[]{:S(2)}) %collective-permute-start.4) | collective-permute-done | bytes 163872 | tf_op jit(solution)/shard_map/ppermute | solution.py:351
  31.7 1.3 %collective-permute-start.5 = (f32[5,64,128]{2,1,0:T(8,128)S(1)}, f32[5,64,128]{2,1,0:T(8,128)S(1)}, u32[]{:S(2)}, u32[]{:S(2)}) collective-permute-start(f32[5,64,128]{2,1,0:T(8,128)S(1)} %add.41), channel_id=1, source_target_pairs={{0,4},{1,5},{2,3},{3,2},{4,0},{5,1},{6,7},{7,6},{8,12},{9,13},{10,... | collective-permute-start | bytes 491528 | tf_op jit(solution)/shard_map/ppermute | solution.py:351
  33.0 3.3 %collective-permute-done.5 = f32[5,64,128]{2,1,0:T(8,128)S(1)} collective-permute-done((f32[5,64,128]{2,1,0:T(8,128)S(1)}, f32[5,64,128]{2,1,0:T(8,128)S(1)}, u32[]{:S(2)}, u32[]{:S(2)}) %collective-permute-start.5) | collective-permute-done | bytes 163872 | tf_op jit(solution)/shard_map/ppermute | solution.py:351
  36.2 1.3 %collective-permute-start.6 = (f32[2,5,64,128]{3,2,1,0:T(8,128)S(1)}, f32[2,5,64,128]{3,2,1,0:T(8,128)S(1)}, u32[]{:S(2)}, u32[]{:S(2)}) collective-permute-start(f32[2,5,64,128]{3,2,1,0:T(8,128)S(1)} %pad_maximum_fusion.near_ref), channel_id=1, source_target_pairs={{0,1},{1,0},{2,6},{3,7},{4,5},{5,4},{6,2},{7,3},{8,9},{9,8},{10,14... | collective-permute-start | bytes 983048 | tf_op jit(solution)/shard_map/ppermute | solution.py:351
  37.5 6.4 %collective-permute-done.6.far_ref = f32[2,5,64,128]{3,2,1,0:T(8,128)S(1)} collective-permute-done((f32[2,5,64,128]{3,2,1,0:T(8,128)S(1)}, f32[2,5,64,128]{3,2,1,0:T(8,128)S(1)}, u32[]{:S(2)}, u32[]{:S(2)}) %collective-permute-start.6) | collective-permute-done | bytes 327712 | tf_op jit(solution)/shard_map/ppermute | solution.py:351
  44.0 4.5 %shard_map.29 = f32[64,576]{1,0:T(8,128)S(1)} custom-call(f32[2,5,64,128]{3,2,1,0:T(8,128)S(1)} %pad_maximum_fusion.near_ref, f32[2,5,64,128]{3,2,1,0:T(8,128)S(1)} %collective-permute-done.6.far_ref), custom_call_target="tpu_custom_call" | custom-call | tf_op jit(solution)/shard_map/pallas_call | solution.py:317
  48.5 7.1 %collective-permute-start.7 = (f32[64,576]{1,0:T(8,128)S(1)}, f32[64,576]{1,0:T(8,128)S(1)}, u32[]{:S(2)}, u32[]{:S(2)}) collective-permute-start(f32[64,576]{1,0:T(8,128)S(1)} %shard_map.29), channel_id=1, source_target_pairs={{0,2},{1,3},{2,0},{3,1},{4,6},{5,7},{6,4},{7,5},{8,10},{9,11},{10,... | collective-permute-start | bytes 442376 | tf_op jit(solution)/shard_map/ppermute | solution.py:351
  55.5 1.0 %collective-permute-done.7 = f32[64,576]{1,0:T(8,128)S(1)} collective-permute-done((f32[64,576]{1,0:T(8,128)S(1)}, f32[64,576]{1,0:T(8,128)S(1)}, u32[]{:S(2)}, u32[]{:S(2)}) %collective-permute-start.7) | collective-permute-done | bytes 147488 | tf_op jit(solution)/shard_map/ppermute | solution.py:351
  56.6 0.7 %maximum_select_fusion = f32[2,64,576]{2,1,0:T(8,128)} fusion(f32[1,64,576]{2,1,0:T(8,128)S(1)} %bitcast.13, f32[1,64,576]{2,1,0:T(8,128)S(1)} %bitcast.10, pred[]{:T(512)S(6)} %eq.3), kind=kLoop, calls=%fused_computation.2 | loop fusion | flops 221184 | bytes 589825 | tf_op jit(solution)/shard_map/jit(_where)/select_n | solution.py:365
  (6 shorter events, 0.2 us)
Async XLA Ops:
  0.0 1.1 %copy-start = (bf16[2,1,56,3584]{3,2,1,0:T(8,128)(2,1)S(1)}, bf16[2,1,56,3584]{3,2,1,0:T(8,128)(2,1)}, u32[]{:S(2)}) copy-start(bf16[2,1,56,3584]{3,2,1,0:T(8,128)(2,1)} %x_hbm.1) | copy-start | bytes 2408452
  1.1 1.1 %copy-start.1 = (bf16[2,1,56,3584]{3,2,1,0:T(8,128)(2,1)S(1)}, bf16[2,1,56,3584]{3,2,1,0:T(8,128)(2,1)}, u32[]{:S(2)}) copy-start(bf16[2,1,56,3584]{3,2,1,0:T(8,128)(2,1)} %g_hbm.1) | copy-start | bytes 2408452
  7.1 2.5 %collective-permute-start = (f32[4,5,64,128]{3,2,1,0:T(8,128)S(1)}, f32[4,5,64,128]{3,2,1,0:T(8,128)S(1)}, u32[]{:S(2)}, u32[]{:S(2)}) collective-permute-start(f32[4,5,64,128]{3,2,1,0:T(8,128)S(1)} %get-tuple-element.8), channel_id=1, source_target_pairs={{0,2},{1,3},{2,0},{3,1},{4,6},{5,7},{6,4},{7,5},{8,10},{9,11},{10,... | collective-permute-start | bytes 1966088 | tf_op jit(solution)/shard_map/ppermute | solution.py:351
  9.6 6.3 %collective-permute-start.1 = (f32[2,5,64,128]{3,2,1,0:T(8,128)S(1)}, f32[2,5,64,128]{3,2,1,0:T(8,128)S(1)}, u32[]{:S(2)}, u32[]{:S(2)}) collective-permute-start(f32[2,5,64,128]{3,2,1,0:T(8,128)S(1)} %slice_add_fusion), channel_id=1, source_target_pairs={{0,1},{1,0},{2,6},{3,7},{4,5},{5,4},{6,2},{7,3},{8,9},{9,8},{10,14... | collective-permute-start | bytes 983048 | tf_op jit(solution)/shard_map/ppermute | solution.py:351
  15.9 4.5 %collective-permute-start.2 = (f32[5,64,128]{2,1,0:T(8,128)S(1)}, f32[5,64,128]{2,1,0:T(8,128)S(1)}, u32[]{:S(2)}, u32[]{:S(2)}) collective-permute-start(f32[5,64,128]{2,1,0:T(8,128)S(1)} %fusion), channel_id=1, source_target_pairs={{0,4},{1,5},{2,3},{3,2},{4,0},{5,1},{6,7},{7,6},{8,12},{9,13},{10,... | collective-permute-start | bytes 491528 | tf_op jit(solution)/shard_map/ppermute | solution.py:351
  20.5 6.9 %collective-permute-start.3 = (f32[5,64,128]{2,1,0:T(8,128)S(1)}, f32[5,64,128]{2,1,0:T(8,128)S(1)}, u32[]{:S(2)}, u32[]{:S(2)}) collective-permute-start(f32[5,64,128]{2,1,0:T(8,128)S(1)} %fusion.2), channel_id=1, source_target_pairs={{0,8},{1,9},{2,18},{3,19},{4,12},{5,13},{6,22},{7,23},{8,0},{9,1},... | collective-permute-start | bytes 491528 | tf_op jit(solution)/shard_map/ppermute | solution.py:351
  27.4 4.2 %collective-permute-start.4 = (f32[5,64,128]{2,1,0:T(8,128)S(1)}, f32[5,64,128]{2,1,0:T(8,128)S(1)}, u32[]{:S(2)}, u32[]{:S(2)}) collective-permute-start(f32[5,64,128]{2,1,0:T(8,128)S(1)} %add.40), channel_id=1, source_target_pairs={{0,16},{1,17},{2,10},{3,11},{4,20},{5,21},{6,14},{7,15},{8,24},{9,... | collective-permute-start | bytes 491528 | tf_op jit(solution)/shard_map/ppermute | solution.py:351
  31.7 4.5 %collective-permute-start.5 = (f32[5,64,128]{2,1,0:T(8,128)S(1)}, f32[5,64,128]{2,1,0:T(8,128)S(1)}, u32[]{:S(2)}, u32[]{:S(2)}) collective-permute-start(f32[5,64,128]{2,1,0:T(8,128)S(1)} %add.41), channel_id=1, source_target_pairs={{0,4},{1,5},{2,3},{3,2},{4,0},{5,1},{6,7},{7,6},{8,12},{9,13},{10,... | collective-permute-start | bytes 491528 | tf_op jit(solution)/shard_map/ppermute | solution.py:351
  36.2 7.7 %collective-permute-start.6 = (f32[2,5,64,128]{3,2,1,0:T(8,128)S(1)}, f32[2,5,64,128]{3,2,1,0:T(8,128)S(1)}, u32[]{:S(2)}, u32[]{:S(2)}) collective-permute-start(f32[2,5,64,128]{3,2,1,0:T(8,128)S(1)} %pad_maximum_fusion.near_ref), channel_id=1, source_target_pairs={{0,1},{1,0},{2,6},{3,7},{4,5},{5,4},{6,2},{7,3},{8,9},{9,8},{10,14... | collective-permute-start | bytes 983048 | tf_op jit(solution)/shard_map/ppermute | solution.py:351
  48.5 8.1 %collective-permute-start.7 = (f32[64,576]{1,0:T(8,128)S(1)}, f32[64,576]{1,0:T(8,128)S(1)}, u32[]{:S(2)}, u32[]{:S(2)}) collective-permute-start(f32[64,576]{1,0:T(8,128)S(1)} %shard_map.29), channel_id=1, source_target_pairs={{0,2},{1,3},{2,0},{3,1},{4,6},{5,7},{6,4},{7,5},{8,10},{9,11},{10,... | collective-permute-start | bytes 442376 | tf_op jit(solution)/shard_map/ppermute | solution.py:351

commit v2 on v1

v2 whole, which is shorter than its diff:
```python
import functools

import jax
import jax.numpy as jnp
import numpy as np
from jax import lax
from jax.experimental import pallas as pl
from jax.experimental.pallas import tpu as pltpu
from jax.sharding import PartitionSpec as P

C = 64
TAPS = 9
PAIR = 2 * C
ROW = 64
QUART = 5
DAMP = 0.1
VMEM_LIMIT = 48 * 2**20
F32 = jnp.float32
BF16 = jnp.bfloat16

PAIRS = (
    "x1m", "x1z", "cc1", "x2m", "x2z",
    "cc2", "x22", "x0z", "cc0", "r0z",
    "r1z", "k0", "k1", "w0z", "w1z",
    "w2z", "h0", "h1", "h2", "gg",
)
PLACE = {name: index for index, name in enumerate(PAIRS)}


def contract0(a, b):
    return lax.dot_general(a, b, (((0,), (0,)), ((), ())), preferred_element_type=F32)


def chip_place():
    dp = lax.axis_index("dp")
    core = lax.rem(dp, 2)
    second = lax.rem(dp // 2, 2)
    first = lax.axis_index("grp")
    return core, first, second


def slot_of(quarter, layer, first, second):
    mine_first = first ^ (quarter // 2)
    mine_second = second ^ (quarter % 2)
    major = jnp.where(layer == 0, mine_first, mine_second)
    minor = jnp.where(layer == 0, mine_second, mine_first)
    return 2 * major + minor


def gathered_slot(quarter, first, second):
    return 2 * (second ^ (quarter % 2)) + (first ^ (quarter // 2))


def local_kernel(height, width, own, x_hbm, g_hbm, out_ref, xbuf, gbuf, shifted, lhs_t, edges, sems):
    core, first, second = chip_place()
    wp = width // 2
    rows = wp * ROW
    layer = core if own else 1 - core
    copy_x = pltpu.make_async_copy(x_hbm.at[layer, 0], xbuf, sems.at[0])
    copy_g = pltpu.make_async_copy(g_hbm.at[layer, 0], gbuf, sems.at[1])
    copy_x.start()
    copy_g.start()
    for d in range(4):
        shifted[d, 0:ROW, :] = jnp.zeros((ROW, PAIR), BF16)
        shifted[d, ROW + rows : 2 * ROW + rows, :] = jnp.zeros((ROW, PAIR), BF16)
    edges[...] = jnp.zeros_like(edges)
    low = lax.broadcasted_iota(jnp.int32, (ROW, PAIR), 1) < C
    pad = jnp.zeros((ROW - height, PAIR), F32)
    n_edge = edges.shape[1] - 16
    copy_x.wait()
    copy_g.wait()
    for pair in range(wp // 2):
        tiles_x = []
        tiles_g = []
        for half in range(2):
            j = 2 * pair + half
            block = jnp.concatenate([xbuf[:, j * PAIR : (j + 1) * PAIR].astype(F32), pad], axis=0)
            at = ROW + j * ROW
            edges[0, 8 + j : 9 + j, :] = block[0:1, :]
            edges[1, 8 + j : 9 + j, :] = block[height - 1 : height, :]
            shifted[0, at : at + ROW, :] = pltpu.roll(block, 1, 0).astype(BF16)
            shifted[1, at : at + ROW, :] = block.astype(BF16)
            shifted[2, at : at + ROW, :] = pltpu.roll(block, ROW - 1, 0).astype(BF16)
            shifted[3, at : at + ROW, :] = pltpu.roll(block, ROW - 2, 0).astype(BF16)
            tiles_x.append(block)
            tiles_g.append(jnp.concatenate([gbuf[:, j * PAIR : (j + 1) * PAIR].astype(F32), pad], axis=0))
        lanes = slice(pair * PAIR, (pair + 1) * PAIR)
        lhs_t[0:PAIR, lanes] = jnp.concatenate(tiles_x, axis=0).T.astype(BF16)
        lhs_t[PAIR : 2 * PAIR, lanes] = jnp.concatenate(tiles_g, axis=0).T.astype(BF16)

    def product(d, s, part):
        left = lhs_t[...] if part is None else lhs_t[part * PAIR : (part + 1) * PAIR, :]
        right = [shifted[d, (1 + one) * ROW : (1 + one) * ROW + rows, :] for one in s]
        right = right[0] if len(right) == 1 else jnp.concatenate(right, axis=1)
        full = jnp.dot(left, right, preferred_element_type=F32)
        return [full[:, k * PAIR : (k + 1) * PAIR] for k in range(len(s))]

    def table(at_s, base, s):
        upper = at_s[s][base : base + C, :]
        here = pltpu.roll(at_s[s][base + C : base + PAIR, :], C, 1)
        if s + 1 not in at_s:
            return upper + here
        after = pltpu.roll(at_s[s + 1][base + C : base + PAIR, :], C, 1)
        return upper + jnp.where(low, here, after)

    def odd(at_s, base, s):
        return at_s[s][base : base + C, :] + pltpu.roll(at_s[s + 1][base + C : base + PAIR, :], C, 1)

    def store(name, value):
        index = PLACE[name]
        slot = slot_of(index // QUART, layer, first, second)
        out_ref[slot, index % QUART] = value

    p = product(0, (-1, 0), 1) + product(0, (1,), 1)
    at_s = dict(zip((-1, 0, 1), p))
    store("w0z", table(at_s, 0, 0))
    w0 = odd(at_s, 0, -1)
    p = product(1, (-1, 0), None) + product(1, (1,), None)
    at_s = dict(zip((-1, 0, 1), p))
    store("x0z", table(at_s, 0, 0))
    store("h0", jnp.where(low, table(at_s, 0, 1), w0))
    store("w1z", table(at_s, PAIR, 0))
    w1 = odd(at_s, PAIR, -1)
    p = product(2, (-1, 0), None) + product(2, (1,), None)
    at_s = dict(zip((-1, 0, 1), p))
    store("x1m", table(at_s, 0, -1))
    store("x1z", table(at_s, 0, 0))
    x12 = table(at_s, 0, 1)
    store("w2z", table(at_s, PAIR, 0))
    w2 = odd(at_s, PAIR, -1)
    p = product(3, (-1, 0), 0) + product(3, (1,), 0)
    at_s = dict(zip((-1, 0, 1), p))
    store("x2m", table(at_s, 0, -1))
    store("x2z", table(at_s, 0, 0))
    store("x22", jnp.where(low, x12, pltpu.roll(table(at_s, 0, 1), C, 1)))
    gl = lhs_t[PAIR : 2 * PAIR, :]
    gg = lax.dot_general(gl, gl, (((1,), (1,)), ((), ())), preferred_element_type=F32)
    store("gg", gg[0:C, :] + pltpu.roll(gg[C:PAIR, :], C, 1))
    fl = [
        jnp.where(
            low,
            shifted[d, ROW : 2 * ROW, :].astype(F32),
            shifted[d, rows : ROW + rows, :].astype(F32),
        ).astype(BF16)
        for d in (1, 2, 3)
    ]
    for d, name in enumerate(("cc0", "cc1", "cc2")):
        q = contract0(fl[0], fl[d])
        store(name, jnp.where(low, q[0:C, :], q[C:PAIR, :]))
    line = lax.broadcasted_iota(jnp.int32, (n_edge, PAIR), 0)
    lane = lax.broadcasted_iota(jnp.int32, (n_edge, PAIR), 1)
    corner = ((line == 0) & (lane < C)) | ((line == wp - 1) & (lane >= C))
    halves = []
    for e in range(2):
        zero = edges[e, 8 : 8 + n_edge, :]
        here = zero.astype(BF16)
        after = edges[e, 9 : 9 + n_edge, :].astype(BF16)
        at_s = {0: contract0(here, here), 1: contract0(here, after)}
        store(("r0z", "r1z")[e], table(at_s, 0, 0))
        halves.append(table(at_s, 0, 1))
        only = jnp.where(corner, zero, 0.0).astype(BF16)
        q = contract0(only, only)
        store(("k0", "k1")[e], jnp.where(low, q[0:C, :], q[C:PAIR, :]))
    store("h1", jnp.where(low, halves[0], w1))
    store("h2", jnp.where(low, halves[1], w2))


def local_sums(feature_maps, output_grads, own):
    height = feature_maps.shape[2]
    width = feature_maps.shape[3] // C
    wp = width // 2
    shape = jax.ShapeDtypeStruct((4, QUART, C, PAIR), F32)
    n_edge = (wp + 15) // 16 * 16
    return pl.pallas_call(
        functools.partial(local_kernel, height, width, own),
        out_shape=shape,
        in_specs=[pl.BlockSpec(memory_space=pltpu.HBM)] * 2,
        out_specs=pl.BlockSpec(memory_space=pltpu.VMEM),
        scratch_shapes=[
            pltpu.VMEM((height, width * C), BF16),
            pltpu.VMEM((height, width * C), BF16),
            pltpu.VMEM((4, (wp + 2) * ROW, PAIR), BF16),
            pltpu.VMEM((2 * PAIR, wp * ROW), BF16),
            pltpu.VMEM((2, n_edge + 16, PAIR), F32),
            pltpu.SemaphoreType.DMA((2,)),
        ],
        compiler_params=pltpu.CompilerParams(vmem_limit_bytes=VMEM_LIMIT),
    )(feature_maps, output_grads)


def split(a):
    high = a.astype(BF16)
    return high, (a - high.astype(F32)).astype(BF16)


def dot3(a, b):
    ah, al = split(a)
    bh, bl = split(b)
    dot = functools.partial(jnp.dot, preferred_element_type=F32)
    return dot(ah, bh) + (dot(ah, bl) + dot(al, bh))


def normalized(m):
    n = m.shape[0]
    diag = lax.broadcasted_iota(jnp.int32, (n, n), 0) == lax.broadcasted_iota(jnp.int32, (n, n), 1)
    trace = jnp.sum(jnp.where(diag, m, 0.0))
    m = m + jnp.where(diag, DAMP * trace / n, 0.0)
    inv = lax.rsqrt(jnp.sum(m * m))
    return jnp.where(diag, 1.0, 0.0) - m * inv, inv


def final_kernel(total_rows, near_ref, far_ref, out_ref, quarters, m_ref, e_hi, e_lo):
    _, first, second = chip_place()
    quarters[0:2] = near_ref[...]
    quarters[2:4] = far_ref[...]

    def load(name):
        index = PLACE[name]
        both = quarters[gathered_slot(index // QUART, first, second), index % QUART]
        return both[:, 0:C], both[:, C:PAIR]

    x0 = dict(zip((0, 1), load("x0z")))
    h0, w00 = load("h0")
    x0[2] = h0
    row0 = dict(zip((0, 1), load("r0z")))
    row0[2], w10 = load("h1")
    row1 = dict(zip((0, 1), load("r1z")))
    row1[2], w20 = load("h2")
    col0 = {}
    col1 = {}
    col0[0], col1[0] = load("cc0")
    corner = load("k0") + load("k1")
    down = {}
    for dr in (1, 2):
        down[dr, -2], down[dr, -1] = load("x%dm" % dr)
        down[dr, 0], down[dr, 1] = load("x%dz" % dr)
        col0[dr], col1[dr] = load("cc%d" % dr)
    down[1, 2], down[2, 2] = load("x22")

    def put(t, u, block):
        m_ref[t * C : (t + 1) * C, u * C : (u + 1) * C] = block

    def put_all(taps, block):
        for t, u in taps:
            put(t, u, block)
        flipped = block.T
        for t, u in taps:
            put(u, t, flipped)

    for a in range(3):
        line = {}
        for dc in range(3):
            line[dc] = x0[dc] - row1[dc] if a == 0 else (x0[dc] - row0[dc] if a == 2 else x0[dc])
        for b in range(3):
            block = line[0]
            if b == 0:
                block = block - col1[0]
                if a == 0:
                    block = block + corner[3]
                if a == 2:
                    block = block + corner[1]
            if b == 2:
                block = block - col0[0]
                if a == 0:
                    block = block + corner[2]
                if a == 2:
                    block = block + corner[0]
            put(3 * a + b, 3 * a + b, block)
        put_all([(3 * a, 3 * a + 1), (3 * a + 1, 3 * a + 2)], line[1])
        put_all([(3 * a, 3 * a + 2)], line[2])
    for dr in (1, 2):
        starts = range(3 - dr)
        for b in range(3):
            block = down[dr, 0]
            if b == 0:
                block = block - col1[dr]
            if b == 2:
                block = block - col0[dr]
            put_all([(3 * a + b, 3 * (a + dr) + b) for a in starts], block)
        for dc in (-2, -1, 1, 2):
            taps = [(3 * a + b, 3 * (a + dr) + b + dc) for a in starts for b in range(3) if 0 <= b + dc < 3]
            put_all(taps, down[dr, dc])

    e, inv_a = normalized(m_ref[...])
    hi, lo = split(e)
    e_hi[...] = hi
    e_lo[...] = lo
    g, _ = load("gg")
    eg, inv_g = normalized(g)
    eg2 = dot3(eg, eg)
    pg = eg + dot3(eg, eg2) + eg2
    w0 = load("w0z")
    w1 = load("w1z")
    w2 = load("w2z")
    w = jnp.concatenate([w00, w0[0], w0[1], w10, w1[0], w1[1], w20, w2[0], w2[1]], axis=1)
    w = w + dot3(pg, w)
    v = w.T * (inv_a * inv_g * total_rows)

    def apply(v):
        vh, vl = split(v)
        both = jnp.dot(e_hi[...], jnp.concatenate([vh, vl], axis=1), preferred_element_type=F32)
        return both[:, 0:C] + (both[:, C:PAIR] + jnp.dot(e_lo[...], vh, preferred_element_type=F32))

    v = v + apply(v)
    v = v + apply(apply(v))
    out_ref[...] = v.T


def precondition(near, far, total_rows):
    n = TAPS * C
    return pl.pallas_call(
        functools.partial(final_kernel, float(total_rows)),
        out_shape=jax.ShapeDtypeStruct((C, n), F32),
        in_specs=[pl.BlockSpec(memory_space=pltpu.VMEM)] * 2,
        out_specs=pl.BlockSpec(memory_space=pltpu.VMEM),
        scratch_shapes=[
            pltpu.VMEM((4, QUART, C, PAIR), F32),
            pltpu.VMEM((n, n), F32),
            pltpu.VMEM((n, n), BF16),
            pltpu.VMEM((n, n), BF16),
        ],
        compiler_params=pltpu.CompilerParams(vmem_limit_bytes=VMEM_LIMIT),
    )(near, far)


def pairings(n_dp, n_grp):
    n = n_dp * n_grp
    core_bit = n_grp
    first, second = 1, 2 * n_grp
    doublings = []
    bit = 4 * n_grp
    while bit < n:
        doublings.append(bit)
        bit *= 2
    orders = ([first, second] + doublings, [second, first] + doublings[::-1])
    pairs = lambda masks: [(i, i ^ masks[1 if i & core_bit else 0]) for i in range(n)]
    rounds = [pairs(masks) for masks in zip(*orders)]
    return pairs((core_bit, core_bit)), rounds[:2], rounds[2:], (pairs((first, first)), pairs((second, second)))


def shards(feature_maps, output_grads):
    n_dp, n_grp = lax.axis_size("dp"), lax.axis_size("grp")
    cores, halvings, doublings, gathers = pairings(n_dp, n_grp)
    swap = lambda a, p: lax.ppermute(a, ("dp", "grp"), p)
    total_rows = feature_maps.shape[2] * feature_maps.shape[3] // C * feature_maps.shape[1] * n_dp * n_grp
    got = swap(local_sums(feature_maps, output_grads, False), cores)
    keep = local_sums(feature_maps, output_grads, True)
    got_far = swap(keep[2:4] + got[2:4], halvings[0])
    got_next = swap(keep[1] + got[1] + got_far[1], halvings[1])
    own = keep[0] + got[0] + got_far[0] + got_next
    for p in doublings:
        own = own + swap(own, p)
    near = jnp.stack([own, swap(own, gathers[0])])
    far = swap(near, gathers[1])
    mine = precondition(near, far, total_rows)
    other = swap(mine, cores)
    core = lax.rem(lax.axis_index("dp"), 2)
    return jnp.where(core == 0, jnp.stack([mine, other]), jnp.stack([other, mine]))


def solution(mesh):
    placed = (P(None, ("dp", "grp"), None, None), P(None, ("dp", "grp"), None, None))
    return jax.shard_map(shards, mesh=mesh, in_specs=placed, out_specs=P(), check_vma=False)
```

time: 57.5 us -> 53.8 us (0.936)
  waiting for transfers between devices: 31.6 us -> 27.9 us
    ppermute x8, waiting for transfers between devices: 31.6 us -> 27.9 us  [shards(): swap = lambda a, p: lax.ppermute(a, ('dp', 'grp'), p)]
    pallas_call x1 -> x2, Pallas kernels: 4.83 us -> 4.87 us  [local_sums(): pl.pallas_call(functools.partial(local_kernel, height, width, own), out_s...]
  transfers between devices with their start and end apart: 8 -> 8, of which waited for: 8 -> 7; matrix products, arithmetic and copies ran while one was open for 0% -> 0% of each run, Pallas kernels for 0% -> 5%
where the time goes in v2:
time: 53.8 us; the launch traced here: 53.6 us
  waiting for transfers between devices  27.9 us (52%)
  starting transfers between devices  13.1 us (24%)
  Pallas kernels  9.36 us (17%)
  local copies, waits for them, and re-layouts  2.28 us (4%)
  other arithmetic  0.91 us (2%)
    ppermute x8, waiting for transfers between devices, shards(): swap = lambda a, p: lax.ppermute(a, ('dp', 'grp'), p)  27.9 us
    ppermute x8, starting transfers between devices, shards(): swap = lambda a, p: lax.ppermute(a, ('dp', 'grp'), p)  13.1 us
    pallas_call x2, Pallas kernels, local_sums(): pl.pallas_call(functools.partial(local_kernel, height, width, own), out_s...  4.87 us
    pallas_call x1, Pallas kernels, precondition(): pl.pallas_call(functools.partial(final_kernel, float(total_rows)), out_sh...  4.5 us
    unnamed x4, local copies, waits for them, and re-layouts  2.28 us
  transfers between devices with their start and end apart: 8, of which 7 were waited for; matrix products, arithmetic and copies ran while one was open for 0% of the time, Pallas kernels for 5%

profile of v2, /device:TPU:25, one launch (start us, length us, event | category | flops | bytes accessed | tf_op | source)
XLA Modules:
  0.0 53.6 jit_solution(904105096719666548)
XLA Ops:
  0.0 0.0 copy-start
  0.0 1.1 %copy-done = bf16[2,1,56,3584]{3,2,1,0:T(8,128)(2,1)S(1)} copy-done((bf16[2,1,56,3584]{3,2,1,0:T(8,128)(2,1)S(1)}, bf16[2,1,56,3584]{3,2,1,0:T(8,128)(2,1)}, u32[]{:S(2)}) %copy-start) | copy-done | bytes 802840
  1.1 0.0 copy-start.1
  1.1 1.1 %copy-done.1 = bf16[2,1,56,3584]{3,2,1,0:T(8,128)(2,1)S(1)} copy-done((bf16[2,1,56,3584]{3,2,1,0:T(8,128)(2,1)S(1)}, bf16[2,1,56,3584]{3,2,1,0:T(8,128)(2,1)}, u32[]{:S(2)}) %copy-start.1) | copy-done | bytes 802840
  2.3 2.4 %shard_map.29 = f32[4,5,64,128]{3,2,1,0:T(8,128)S(1)} custom-call(bf16[2,1,56,3584]{3,2,1,0:T(8,128)(2,1)S(1)} %copy-done, bf16[2,1,56,3584]{3,2,1,0:T(8,128)(2,1)S(1)} %copy-done.1), custom_call_target="tpu_custom_call" | custom-call | tf_op jit(solution)/shard_map/pallas_call | solution.py:174
  4.7 0.7 %collective-permute-start = (f32[4,5,64,128]{3,2,1,0:T(8,128)S(1)}, f32[4,5,64,128]{3,2,1,0:T(8,128)S(1)}, u32[]{:S(2)}, u32[]{:S(2)}) collective-permute-start(f32[4,5,64,128]{3,2,1,0:T(8,128)S(1)} %shard_map.29), channel_id=1, source_target_pairs={{0,2},{1,3},{2,0},{3,1},{4,6},{5,7},{6,4},{7,5},{8,10},{9,11},{10,... | collective-permute-start | bytes 1966088 | tf_op jit(solution)/shard_map/ppermute | solution.py:344
  5.5 2.4 %shard_map.28 = f32[4,5,64,128]{3,2,1,0:T(8,128)S(1)} custom-call(bf16[2,1,56,3584]{3,2,1,0:T(8,128)(2,1)S(1)} %copy-done, bf16[2,1,56,3584]{3,2,1,0:T(8,128)(2,1)S(1)} %copy-done.1), custom_call_target="tpu_custom_call" | custom-call | tf_op jit(solution)/shard_map/pallas_call | solution.py:174
  7.9 0.0 collective-permute-done
  8.0 1.3 %collective-permute-start.1 = (f32[2,5,64,128]{3,2,1,0:T(8,128)S(1)}, f32[2,5,64,128]{3,2,1,0:T(8,128)S(1)}, u32[]{:S(2)}, u32[]{:S(2)}) collective-permute-start(f32[2,5,64,128]{3,2,1,0:T(8,128)S(1)} %slice_add_fusion), channel_id=1, source_target_pairs={{0,1},{1,0},{2,6},{3,7},{4,5},{5,4},{6,2},{7,3},{8,9},{9,8},{10,14... | collective-permute-start | bytes 983048 | tf_op jit(solution)/shard_map/ppermute | solution.py:344
  9.3 5.0 %collective-permute-done.1 = f32[2,5,64,128]{3,2,1,0:T(8,128)S(1)} collective-permute-done((f32[2,5,64,128]{3,2,1,0:T(8,128)S(1)}, f32[2,5,64,128]{3,2,1,0:T(8,128)S(1)}, u32[]{:S(2)}, u32[]{:S(2)}) %collective-permute-start.1) | collective-permute-done | bytes 327712 | tf_op jit(solution)/shard_map/ppermute | solution.py:344
  14.3 1.3 %collective-permute-start.2 = (f32[5,64,128]{2,1,0:T(8,128)S(1)}, f32[5,64,128]{2,1,0:T(8,128)S(1)}, u32[]{:S(2)}, u32[]{:S(2)}) collective-permute-start(f32[5,64,128]{2,1,0:T(8,128)S(1)} %fusion), channel_id=1, source_target_pairs={{0,4},{1,5},{2,3},{3,2},{4,0},{5,1},{6,7},{7,6},{8,12},{9,13},{10,... | collective-permute-start | bytes 491528 | tf_op jit(solution)/shard_map/ppermute | solution.py:344
  15.6 3.3 %collective-permute-done.2 = f32[5,64,128]{2,1,0:T(8,128)S(1)} collective-permute-done((f32[5,64,128]{2,1,0:T(8,128)S(1)}, f32[5,64,128]{2,1,0:T(8,128)S(1)}, u32[]{:S(2)}, u32[]{:S(2)}) %collective-permute-start.2) | collective-permute-done | bytes 163872 | tf_op jit(solution)/shard_map/ppermute | solution.py:344
  18.8 0.1 collective-permute-start.3
  19.0 6.8 %collective-permute-done.3 = f32[5,64,128]{2,1,0:T(8,128)S(1)} collective-permute-done((f32[5,64,128]{2,1,0:T(8,128)S(1)}, f32[5,64,128]{2,1,0:T(8,128)S(1)}, u32[]{:S(2)}, u32[]{:S(2)}) %collective-permute-start.3) | collective-permute-done | bytes 163872 | tf_op jit(solution)/shard_map/ppermute | solution.py:344
  25.8 0.1 collective-permute-start.4
  25.8 4.2 %collective-permute-done.4 = f32[5,64,128]{2,1,0:T(8,128)S(1)} collective-permute-done((f32[5,64,128]{2,1,0:T(8,128)S(1)}, f32[5,64,128]{2,1,0:T(8,128)S(1)}, u32[]{:S(2)}, u32[]{:S(2)}) %collective-permute-start.4) | collective-permute-done | bytes 163872 | tf_op jit(solution)/shard_map/ppermute | solution.py:344
  30.0 1.3 %collective-permute-start.5 = (f32[5,64,128]{2,1,0:T(8,128)S(1)}, f32[5,64,128]{2,1,0:T(8,128)S(1)}, u32[]{:S(2)}, u32[]{:S(2)}) collective-permute-start(f32[5,64,128]{2,1,0:T(8,128)S(1)} %add.41), channel_id=1, source_target_pairs={{0,1},{1,0},{2,3},{3,2},{4,5},{5,4},{6,7},{7,6},{8,9},{9,8},{10,11... | collective-permute-start | bytes 491528 | tf_op jit(solution)/shard_map/ppermute | solution.py:344
  31.3 3.0 %collective-permute-done.5 = f32[5,64,128]{2,1,0:T(8,128)S(1)} collective-permute-done((f32[5,64,128]{2,1,0:T(8,128)S(1)}, f32[5,64,128]{2,1,0:T(8,128)S(1)}, u32[]{:S(2)}, u32[]{:S(2)}) %collective-permute-start.5) | collective-permute-done | bytes 163872 | tf_op jit(solution)/shard_map/ppermute | solution.py:344
  34.3 1.3 %collective-permute-start.6 = (f32[2,5,64,128]{3,2,1,0:T(8,128)S(1)}, f32[2,5,64,128]{3,2,1,0:T(8,128)S(1)}, u32[]{:S(2)}, u32[]{:S(2)}) collective-permute-start(f32[2,5,64,128]{3,2,1,0:T(8,128)S(1)} %pad_maximum_fusion.near_ref), channel_id=1, source_target_pairs={{0,4},{1,5},{2,6},{3,7},{4,0},{5,1},{6,2},{7,3},{8,12},{9,13},{10,... | collective-permute-start | bytes 983048 | tf_op jit(solution)/shard_map/ppermute | solution.py:344
  35.6 4.7 %collective-permute-done.6.far_ref = f32[2,5,64,128]{3,2,1,0:T(8,128)S(1)} collective-permute-done((f32[2,5,64,128]{3,2,1,0:T(8,128)S(1)}, f32[2,5,64,128]{3,2,1,0:T(8,128)S(1)}, u32[]{:S(2)}, u32[]{:S(2)}) %collective-permute-start.6) | collective-permute-done | bytes 327712 | tf_op jit(solution)/shard_map/ppermute | solution.py:344
  40.3 4.5 %shard_map.30 = f32[64,576]{1,0:T(8,128)S(1)} custom-call(f32[2,5,64,128]{3,2,1,0:T(8,128)S(1)} %pad_maximum_fusion.near_ref, f32[2,5,64,128]{3,2,1,0:T(8,128)S(1)} %collective-permute-done.6.far_ref), custom_call_target="tpu_custom_call" | custom-call | tf_op jit(solution)/shard_map/pallas_call | solution.py:311
  44.8 7.0 %collective-permute-start.7 = (f32[64,576]{1,0:T(8,128)S(1)}, f32[64,576]{1,0:T(8,128)S(1)}, u32[]{:S(2)}, u32[]{:S(2)}) collective-permute-start(f32[64,576]{1,0:T(8,128)S(1)} %shard_map.30), channel_id=1, source_target_pairs={{0,2},{1,3},{2,0},{3,1},{4,6},{5,7},{6,4},{7,5},{8,10},{9,11},{10,... | collective-permute-start | bytes 442376 | tf_op jit(solution)/shard_map/ppermute | solution.py:344
  51.8 1.0 %collective-permute-done.7 = f32[64,576]{1,0:T(8,128)S(1)} collective-permute-done((f32[64,576]{1,0:T(8,128)S(1)}, f32[64,576]{1,0:T(8,128)S(1)}, u32[]{:S(2)}, u32[]{:S(2)}) %collective-permute-start.7) | collective-permute-done | bytes 147488 | tf_op jit(solution)/shard_map/ppermute | solution.py:344
  52.8 0.7 %maximum_select_fusion = f32[2,64,576]{2,1,0:T(8,128)} fusion(f32[1,64,576]{2,1,0:T(8,128)S(1)} %bitcast.13, f32[1,64,576]{2,1,0:T(8,128)S(1)} %bitcast.10, pred[]{:T(512)S(6)} %eq.3), kind=kLoop, calls=%fused_computation.2 | loop fusion | flops 221184 | bytes 589825 | tf_op jit(solution)/shard_map/jit(_where)/select_n | solution.py:358
  (6 shorter events, 0.2 us)
Async XLA Ops:
  0.0 1.1 %copy-start = (bf16[2,1,56,3584]{3,2,1,0:T(8,128)(2,1)S(1)}, bf16[2,1,56,3584]{3,2,1,0:T(8,128)(2,1)}, u32[]{:S(2)}) copy-start(bf16[2,1,56,3584]{3,2,1,0:T(8,128)(2,1)} %x_hbm.3) | copy-start | bytes 2408452
  1.1 1.1 %copy-start.1 = (bf16[2,1,56,3584]{3,2,1,0:T(8,128)(2,1)S(1)}, bf16[2,1,56,3584]{3,2,1,0:T(8,128)(2,1)}, u32[]{:S(2)}) copy-start(bf16[2,1,56,3584]{3,2,1,0:T(8,128)(2,1)} %g_hbm.3) | copy-start | bytes 2408452
  4.7 3.2 %collective-permute-start = (f32[4,5,64,128]{3,2,1,0:T(8,128)S(1)}, f32[4,5,64,128]{3,2,1,0:T(8,128)S(1)}, u32[]{:S(2)}, u32[]{:S(2)}) collective-permute-start(f32[4,5,64,128]{3,2,1,0:T(8,128)S(1)} %shard_map.29), channel_id=1, source_target_pairs={{0,2},{1,3},{2,0},{3,1},{4,6},{5,7},{6,4},{7,5},{8,10},{9,11},{10,... | collective-permute-start | bytes 1966088 | tf_op jit(solution)/shard_map/ppermute | solution.py:344
  8.0 6.3 %collective-permute-start.1 = (f32[2,5,64,128]{3,2,1,0:T(8,128)S(1)}, f32[2,5,64,128]{3,2,1,0:T(8,128)S(1)}, u32[]{:S(2)}, u32[]{:S(2)}) collective-permute-start(f32[2,5,64,128]{3,2,1,0:T(8,128)S(1)} %slice_add_fusion), channel_id=1, source_target_pairs={{0,1},{1,0},{2,6},{3,7},{4,5},{5,4},{6,2},{7,3},{8,9},{9,8},{10,14... | collective-permute-start | bytes 983048 | tf_op jit(solution)/shard_map/ppermute | solution.py:344
  14.3 4.5 %collective-permute-start.2 = (f32[5,64,128]{2,1,0:T(8,128)S(1)}, f32[5,64,128]{2,1,0:T(8,128)S(1)}, u32[]{:S(2)}, u32[]{:S(2)}) collective-permute-start(f32[5,64,128]{2,1,0:T(8,128)S(1)} %fusion), channel_id=1, source_target_pairs={{0,4},{1,5},{2,3},{3,2},{4,0},{5,1},{6,7},{7,6},{8,12},{9,13},{10,... | collective-permute-start | bytes 491528 | tf_op jit(solution)/shard_map/ppermute | solution.py:344
  18.8 6.9 %collective-permute-start.3 = (f32[5,64,128]{2,1,0:T(8,128)S(1)}, f32[5,64,128]{2,1,0:T(8,128)S(1)}, u32[]{:S(2)}, u32[]{:S(2)}) collective-permute-start(f32[5,64,128]{2,1,0:T(8,128)S(1)} %fusion.2), channel_id=1, source_target_pairs={{0,8},{1,9},{2,18},{3,19},{4,12},{5,13},{6,22},{7,23},{8,0},{9,1},... | collective-permute-start | bytes 491528 | tf_op jit(solution)/shard_map/ppermute | solution.py:344
  25.8 4.2 %collective-permute-start.4 = (f32[5,64,128]{2,1,0:T(8,128)S(1)}, f32[5,64,128]{2,1,0:T(8,128)S(1)}, u32[]{:S(2)}, u32[]{:S(2)}) collective-permute-start(f32[5,64,128]{2,1,0:T(8,128)S(1)} %add.40), channel_id=1, source_target_pairs={{0,16},{1,17},{2,10},{3,11},{4,20},{5,21},{6,14},{7,15},{8,24},{9,... | collective-permute-start | bytes 491528 | tf_op jit(solution)/shard_map/ppermute | solution.py:344
  30.0 4.3 %collective-permute-start.5 = (f32[5,64,128]{2,1,0:T(8,128)S(1)}, f32[5,64,128]{2,1,0:T(8,128)S(1)}, u32[]{:S(2)}, u32[]{:S(2)}) collective-permute-start(f32[5,64,128]{2,1,0:T(8,128)S(1)} %add.41), channel_id=1, source_target_pairs={{0,1},{1,0},{2,3},{3,2},{4,5},{5,4},{6,7},{7,6},{8,9},{9,8},{10,11... | collective-permute-start | bytes 491528 | tf_op jit(solution)/shard_map/ppermute | solution.py:344
  34.3 6.0 %collective-permute-start.6 = (f32[2,5,64,128]{3,2,1,0:T(8,128)S(1)}, f32[2,5,64,128]{3,2,1,0:T(8,128)S(1)}, u32[]{:S(2)}, u32[]{:S(2)}) collective-permute-start(f32[2,5,64,128]{3,2,1,0:T(8,128)S(1)} %pad_maximum_fusion.near_ref), channel_id=1, source_target_pairs={{0,4},{1,5},{2,6},{3,7},{4,0},{5,1},{6,2},{7,3},{8,12},{9,13},{10,... | collective-permute-start | bytes 983048 | tf_op jit(solution)/shard_map/ppermute | solution.py:344
  44.8 8.0 %collective-permute-start.7 = (f32[64,576]{1,0:T(8,128)S(1)}, f32[64,576]{1,0:T(8,128)S(1)}, u32[]{:S(2)}, u32[]{:S(2)}) collective-permute-start(f32[64,576]{1,0:T(8,128)S(1)} %shard_map.30), channel_id=1, source_target_pairs={{0,2},{1,3},{2,0},{3,1},{4,6},{5,7},{6,4},{7,5},{8,10},{9,11},{10,... | collective-permute-start | bytes 442376 | tf_op jit(solution)/shard_map/ppermute | solution.py:344

commit v3 on v2

--- a/solution.py
+++ b/solution.py
@@ -14,6 +14,7 @@
 ROW = 64
 QUART = 5
 DAMP = 0.1
+SUMS_VMEM = 53 * 2**20
 VMEM_LIMIT = 48 * 2**20
 F32 = jnp.float32
 BF16 = jnp.bfloat16
@@ -184,7 +185,7 @@
             pltpu.VMEM((2, n_edge + 16, PAIR), F32),
             pltpu.SemaphoreType.DMA((2,)),
         ],
-        compiler_params=pltpu.CompilerParams(vmem_limit_bytes=VMEM_LIMIT),
+        compiler_params=pltpu.CompilerParams(vmem_limit_bytes=SUMS_VMEM),
     )(feature_maps, output_grads)
 
 
@@ -209,10 +210,10 @@
     return jnp.where(diag, 1.0, 0.0) - m * inv, inv
 
 
-def final_kernel(total_rows, near_ref, far_ref, out_ref, quarters, m_ref, e_hi, e_lo):
+def final_kernel(total_rows, own_ref, beside_ref, below_ref, across_ref, out_ref, quarters, m_ref, e_hi, e_lo):
     _, first, second = chip_place()
-    quarters[0:2] = near_ref[...]
-    quarters[2:4] = far_ref[...]
+    for slot, ref in enumerate((own_ref, beside_ref, below_ref, across_ref)):
+        quarters[slot] = ref[...]
 
     def load(name):
         index = PLACE[name]
@@ -306,12 +307,12 @@
     out_ref[...] = v.T
 
 
-def precondition(near, far, total_rows):
+def precondition(parts, total_rows):
     n = TAPS * C
     return pl.pallas_call(
         functools.partial(final_kernel, float(total_rows)),
         out_shape=jax.ShapeDtypeStruct((C, n), F32),
-        in_specs=[pl.BlockSpec(memory_space=pltpu.VMEM)] * 2,
+        in_specs=[pl.BlockSpec(memory_space=pltpu.VMEM)] * 4,
         out_specs=pl.BlockSpec(memory_space=pltpu.VMEM),
         scratch_shapes=[
             pltpu.VMEM((4, QUART, C, PAIR), F32),
@@ -320,7 +321,7 @@
             pltpu.VMEM((n, n), BF16),
         ],
         compiler_params=pltpu.CompilerParams(vmem_limit_bytes=VMEM_LIMIT),
-    )(near, far)
+    )(*parts)
 
 
 def pairings(n_dp, n_grp):
@@ -345,14 +346,16 @@
     total_rows = feature_maps.shape[2] * feature_maps.shape[3] // C * feature_maps.shape[1] * n_dp * n_grp
     got = swap(local_sums(feature_maps, output_grads, False), cores)
     keep = local_sums(feature_maps, output_grads, True)
-    got_far = swap(keep[2:4] + got[2:4], halvings[0])
-    got_next = swap(keep[1] + got[1] + got_far[1], halvings[1])
-    own = keep[0] + got[0] + got_far[0] + got_next
+    far_next = swap(keep[3] + got[3], halvings[0])
+    far_own = swap(keep[2] + got[2], halvings[0])
+    got_next = swap(keep[1] + got[1] + far_next, halvings[1])
+    own = keep[0] + got[0] + far_own + got_next
     for p in doublings:
         own = own + swap(own, p)
-    near = jnp.stack([own, swap(own, gathers[0])])
-    far = swap(near, gathers[1])
-    mine = precondition(near, far, total_rows)
+    beside = swap(own, gathers[0])
+    below = swap(own, gathers[1])
+    across = swap(beside, gathers[1])
+    mine = precondition((own, beside, below, across), total_rows)
     other = swap(mine, cores)
     core = lax.rem(lax.axis_index("dp"), 2)
     return jnp.where(core == 0, jnp.stack([mine, other]), jnp.stack([other, mine]))

time: 53.8 us -> 49.3 us (0.916)
  waiting for transfers between devices: 27.9 us -> 23.1 us
  local copies, waits for them, and re-layouts: 2.28 us -> 0 us
  Pallas kernels: 9.36 us -> 10.8 us
  starting transfers between devices: 13.1 us -> 14.2 us
    ppermute x8 -> x10, waiting for transfers between devices: 27.9 us -> 23.1 us  [shards(): swap = lambda a, p: lax.ppermute(a, ('dp', 'grp'), p)]
    unnamed x4 -> x0, local copies, waits for them, and re-layouts: 2.28 us -> none
    pallas_call x2, Pallas kernels: 4.87 us -> 6.31 us  [local_sums(): pl.pallas_call(functools.partial(local_kernel, height, width, own), out_s...]
    ppermute x8 -> x10, starting transfers between devices: 13.1 us -> 14.2 us  [shards(): swap = lambda a, p: lax.ppermute(a, ('dp', 'grp'), p)]
  transfers between devices with their start and end apart: 8 -> 10, of which waited for: 7 -> 8; matrix products, arithmetic and copies ran while one was open for 0% -> 0% of each run, Pallas kernels for 5% -> 6%
where the time goes in v3:
time: 49.3 us; the launch traced here: 49.1 us
  waiting for transfers between devices  23.1 us (47%)
  starting transfers between devices  14.2 us (29%)
  Pallas kernels  10.8 us (22%)
  other arithmetic  0.89 us (2%)
    ppermute x10, waiting for transfers between devices, shards(): swap = lambda a, p: lax.ppermute(a, ('dp', 'grp'), p)  23.1 us
    ppermute x10, starting transfers between devices, shards(): swap = lambda a, p: lax.ppermute(a, ('dp', 'grp'), p)  14.2 us
    pallas_call x2, Pallas kernels, local_sums(): pl.pallas_call(functools.partial(local_kernel, height, width, own), out_s...  6.31 us
    pallas_call x1, Pallas kernels, precondition(): pl.pallas_call(functools.partial(final_kernel, float(total_rows)), out_sh...  4.49 us
  transfers between devices with their start and end apart: 10, of which 8 were waited for; matrix products, arithmetic and copies ran while one was open for 0% of the time, Pallas kernels for 6%

profile of v3, /device:TPU:25, one launch (start us, length us, event | category | flops | bytes accessed | tf_op | source)
XLA Modules:
  0.0 49.1 jit_solution(3219562583563385667)
XLA Ops:
  0.0 3.2 %shard_map.29 = f32[4,5,64,128]{3,2,1,0:T(8,128)S(1)} custom-call(bf16[2,1,56,3584]{3,2,1,0:T(8,128)(2,1)} %x_hbm.3, bf16[2,1,56,3584]{3,2,1,0:T(8,128)(2,1)} %g_hbm.3), custom_call_target="tpu_custom_call" | custom-call | tf_op jit(solution)/shard_map/pallas_call | solution.py:175
  3.2 0.7 %collective-permute-start = (f32[4,5,64,128]{3,2,1,0:T(8,128)S(1)}, f32[4,5,64,128]{3,2,1,0:T(8,128)S(1)}, u32[]{:S(2)}, u32[]{:S(2)}) collective-permute-start(f32[4,5,64,128]{3,2,1,0:T(8,128)S(1)} %shard_map.29), channel_id=1, source_target_pairs={{0,2},{1,3},{2,0},{3,1},{4,6},{5,7},{6,4},{7,5},{8,10},{9,11},{10,... | collective-permute-start | bytes 1966088 | tf_op jit(solution)/shard_map/ppermute | solution.py:345
  3.9 3.2 %shard_map.28 = f32[4,5,64,128]{3,2,1,0:T(8,128)S(1)} custom-call(bf16[2,1,56,3584]{3,2,1,0:T(8,128)(2,1)} %x_hbm.3, bf16[2,1,56,3584]{3,2,1,0:T(8,128)(2,1)} %g_hbm.3), custom_call_target="tpu_custom_call" | custom-call | tf_op jit(solution)/shard_map/pallas_call | solution.py:175
  7.1 0.0 collective-permute-done
  7.1 1.3 %collective-permute-start.2 = (f32[5,64,128]{2,1,0:T(8,128)S(1)}, f32[5,64,128]{2,1,0:T(8,128)S(1)}, u32[]{:S(2)}, u32[]{:S(2)}) collective-permute-start(f32[5,64,128]{2,1,0:T(8,128)S(1)} %get-tuple-element.6), channel_id=1, source_target_pairs={{0,1},{1,0},{2,6},{3,7},{4,5},{5,4},{6,2},{7,3},{8,9},{9,8},{10,14... | collective-permute-start | bytes 491528 | tf_op jit(solution)/shard_map/ppermute | solution.py:345
  8.4 0.2 collective-permute-start.1
  8.7 3.0 %collective-permute-done.2 = f32[5,64,128]{2,1,0:T(8,128)S(1)} collective-permute-done((f32[5,64,128]{2,1,0:T(8,128)S(1)}, f32[5,64,128]{2,1,0:T(8,128)S(1)}, u32[]{:S(2)}, u32[]{:S(2)}) %collective-permute-start.2) | collective-permute-done | bytes 163872 | tf_op jit(solution)/shard_map/ppermute | solution.py:345
  11.7 1.3 %collective-permute-start.3 = (f32[5,64,128]{2,1,0:T(8,128)S(1)}, f32[5,64,128]{2,1,0:T(8,128)S(1)}, u32[]{:S(2)}, u32[]{:S(2)}) collective-permute-start(f32[5,64,128]{2,1,0:T(8,128)S(1)} %fusion.2), channel_id=1, source_target_pairs={{0,4},{1,5},{2,3},{3,2},{4,0},{5,1},{6,7},{7,6},{8,12},{9,13},{10,... | collective-permute-start | bytes 491528 | tf_op jit(solution)/shard_map/ppermute | solution.py:345
  13.0 0.4 collective-permute-done.1
  13.4 2.8 %collective-permute-done.3 = f32[5,64,128]{2,1,0:T(8,128)S(1)} collective-permute-done((f32[5,64,128]{2,1,0:T(8,128)S(1)}, f32[5,64,128]{2,1,0:T(8,128)S(1)}, u32[]{:S(2)}, u32[]{:S(2)}) %collective-permute-start.3) | collective-permute-done | bytes 163872 | tf_op jit(solution)/shard_map/ppermute | solution.py:345
  16.3 0.1 collective-permute-start.4
  16.4 6.8 %collective-permute-done.4 = f32[5,64,128]{2,1,0:T(8,128)S(1)} collective-permute-done((f32[5,64,128]{2,1,0:T(8,128)S(1)}, f32[5,64,128]{2,1,0:T(8,128)S(1)}, u32[]{:S(2)}, u32[]{:S(2)}) %collective-permute-start.4) | collective-permute-done | bytes 163872 | tf_op jit(solution)/shard_map/ppermute | solution.py:345
  23.2 0.1 collective-permute-start.5
  23.2 4.2 %collective-permute-done.5 = f32[5,64,128]{2,1,0:T(8,128)S(1)} collective-permute-done((f32[5,64,128]{2,1,0:T(8,128)S(1)}, f32[5,64,128]{2,1,0:T(8,128)S(1)}, u32[]{:S(2)}, u32[]{:S(2)}) %collective-permute-start.5) | collective-permute-done | bytes 163872 | tf_op jit(solution)/shard_map/ppermute | solution.py:345
  27.4 1.3 %collective-permute-start.6 = (f32[5,64,128]{2,1,0:T(8,128)S(1)}, f32[5,64,128]{2,1,0:T(8,128)S(1)}, u32[]{:S(2)}, u32[]{:S(2)}) collective-permute-start(f32[5,64,128]{2,1,0:T(8,128)S(1)} %add.51.own_ref), channel_id=1, source_target_pairs={{0,1},{1,0},{2,3},{3,2},{4,5},{5,4},{6,7},{7,6},{8,9},{9,8},{10,11... | collective-permute-start | bytes 491528 | tf_op jit(solution)/shard_map/ppermute | solution.py:345
  28.7 1.2 %collective-permute-start.7 = (f32[5,64,128]{2,1,0:T(8,128)S(1)}, f32[5,64,128]{2,1,0:T(8,128)S(1)}, u32[]{:S(2)}, u32[]{:S(2)}) collective-permute-start(f32[5,64,128]{2,1,0:T(8,128)S(1)} %add.51.own_ref), channel_id=1, source_target_pairs={{0,4},{1,5},{2,6},{3,7},{4,0},{5,1},{6,2},{7,3},{8,12},{9,13},{10,... | collective-permute-start | bytes 491528 | tf_op jit(solution)/shard_map/ppermute | solution.py:345
  29.9 1.7 %collective-permute-done.6.beside_ref = f32[5,64,128]{2,1,0:T(8,128)S(1)} collective-permute-done((f32[5,64,128]{2,1,0:T(8,128)S(1)}, f32[5,64,128]{2,1,0:T(8,128)S(1)}, u32[]{:S(2)}, u32[]{:S(2)}) %collective-permute-start.6) | collective-permute-done | bytes 163872 | tf_op jit(solution)/shard_map/ppermute | solution.py:345
  31.7 1.2 %collective-permute-start.8 = (f32[5,64,128]{2,1,0:T(8,128)S(1)}, f32[5,64,128]{2,1,0:T(8,128)S(1)}, u32[]{:S(2)}, u32[]{:S(2)}) collective-permute-start(f32[5,64,128]{2,1,0:T(8,128)S(1)} %collective-permute-done.6.beside_ref), channel_id=1, source_target_pairs={{0,4},{1,5},{2,6},{3,7},{4,0},{5,1},{6,2},{7,3},{8,12},{9,13},{10,... | collective-permute-start | bytes 491528 | tf_op jit(solution)/shard_map/ppermute | solution.py:345
  32.9 0.0 collective-permute-done.7.below_ref
  32.9 3.2 %collective-permute-done.8.across_ref = f32[5,64,128]{2,1,0:T(8,128)S(1)} collective-permute-done((f32[5,64,128]{2,1,0:T(8,128)S(1)}, f32[5,64,128]{2,1,0:T(8,128)S(1)}, u32[]{:S(2)}, u32[]{:S(2)}) %collective-permute-start.8) | collective-permute-done | bytes 163872 | tf_op jit(solution)/shard_map/ppermute | solution.py:345
  36.1 4.5 %shard_map.30 = f32[64,576]{1,0:T(8,128)S(1)} custom-call(f32[5,64,128]{2,1,0:T(8,128)S(1)} %add.51.own_ref, f32[5,64,128]{2,1,0:T(8,128)S(1)} %collective-permute-done.6.beside_ref, f32[5,64,128]{2,1,0:T(8,128)S(1)} %collective-permute-done.7.below_ref, f32[5,64,128]{2,1,0:T(8,128)S(1)} %collective-permute-done.8.across_ref), custom_call_target="tpu_custom_call" | custom-call | tf_op jit(solution)/shard_map/pallas_call | solution.py:312
  40.6 6.7 %collective-permute-start.9 = (f32[64,576]{1,0:T(8,128)S(1)}, f32[64,576]{1,0:T(8,128)S(1)}, u32[]{:S(2)}, u32[]{:S(2)}) collective-permute-start(f32[64,576]{1,0:T(8,128)S(1)} %shard_map.30), channel_id=1, source_target_pairs={{0,2},{1,3},{2,0},{3,1},{4,6},{5,7},{6,4},{7,5},{8,10},{9,11},{10,... | collective-permute-start | bytes 442376 | tf_op jit(solution)/shard_map/ppermute | solution.py:345
  47.3 1.0 %collective-permute-done.9 = f32[64,576]{1,0:T(8,128)S(1)} collective-permute-done((f32[64,576]{1,0:T(8,128)S(1)}, f32[64,576]{1,0:T(8,128)S(1)}, u32[]{:S(2)}, u32[]{:S(2)}) %collective-permute-start.9) | collective-permute-done | bytes 147488 | tf_op jit(solution)/shard_map/ppermute | solution.py:345
  48.4 0.7 %maximum_select_fusion = f32[2,64,576]{2,1,0:T(8,128)} fusion(f32[1,64,576]{2,1,0:T(8,128)S(1)} %bitcast.17, f32[1,64,576]{2,1,0:T(8,128)S(1)} %bitcast.16, pred[]{:T(512)S(6)} %eq.3), kind=kLoop, calls=%fused_computation | loop fusion | flops 221184 | bytes 589825 | tf_op jit(solution)/shard_map/jit(_where)/select_n | solution.py:361
  (5 shorter events, 0.1 us)
Async XLA Ops:
  3.2 3.9 %collective-permute-start = (f32[4,5,64,128]{3,2,1,0:T(8,128)S(1)}, f32[4,5,64,128]{3,2,1,0:T(8,128)S(1)}, u32[]{:S(2)}, u32[]{:S(2)}) collective-permute-start(f32[4,5,64,128]{3,2,1,0:T(8,128)S(1)} %shard_map.29), channel_id=1, source_target_pairs={{0,2},{1,3},{2,0},{3,1},{4,6},{5,7},{6,4},{7,5},{8,10},{9,11},{10,... | collective-permute-start | bytes 1966088 | tf_op jit(solution)/shard_map/ppermute | solution.py:345
  7.1 4.5 %collective-permute-start.2 = (f32[5,64,128]{2,1,0:T(8,128)S(1)}, f32[5,64,128]{2,1,0:T(8,128)S(1)}, u32[]{:S(2)}, u32[]{:S(2)}) collective-permute-start(f32[5,64,128]{2,1,0:T(8,128)S(1)} %get-tuple-element.6), channel_id=1, source_target_pairs={{0,1},{1,0},{2,6},{3,7},{4,5},{5,4},{6,2},{7,3},{8,9},{9,8},{10,14... | collective-permute-start | bytes 491528 | tf_op jit(solution)/shard_map/ppermute | solution.py:345
  8.4 5.0 %collective-permute-start.1 = (f32[5,64,128]{2,1,0:T(8,128)S(1)}, f32[5,64,128]{2,1,0:T(8,128)S(1)}, u32[]{:S(2)}, u32[]{:S(2)}) collective-permute-start(f32[5,64,128]{2,1,0:T(8,128)S(1)} %get-tuple-element.5), channel_id=1, source_target_pairs={{0,1},{1,0},{2,6},{3,7},{4,5},{5,4},{6,2},{7,3},{8,9},{9,8},{10,14... | collective-permute-start | bytes 491528 | tf_op jit(solution)/shard_map/ppermute | solution.py:345
  11.7 4.5 %collective-permute-start.3 = (f32[5,64,128]{2,1,0:T(8,128)S(1)}, f32[5,64,128]{2,1,0:T(8,128)S(1)}, u32[]{:S(2)}, u32[]{:S(2)}) collective-permute-start(f32[5,64,128]{2,1,0:T(8,128)S(1)} %fusion.2), channel_id=1, source_target_pairs={{0,4},{1,5},{2,3},{3,2},{4,0},{5,1},{6,7},{7,6},{8,12},{9,13},{10,... | collective-permute-start | bytes 491528 | tf_op jit(solution)/shard_map/ppermute | solution.py:345
  16.3 6.9 %collective-permute-start.4 = (f32[5,64,128]{2,1,0:T(8,128)S(1)}, f32[5,64,128]{2,1,0:T(8,128)S(1)}, u32[]{:S(2)}, u32[]{:S(2)}) collective-permute-start(f32[5,64,128]{2,1,0:T(8,128)S(1)} %fusion.6), channel_id=1, source_target_pairs={{0,8},{1,9},{2,18},{3,19},{4,12},{5,13},{6,22},{7,23},{8,0},{9,1},... | collective-permute-start | bytes 491528 | tf_op jit(solution)/shard_map/ppermute | solution.py:345
  23.2 4.2 %collective-permute-start.5 = (f32[5,64,128]{2,1,0:T(8,128)S(1)}, f32[5,64,128]{2,1,0:T(8,128)S(1)}, u32[]{:S(2)}, u32[]{:S(2)}) collective-permute-start(f32[5,64,128]{2,1,0:T(8,128)S(1)} %add.50), channel_id=1, source_target_pairs={{0,16},{1,17},{2,10},{3,11},{4,20},{5,21},{6,14},{7,15},{8,24},{9,... | collective-permute-start | bytes 491528 | tf_op jit(solution)/shard_map/ppermute | solution.py:345
  27.4 4.2 %collective-permute-start.6 = (f32[5,64,128]{2,1,0:T(8,128)S(1)}, f32[5,64,128]{2,1,0:T(8,128)S(1)}, u32[]{:S(2)}, u32[]{:S(2)}) collective-permute-start(f32[5,64,128]{2,1,0:T(8,128)S(1)} %add.51.own_ref), channel_id=1, source_target_pairs={{0,1},{1,0},{2,3},{3,2},{4,5},{5,4},{6,7},{7,6},{8,9},{9,8},{10,11... | collective-permute-start | bytes 491528 | tf_op jit(solution)/shard_map/ppermute | solution.py:345
  28.7 4.2 %collective-permute-start.7 = (f32[5,64,128]{2,1,0:T(8,128)S(1)}, f32[5,64,128]{2,1,0:T(8,128)S(1)}, u32[]{:S(2)}, u32[]{:S(2)}) collective-permute-start(f32[5,64,128]{2,1,0:T(8,128)S(1)} %add.51.own_ref), channel_id=1, source_target_pairs={{0,4},{1,5},{2,6},{3,7},{4,0},{5,1},{6,2},{7,3},{8,12},{9,13},{10,... | collective-permute-start | bytes 491528 | tf_op jit(solution)/shard_map/ppermute | solution.py:345
  31.7 4.5 %collective-permute-start.8 = (f32[5,64,128]{2,1,0:T(8,128)S(1)}, f32[5,64,128]{2,1,0:T(8,128)S(1)}, u32[]{:S(2)}, u32[]{:S(2)}) collective-permute-start(f32[5,64,128]{2,1,0:T(8,128)S(1)} %collective-permute-done.6.beside_ref), channel_id=1, source_target_pairs={{0,4},{1,5},{2,6},{3,7},{4,0},{5,1},{6,2},{7,3},{8,12},{9,13},{10,... | collective-permute-start | bytes 491528 | tf_op jit(solution)/shard_map/ppermute | solution.py:345
  40.6 7.7 %collective-permute-start.9 = (f32[64,576]{1,0:T(8,128)S(1)}, f32[64,576]{1,0:T(8,128)S(1)}, u32[]{:S(2)}, u32[]{:S(2)}) collective-permute-start(f32[64,576]{1,0:T(8,128)S(1)} %shard_map.30), channel_id=1, source_target_pairs={{0,2},{1,3},{2,0},{3,1},{4,6},{5,7},{6,4},{7,5},{8,10},{9,11},{10,... | collective-permute-start | bytes 442376 | tf_op jit(solution)/shard_map/ppermute | solution.py:345

commit v4 on v3

--- a/solution.py
+++ b/solution.py
@@ -12,7 +12,7 @@
 TAPS = 9
 PAIR = 2 * C
 ROW = 64
-QUART = 5
+QUART = 4
 DAMP = 0.1
 SUMS_VMEM = 53 * 2**20
 VMEM_LIMIT = 48 * 2**20
@@ -20,12 +20,16 @@
 BF16 = jnp.bfloat16
 
 PAIRS = (
-    "x1m", "x1z", "cc1", "x2m", "x2z",
-    "cc2", "x22", "x0z", "cc0", "r0z",
-    "r1z", "k0", "k1", "w0z", "w1z",
-    "w2z", "h0", "h1", "h2", "gg",
+    "x1m", "x1z", "cc1", "x2m",
+    "x2z", "cc2", "x22", "kk",
+    "cg", "w0z", "w1z", "w2z",
+    "h0", "h1", "h2", "r01",
 )
 PLACE = {name: index for index, name in enumerate(PAIRS)}
+LAST = QUART * ROW
+PIECE = ROW // 4
+DIAGS = LAST + PIECE
+QROWS = DIAGS + 8
 
 
 def contract0(a, b):
@@ -110,7 +114,13 @@
     def store(name, value):
         index = PLACE[name]
         slot = slot_of(index // QUART, layer, first, second)
-        out_ref[slot, index % QUART] = value
+        at = index % QUART * ROW
+        out_ref[slot, at : at + ROW, :] = value
+
+    row = lax.broadcasted_iota(jnp.int32, (ROW, PAIR), 0)
+    col = lax.rem(lax.broadcasted_iota(jnp.int32, (ROW, PAIR), 1), C)
+    pack = lambda a, b: jnp.where(row >= col, a, b)
+    diagonal = lambda a: jnp.sum(jnp.where(row == col, a, 0.0), axis=0, keepdims=True)
 
     p = product(0, (-1, 0), 1) + product(0, (1,), 1)
     at_s = dict(zip((-1, 0, 1), p))
@@ -118,7 +128,7 @@
     w0 = odd(at_s, 0, -1)
     p = product(1, (-1, 0), None) + product(1, (1,), None)
     at_s = dict(zip((-1, 0, 1), p))
-    store("x0z", table(at_s, 0, 0))
+    x0z = table(at_s, 0, 0)
     store("h0", jnp.where(low, table(at_s, 0, 1), w0))
     store("w1z", table(at_s, PAIR, 0))
     w1 = odd(at_s, PAIR, -1)
@@ -136,7 +146,7 @@
     store("x22", jnp.where(low, x12, pltpu.roll(table(at_s, 0, 1), C, 1)))
     gl = lhs_t[PAIR : 2 * PAIR, :]
     gg = lax.dot_general(gl, gl, (((1,), (1,)), ((), ())), preferred_element_type=F32)
-    store("gg", gg[0:C, :] + pltpu.roll(gg[C:PAIR, :], C, 1))
+    gx = jnp.where(low, gg[0:C, :] + pltpu.roll(gg[C:PAIR, :], C, 1), pltpu.roll(x0z, C, 1))
     fl = [
         jnp.where(
             low,
@@ -145,32 +155,47 @@
         ).astype(BF16)
         for d in (1, 2, 3)
     ]
-    for d, name in enumerate(("cc0", "cc1", "cc2")):
+    for d, name in enumerate(("cg", "cc1", "cc2")):
         q = contract0(fl[0], fl[d])
-        store(name, jnp.where(low, q[0:C, :], q[C:PAIR, :]))
+        both = jnp.where(low, q[0:C, :], q[C:PAIR, :])
+        if d == 0:
+            name, both = "cg", pack(both, gx)
+        store(name, both)
     line = lax.broadcasted_iota(jnp.int32, (n_edge, PAIR), 0)
     lane = lax.broadcasted_iota(jnp.int32, (n_edge, PAIR), 1)
     corner = ((line == 0) & (lane < C)) | ((line == wp - 1) & (lane >= C))
     halves = []
+    lines = []
+    corners = []
     for e in range(2):
         zero = edges[e, 8 : 8 + n_edge, :]
         here = zero.astype(BF16)
         after = edges[e, 9 : 9 + n_edge, :].astype(BF16)
         at_s = {0: contract0(here, here), 1: contract0(here, after)}
-        store(("r0z", "r1z")[e], table(at_s, 0, 0))
+        lines.append(table(at_s, 0, 0))
         halves.append(table(at_s, 0, 1))
         only = jnp.where(corner, zero, 0.0).astype(BF16)
         q = contract0(only, only)
-        store(("k0", "k1")[e], jnp.where(low, q[0:C, :], q[C:PAIR, :]))
+        corners.append(jnp.where(low, q[0:C, :], q[C:PAIR, :]))
     store("h1", jnp.where(low, halves[0], w1))
     store("h2", jnp.where(low, halves[1], w2))
+    store("kk", pack(corners[0], corners[1]))
+    store("r01", jnp.where(low, pltpu.roll(lines[0], C, 1), lines[1]))
+    rx = jnp.where(low, pack(lines[0], lines[1]), x0z)
+    diags = jnp.concatenate(
+        [diagonal(corners[1]), diagonal(gx), diagonal(lines[1]), jnp.zeros((5, PAIR), F32)], axis=0
+    )
+    for quarter in range(4):
+        slot = slot_of(quarter, layer, first, second)
+        out_ref[slot, LAST:DIAGS, :] = rx[quarter * PIECE : (quarter + 1) * PIECE, :]
+        out_ref[slot, DIAGS:QROWS, :] = diags
 
 
 def local_sums(feature_maps, output_grads, own):
     height = feature_maps.shape[2]
     width = feature_maps.shape[3] // C
     wp = width // 2
-    shape = jax.ShapeDtypeStruct((4, QUART, C, PAIR), F32)
+    shape = jax.ShapeDtypeStruct((4, QROWS, PAIR), F32)
     n_edge = (wp + 15) // 16 * 16
     return pl.pallas_call(
         functools.partial(local_kernel, height, width, own),
@@ -210,27 +235,48 @@
     return jnp.where(diag, 1.0, 0.0) - m * inv, inv
 
 
-def final_kernel(total_rows, own_ref, beside_ref, below_ref, across_ref, out_ref, quarters, m_ref, e_hi, e_lo):
+def final_kernel(total_rows, own_ref, beside_ref, below_ref, across_ref, out_ref, quarters, m_hi, m_lo):
     _, first, second = chip_place()
     for slot, ref in enumerate((own_ref, beside_ref, below_ref, across_ref)):
         quarters[slot] = ref[...]
 
+    def slot(quarter):
+        return gathered_slot(quarter, first, second)
+
     def load(name):
         index = PLACE[name]
-        both = quarters[gathered_slot(index // QUART, first, second), index % QUART]
+        at = index % QUART * ROW
+        both = quarters[slot(index // QUART), at : at + ROW, :]
         return both[:, 0:C], both[:, C:PAIR]
 
-    x0 = dict(zip((0, 1), load("x0z")))
-    h0, w00 = load("h0")
-    x0[2] = h0
-    row0 = dict(zip((0, 1), load("r0z")))
-    row0[2], w10 = load("h1")
-    row1 = dict(zip((0, 1), load("r1z")))
-    row1[2], w20 = load("h2")
+    row = lax.broadcasted_iota(jnp.int32, (C, C), 0)
+    col = lax.broadcasted_iota(jnp.int32, (C, C), 1)
+    diags = quarters[slot(0), DIAGS:QROWS, :]
+
+    def unpack(block, line, at):
+        flipped = block.T
+        mirrored = jnp.where(row < col, block, flipped)
+        diagonal = jnp.broadcast_to(diags[line : line + 1, at : at + C], (C, C))
+        return jnp.where(row >= col, block, flipped), jnp.where(row == col, diagonal, mirrored)
+
+    rx = jnp.concatenate([quarters[slot(quarter), LAST:DIAGS, :] for quarter in range(4)], axis=0)
+    x0 = {1: rx[:, C:PAIR]}
+    row0 = {}
+    row1 = {}
     col0 = {}
     col1 = {}
-    col0[0], col1[0] = load("cc0")
-    corner = load("k0") + load("k1")
+    row0[0], row1[0] = unpack(rx[:, 0:C], 2, 0)
+    row0[1], row1[1] = load("r01")
+    x0[2], w00 = load("h0")
+    row0[2], w10 = load("h1")
+    row1[2], w20 = load("h2")
+    low, high = load("cg")
+    col0[0], g = unpack(low, 1, 0)
+    col1[0], x0[0] = unpack(high, 1, C)
+    low, high = load("kk")
+    k00, k10 = unpack(low, 0, 0)
+    k01, k11 = unpack(high, 0, C)
+    corner = (k00, k01, k10, k11)
     down = {}
     for dr in (1, 2):
         down[dr, -2], down[dr, -1] = load("x%dm" % dr)
@@ -238,16 +284,22 @@
         col0[dr], col1[dr] = load("cc%d" % dr)
     down[1, 2], down[2, 2] = load("x22")
 
+    squares = []
+
     def put(t, u, block):
-        m_ref[t * C : (t + 1) * C, u * C : (u + 1) * C] = block
+        high, rest = split(block)
+        m_hi[t * C : (t + 1) * C, u * C : (u + 1) * C] = high
+        m_lo[t * C : (t + 1) * C, u * C : (u + 1) * C] = rest
 
     def put_all(taps, block):
+        squares.append(2.0 * len(taps) * (block * block))
         for t, u in taps:
             put(t, u, block)
         flipped = block.T
         for t, u in taps:
             put(u, t, flipped)
 
+    on_diagonal = []
     for a in range(3):
         line = {}
         for dc in range(3):
@@ -266,6 +318,8 @@
                     block = block + corner[2]
                 if a == 2:
                     block = block + corner[0]
+            squares.append(block * block)
+            on_diagonal.append(block)
             put(3 * a + b, 3 * a + b, block)
         put_all([(3 * a, 3 * a + 1), (3 * a + 1, 3 * a + 2)], line[1])
         put_all([(3 * a, 3 * a + 2)], line[2])
@@ -282,11 +336,11 @@
             taps = [(3 * a + b, 3 * (a + dr) + b + dc) for a in starts for b in range(3) if 0 <= b + dc < 3]
             put_all(taps, down[dr, dc])
 
-    e, inv_a = normalized(m_ref[...])
-    hi, lo = split(e)
-    e_hi[...] = hi
-    e_lo[...] = lo
-    g, _ = load("gg")
+    n = TAPS * C
+    trace = jnp.sum(jnp.where(row == col, sum(on_diagonal), 0.0))
+    shift = DAMP * trace / n
+    inv_a = lax.rsqrt(jnp.sum(sum(squares)) + shift * (2.0 * trace + n * shift))
+    keep = 1.0 - inv_a * shift
     eg, inv_g = normalized(g)
     eg2 = dot3(eg, eg)
     pg = eg + dot3(eg, eg2) + eg2
@@ -299,8 +353,9 @@
 
     def apply(v):
         vh, vl = split(v)
-        both = jnp.dot(e_hi[...], jnp.concatenate([vh, vl], axis=1), preferred_element_type=F32)
-        return both[:, 0:C] + (both[:, C:PAIR] + jnp.dot(e_lo[...], vh, preferred_element_type=F32))
+        both = jnp.dot(m_hi[...], jnp.concatenate([vh, vl], axis=1), preferred_element_type=F32)
+        mv = both[:, 0:C] + (both[:, C:PAIR] + jnp.dot(m_lo[...], vh, preferred_element_type=F32))
+        return keep * v - inv_a * mv
 
     v = v + apply(v)
     v = v + apply(apply(v))
@@ -315,8 +370,7 @@
         in_specs=[pl.BlockSpec(memory_space=pltpu.VMEM)] * 4,
         out_specs=pl.BlockSpec(memory_space=pltpu.VMEM),
         scratch_shapes=[
-            pltpu.VMEM((4, QUART, C, PAIR), F32),
-            pltpu.VMEM((n, n), F32),
+            pltpu.VMEM((4, QROWS, PAIR), F32),
             pltpu.VMEM((n, n), BF16),
             pltpu.VMEM((n, n), BF16),
         ],
@@ -336,7 +390,7 @@
     orders = ([first, second] + doublings, [second, first] + doublings[::-1])
     pairs = lambda masks: [(i, i ^ masks[1 if i & core_bit else 0]) for i in range(n)]
     rounds = [pairs(masks) for masks in zip(*orders)]
-    return pairs((core_bit, core_bit)), rounds[:2], rounds[2:], (pairs((first, first)), pairs((second, second)))
+    return pairs((core_bit, core_bit)), rounds[:2], rounds[2:], (pairs((first, first)), pairs((second, second)), pairs((first + second, first + second)))
 
 
 def shards(feature_maps, output_grads):
@@ -354,7 +408,7 @@
         own = own + swap(own, p)
     beside = swap(own, gathers[0])
     below = swap(own, gathers[1])
-    across = swap(beside, gathers[1])
+    across = swap(own, gathers[2])
     mine = precondition((own, beside, below, across), total_rows)
     other = swap(mine, cores)
     core = lax.rem(lax.axis_index("dp"), 2)

time: 49.3 us -> 45.9 us (0.931)
  starting transfers between devices: 14.2 us -> 12.7 us
  waiting for transfers between devices: 23.1 us -> 21.7 us
    ppermute x10, starting transfers between devices: 14.2 us -> 12.7 us  [shards(): swap = lambda a, p: lax.ppermute(a, ('dp', 'grp'), p)]
    ppermute x10, waiting for transfers between devices: 23.1 us -> 21.7 us  [shards(): swap = lambda a, p: lax.ppermute(a, ('dp', 'grp'), p)]
  transfers between devices with their start and end apart: 10 -> 10, of which waited for: 8 -> 9; matrix products, arithmetic and copies ran while one was open for 0% -> 0% of each run, Pallas kernels for 6% -> 7%
where the time goes in v4:
time: 45.9 us; the launch traced here: 45.8 us
  waiting for transfers between devices  21.7 us (47%)
  starting transfers between devices  12.7 us (28%)
  Pallas kernels  10.4 us (23%)
  other arithmetic  0.91 us (2%)
    ppermute x10, waiting for transfers between devices, shards(): swap = lambda a, p: lax.ppermute(a, ('dp', 'grp'), p)  21.7 us
    ppermute x10, starting transfers between devices, shards(): swap = lambda a, p: lax.ppermute(a, ('dp', 'grp'), p)  12.7 us
    pallas_call x2, Pallas kernels, local_sums(): pl.pallas_call(functools.partial(local_kernel, height, width, own), out_s...  6.32 us
    pallas_call x1, Pallas kernels, precondition(): pl.pallas_call(functools.partial(final_kernel, float(total_rows)), out_sh...  4.07 us
  transfers between devices with their start and end apart: 10, of which 9 were waited for; matrix products, arithmetic and copies ran while one was open for 0% of the time, Pallas kernels for 7%

profile of v4, /device:TPU:25, one launch (start us, length us, event | category | flops | bytes accessed | tf_op | source)
XLA Modules:
  0.0 45.8 jit_solution(9300947020595392355)
XLA Ops:
  0.0 3.2 %shard_map.29 = f32[4,280,128]{2,1,0:T(8,128)S(1)} custom-call(bf16[2,1,56,3584]{3,2,1,0:T(8,128)(2,1)} %x_hbm.3, bf16[2,1,56,3584]{3,2,1,0:T(8,128)(2,1)} %g_hbm.3), custom_call_target="tpu_custom_call" | custom-call | tf_op jit(solution)/shard_map/pallas_call | solution.py:200
  3.2 0.7 %collective-permute-start = (f32[4,280,128]{2,1,0:T(8,128)S(1)}, f32[4,280,128]{2,1,0:T(8,128)S(1)}, u32[]{:S(2)}, u32[]{:S(2)}) collective-permute-start(f32[4,280,128]{2,1,0:T(8,128)S(1)} %shard_map.29), channel_id=1, source_target_pairs={{0,2},{1,3},{2,0},{3,1},{4,6},{5,7},{6,4},{7,5},{8,10},{9,11},{10,... | collective-permute-start | bytes 1720328 | tf_op jit(solution)/shard_map/ppermute | solution.py:399
  3.9 3.2 %shard_map.28 = f32[4,280,128]{2,1,0:T(8,128)S(1)} custom-call(bf16[2,1,56,3584]{3,2,1,0:T(8,128)(2,1)} %x_hbm.3, bf16[2,1,56,3584]{3,2,1,0:T(8,128)(2,1)} %g_hbm.3), custom_call_target="tpu_custom_call" | custom-call | tf_op jit(solution)/shard_map/pallas_call | solution.py:200
  7.1 0.0 collective-permute-done
  7.1 1.3 %collective-permute-start.2 = (f32[280,128]{1,0:T(8,128)S(1)}, f32[280,128]{1,0:T(8,128)S(1)}, u32[]{:S(2)}, u32[]{:S(2)}) collective-permute-start(f32[280,128]{1,0:T(8,128)S(1)} %get-tuple-element.6), channel_id=1, source_target_pairs={{0,1},{1,0},{2,6},{3,7},{4,5},{5,4},{6,2},{7,3},{8,9},{9,8},{10,14... | collective-permute-start | bytes 430088 | tf_op jit(solution)/shard_map/ppermute | solution.py:399
  8.4 0.2 collective-permute-start.1
  8.7 2.8 %collective-permute-done.2 = f32[280,128]{1,0:T(8,128)S(1)} collective-permute-done((f32[280,128]{1,0:T(8,128)S(1)}, f32[280,128]{1,0:T(8,128)S(1)}, u32[]{:S(2)}, u32[]{:S(2)}) %collective-permute-start.2) | collective-permute-done | bytes 143392 | tf_op jit(solution)/shard_map/ppermute | solution.py:399
  11.5 1.3 %collective-permute-start.3 = (f32[280,128]{1,0:T(8,128)S(1)}, f32[280,128]{1,0:T(8,128)S(1)}, u32[]{:S(2)}, u32[]{:S(2)}) collective-permute-start(f32[280,128]{1,0:T(8,128)S(1)} %fusion.2), channel_id=1, source_target_pairs={{0,4},{1,5},{2,3},{3,2},{4,0},{5,1},{6,7},{7,6},{8,12},{9,13},{10,... | collective-permute-start | bytes 430088 | tf_op jit(solution)/shard_map/ppermute | solution.py:399
  12.8 0.2 collective-permute-done.1
  13.0 2.8 %collective-permute-done.3 = f32[280,128]{1,0:T(8,128)S(1)} collective-permute-done((f32[280,128]{1,0:T(8,128)S(1)}, f32[280,128]{1,0:T(8,128)S(1)}, u32[]{:S(2)}, u32[]{:S(2)}) %collective-permute-start.3) | collective-permute-done | bytes 143392 | tf_op jit(solution)/shard_map/ppermute | solution.py:399
  15.8 0.1 fusion.6
  15.8 0.1 collective-permute-start.4
  16.0 6.3 %collective-permute-done.4 = f32[280,128]{1,0:T(8,128)S(1)} collective-permute-done((f32[280,128]{1,0:T(8,128)S(1)}, f32[280,128]{1,0:T(8,128)S(1)}, u32[]{:S(2)}, u32[]{:S(2)}) %collective-permute-start.4) | collective-permute-done | bytes 143392 | tf_op jit(solution)/shard_map/ppermute | solution.py:399
  22.3 0.1 collective-permute-start.5
  22.4 3.9 %collective-permute-done.5 = f32[280,128]{1,0:T(8,128)S(1)} collective-permute-done((f32[280,128]{1,0:T(8,128)S(1)}, f32[280,128]{1,0:T(8,128)S(1)}, u32[]{:S(2)}, u32[]{:S(2)}) %collective-permute-start.5) | collective-permute-done | bytes 143392 | tf_op jit(solution)/shard_map/ppermute | solution.py:399
  26.3 1.3 %collective-permute-start.6 = (f32[280,128]{1,0:T(8,128)S(1)}, f32[280,128]{1,0:T(8,128)S(1)}, u32[]{:S(2)}, u32[]{:S(2)}) collective-permute-start(f32[280,128]{1,0:T(8,128)S(1)} %add.51.own_ref), channel_id=1, source_target_pairs={{0,1},{1,0},{2,3},{3,2},{4,5},{5,4},{6,7},{7,6},{8,9},{9,8},{10,11... | collective-permute-start | bytes 430088 | tf_op jit(solution)/shard_map/ppermute | solution.py:399
  27.6 1.2 %collective-permute-start.7 = (f32[280,128]{1,0:T(8,128)S(1)}, f32[280,128]{1,0:T(8,128)S(1)}, u32[]{:S(2)}, u32[]{:S(2)}) collective-permute-start(f32[280,128]{1,0:T(8,128)S(1)} %add.51.own_ref), channel_id=1, source_target_pairs={{0,4},{1,5},{2,6},{3,7},{4,0},{5,1},{6,2},{7,3},{8,12},{9,13},{10,... | collective-permute-start | bytes 430088 | tf_op jit(solution)/shard_map/ppermute | solution.py:399
  28.9 0.2 collective-permute-start.8
  29.1 1.3 %collective-permute-done.6.beside_ref = f32[280,128]{1,0:T(8,128)S(1)} collective-permute-done((f32[280,128]{1,0:T(8,128)S(1)}, f32[280,128]{1,0:T(8,128)S(1)}, u32[]{:S(2)}, u32[]{:S(2)}) %collective-permute-start.6) | collective-permute-done | bytes 143392 | tf_op jit(solution)/shard_map/ppermute | solution.py:399
  30.4 2.1 %collective-permute-done.7.below_ref = f32[280,128]{1,0:T(8,128)S(1)} collective-permute-done((f32[280,128]{1,0:T(8,128)S(1)}, f32[280,128]{1,0:T(8,128)S(1)}, u32[]{:S(2)}, u32[]{:S(2)}) %collective-permute-start.7) | collective-permute-done | bytes 143392 | tf_op jit(solution)/shard_map/ppermute | solution.py:399
  32.4 1.3 %collective-permute-done.8.across_ref = f32[280,128]{1,0:T(8,128)S(1)} collective-permute-done((f32[280,128]{1,0:T(8,128)S(1)}, f32[280,128]{1,0:T(8,128)S(1)}, u32[]{:S(2)}, u32[]{:S(2)}) %collective-permute-start.8) | collective-permute-done | bytes 143392 | tf_op jit(solution)/shard_map/ppermute | solution.py:399
  33.7 4.1 %shard_map.30 = f32[64,576]{1,0:T(8,128)S(1)} custom-call(f32[280,128]{1,0:T(8,128)S(1)} %add.51.own_ref, f32[280,128]{1,0:T(8,128)S(1)} %collective-permute-done.6.beside_ref, f32[280,128]{1,0:T(8,128)S(1)} %collective-permute-done.7.below_ref, f32[280,128]{1,0:T(8,128)S(1)} %collective-permute-done.8.across_ref), custom_call_target="tpu_custom_call" | custom-call | tf_op jit(solution)/shard_map/pallas_call | solution.py:367
  37.8 6.2 %collective-permute-start.9 = (f32[64,576]{1,0:T(8,128)S(1)}, f32[64,576]{1,0:T(8,128)S(1)}, u32[]{:S(2)}, u32[]{:S(2)}) collective-permute-start(f32[64,576]{1,0:T(8,128)S(1)} %shard_map.30), channel_id=1, source_target_pairs={{0,2},{1,3},{2,0},{3,1},{4,6},{5,7},{6,4},{7,5},{8,10},{9,11},{10,... | collective-permute-start | bytes 442376 | tf_op jit(solution)/shard_map/ppermute | solution.py:399
  44.0 1.0 %collective-permute-done.9 = f32[64,576]{1,0:T(8,128)S(1)} collective-permute-done((f32[64,576]{1,0:T(8,128)S(1)}, f32[64,576]{1,0:T(8,128)S(1)}, u32[]{:S(2)}, u32[]{:S(2)}) %collective-permute-start.9) | collective-permute-done | bytes 147488 | tf_op jit(solution)/shard_map/ppermute | solution.py:399
  45.0 0.7 %maximum_select_fusion = f32[2,64,576]{2,1,0:T(8,128)} fusion(f32[1,64,576]{2,1,0:T(8,128)S(1)} %bitcast.17, f32[1,64,576]{2,1,0:T(8,128)S(1)} %bitcast.16, pred[]{:T(512)S(6)} %eq.3), kind=kLoop, calls=%fused_computation | loop fusion | flops 221184 | bytes 589825 | tf_op jit(solution)/shard_map/jit(_where)/select_n | solution.py:415
  (4 shorter events, 0.1 us)
Async XLA Ops:
  3.2 3.9 %collective-permute-start = (f32[4,280,128]{2,1,0:T(8,128)S(1)}, f32[4,280,128]{2,1,0:T(8,128)S(1)}, u32[]{:S(2)}, u32[]{:S(2)}) collective-permute-start(f32[4,280,128]{2,1,0:T(8,128)S(1)} %shard_map.29), channel_id=1, source_target_pairs={{0,2},{1,3},{2,0},{3,1},{4,6},{5,7},{6,4},{7,5},{8,10},{9,11},{10,... | collective-permute-start | bytes 1720328 | tf_op jit(solution)/shard_map/ppermute | solution.py:399
  7.1 4.3 %collective-permute-start.2 = (f32[280,128]{1,0:T(8,128)S(1)}, f32[280,128]{1,0:T(8,128)S(1)}, u32[]{:S(2)}, u32[]{:S(2)}) collective-permute-start(f32[280,128]{1,0:T(8,128)S(1)} %get-tuple-element.6), channel_id=1, source_target_pairs={{0,1},{1,0},{2,6},{3,7},{4,5},{5,4},{6,2},{7,3},{8,9},{9,8},{10,14... | collective-permute-start | bytes 430088 | tf_op jit(solution)/shard_map/ppermute | solution.py:399
  8.4 4.5 %collective-permute-start.1 = (f32[280,128]{1,0:T(8,128)S(1)}, f32[280,128]{1,0:T(8,128)S(1)}, u32[]{:S(2)}, u32[]{:S(2)}) collective-permute-start(f32[280,128]{1,0:T(8,128)S(1)} %get-tuple-element.5), channel_id=1, source_target_pairs={{0,1},{1,0},{2,6},{3,7},{4,5},{5,4},{6,2},{7,3},{8,9},{9,8},{10,14... | collective-permute-start | bytes 430088 | tf_op jit(solution)/shard_map/ppermute | solution.py:399
  11.5 4.3 %collective-permute-start.3 = (f32[280,128]{1,0:T(8,128)S(1)}, f32[280,128]{1,0:T(8,128)S(1)}, u32[]{:S(2)}, u32[]{:S(2)}) collective-permute-start(f32[280,128]{1,0:T(8,128)S(1)} %fusion.2), channel_id=1, source_target_pairs={{0,4},{1,5},{2,3},{3,2},{4,0},{5,1},{6,7},{7,6},{8,12},{9,13},{10,... | collective-permute-start | bytes 430088 | tf_op jit(solution)/shard_map/ppermute | solution.py:399
  15.8 6.4 %collective-permute-start.4 = (f32[280,128]{1,0:T(8,128)S(1)}, f32[280,128]{1,0:T(8,128)S(1)}, u32[]{:S(2)}, u32[]{:S(2)}) collective-permute-start(f32[280,128]{1,0:T(8,128)S(1)} %fusion.6), channel_id=1, source_target_pairs={{0,8},{1,9},{2,18},{3,19},{4,12},{5,13},{6,22},{7,23},{8,0},{9,1},... | collective-permute-start | bytes 430088 | tf_op jit(solution)/shard_map/ppermute | solution.py:399
  22.3 4.0 %collective-permute-start.5 = (f32[280,128]{1,0:T(8,128)S(1)}, f32[280,128]{1,0:T(8,128)S(1)}, u32[]{:S(2)}, u32[]{:S(2)}) collective-permute-start(f32[280,128]{1,0:T(8,128)S(1)} %add.50), channel_id=1, source_target_pairs={{0,16},{1,17},{2,10},{3,11},{4,20},{5,21},{6,14},{7,15},{8,24},{9,... | collective-permute-start | bytes 430088 | tf_op jit(solution)/shard_map/ppermute | solution.py:399
  26.3 4.0 %collective-permute-start.6 = (f32[280,128]{1,0:T(8,128)S(1)}, f32[280,128]{1,0:T(8,128)S(1)}, u32[]{:S(2)}, u32[]{:S(2)}) collective-permute-start(f32[280,128]{1,0:T(8,128)S(1)} %add.51.own_ref), channel_id=1, source_target_pairs={{0,1},{1,0},{2,3},{3,2},{4,5},{5,4},{6,7},{7,6},{8,9},{9,8},{10,11... | collective-permute-start | bytes 430088 | tf_op jit(solution)/shard_map/ppermute | solution.py:399
  27.6 4.8 %collective-permute-start.7 = (f32[280,128]{1,0:T(8,128)S(1)}, f32[280,128]{1,0:T(8,128)S(1)}, u32[]{:S(2)}, u32[]{:S(2)}) collective-permute-start(f32[280,128]{1,0:T(8,128)S(1)} %add.51.own_ref), channel_id=1, source_target_pairs={{0,4},{1,5},{2,6},{3,7},{4,0},{5,1},{6,2},{7,3},{8,12},{9,13},{10,... | collective-permute-start | bytes 430088 | tf_op jit(solution)/shard_map/ppermute | solution.py:399
  28.9 4.8 %collective-permute-start.8 = (f32[280,128]{1,0:T(8,128)S(1)}, f32[280,128]{1,0:T(8,128)S(1)}, u32[]{:S(2)}, u32[]{:S(2)}) collective-permute-start(f32[280,128]{1,0:T(8,128)S(1)} %add.51.own_ref), channel_id=1, source_target_pairs={{0,5},{1,4},{2,7},{3,6},{4,1},{5,0},{6,3},{7,2},{8,13},{9,12},{10,... | collective-permute-start | bytes 430088 | tf_op jit(solution)/shard_map/ppermute | solution.py:399
  37.8 7.2 %collective-permute-start.9 = (f32[64,576]{1,0:T(8,128)S(1)}, f32[64,576]{1,0:T(8,128)S(1)}, u32[]{:S(2)}, u32[]{:S(2)}) collective-permute-start(f32[64,576]{1,0:T(8,128)S(1)} %shard_map.30), channel_id=1, source_target_pairs={{0,2},{1,3},{2,0},{3,1},{4,6},{5,7},{6,4},{7,5},{8,10},{9,11},{10,... | collective-permute-start | bytes 442376 | tf_op jit(solution)/shard_map/ppermute | solution.py:399

commit v5 on v4

--- a/solution.py
+++ b/solution.py
@@ -14,7 +14,7 @@
 ROW = 64
 QUART = 4
 DAMP = 0.1
-SUMS_VMEM = 53 * 2**20
+SUMS_VMEM = 52 * 2**20
 VMEM_LIMIT = 48 * 2**20
 F32 = jnp.float32
 BF16 = jnp.bfloat16
@@ -56,15 +56,24 @@
     return 2 * (second ^ (quarter % 2)) + (first ^ (quarter // 2))
 
 
-def local_kernel(height, width, own, x_hbm, g_hbm, out_ref, xbuf, gbuf, shifted, lhs_t, edges, sems):
+def local_kernel(height, width, own, *refs):
+    if own:
+        xbuf, gbuf, out_ref, shifted, lhs_t, edges = refs
+    else:
+        x_hbm, g_hbm, out_ref, next_x, next_g, xbuf, gbuf, shifted, lhs_t, edges, sems = refs
     core, first, second = chip_place()
     wp = width // 2
     rows = wp * ROW
     layer = core if own else 1 - core
-    copy_x = pltpu.make_async_copy(x_hbm.at[layer, 0], xbuf, sems.at[0])
-    copy_g = pltpu.make_async_copy(g_hbm.at[layer, 0], gbuf, sems.at[1])
-    copy_x.start()
-    copy_g.start()
+    if not own:
+        copies = [
+            pltpu.make_async_copy(x_hbm.at[layer, 0], xbuf, sems.at[0]),
+            pltpu.make_async_copy(g_hbm.at[layer, 0], gbuf, sems.at[1]),
+            pltpu.make_async_copy(x_hbm.at[core, 0], next_x, sems.at[2]),
+            pltpu.make_async_copy(g_hbm.at[core, 0], next_g, sems.at[3]),
+        ]
+        for one in copies:
+            one.start()
     for d in range(4):
         shifted[d, 0:ROW, :] = jnp.zeros((ROW, PAIR), BF16)
         shifted[d, ROW + rows : 2 * ROW + rows, :] = jnp.zeros((ROW, PAIR), BF16)
@@ -72,8 +81,9 @@
     low = lax.broadcasted_iota(jnp.int32, (ROW, PAIR), 1) < C
     pad = jnp.zeros((ROW - height, PAIR), F32)
     n_edge = edges.shape[1] - 16
-    copy_x.wait()
-    copy_g.wait()
+    if not own:
+        copies[0].wait()
+        copies[1].wait()
     for pair in range(wp // 2):
         tiles_x = []
         tiles_g = []
@@ -189,29 +199,32 @@
         slot = slot_of(quarter, layer, first, second)
         out_ref[slot, LAST:DIAGS, :] = rx[quarter * PIECE : (quarter + 1) * PIECE, :]
         out_ref[slot, DIAGS:QROWS, :] = diags
-
-
-def local_sums(feature_maps, output_grads, own):
-    height = feature_maps.shape[2]
-    width = feature_maps.shape[3] // C
+    if not own:
+        copies[2].wait()
+        copies[3].wait()
+
+
+def local_sums(height, width, own, x, g):
     wp = width // 2
-    shape = jax.ShapeDtypeStruct((4, QROWS, PAIR), F32)
+    sums = jax.ShapeDtypeStruct((4, QROWS, PAIR), F32)
+    image = jax.ShapeDtypeStruct((height, width * C), BF16)
     n_edge = (wp + 15) // 16 * 16
+    vmem = pl.BlockSpec(memory_space=pltpu.VMEM)
+    scratch = [
+        pltpu.VMEM((4, (wp + 2) * ROW, PAIR), BF16),
+        pltpu.VMEM((2 * PAIR, wp * ROW), BF16),
+        pltpu.VMEM((2, n_edge + 16, PAIR), F32),
+    ]
+    if not own:
+        scratch = [pltpu.VMEM(image.shape, BF16)] * 2 + scratch + [pltpu.SemaphoreType.DMA((4,))]
     return pl.pallas_call(
         functools.partial(local_kernel, height, width, own),
-        out_shape=shape,
-        in_specs=[pl.BlockSpec(memory_space=pltpu.HBM)] * 2,
-        out_specs=pl.BlockSpec(memory_space=pltpu.VMEM),
-        scratch_shapes=[
-            pltpu.VMEM((height, width * C), BF16),
-            pltpu.VMEM((height, width * C), BF16),
-            pltpu.VMEM((4, (wp + 2) * ROW, PAIR), BF16),
-            pltpu.VMEM((2 * PAIR, wp * ROW), BF16),
-            pltpu.VMEM((2, n_edge + 16, PAIR), F32),
-            pltpu.SemaphoreType.DMA((2,)),
-        ],
+        out_shape=sums if own else (sums, image, image),
+        in_specs=[vmem if own else pl.BlockSpec(memory_space=pltpu.HBM)] * 2,
+        out_specs=vmem if own else (vmem,) * 3,
+        scratch_shapes=scratch,
         compiler_params=pltpu.CompilerParams(vmem_limit_bytes=SUMS_VMEM),
-    )(feature_maps, output_grads)
+    )(x, g)
 
 
 def split(a):
@@ -398,8 +411,11 @@
     cores, halvings, doublings, gathers = pairings(n_dp, n_grp)
     swap = lambda a, p: lax.ppermute(a, ("dp", "grp"), p)
     total_rows = feature_maps.shape[2] * feature_maps.shape[3] // C * feature_maps.shape[1] * n_dp * n_grp
-    got = swap(local_sums(feature_maps, output_grads, False), cores)
-    keep = local_sums(feature_maps, output_grads, True)
+    height = feature_maps.shape[2]
+    width = feature_maps.shape[3] // C
+    send, own_x, own_g = local_sums(height, width, False, feature_maps, output_grads)
+    got = swap(send, cores)
+    keep = local_sums(height, width, True, own_x, own_g)
     far_next = swap(keep[3] + got[3], halvings[0])
     far_own = swap(keep[2] + got[2], halvings[0])
     got_next = swap(keep[1] + got[1] + far_next, halvings[1])

time: 45.9 us -> 44.8 us (0.976)
  Pallas kernels: 10.4 us -> 9.26 us
    pallas_call x2, Pallas kernels: 6.32 us -> 5.19 us  [local_sums(): pl.pallas_call(functools.partial(local_kernel, height, width, own), out_s...]
  transfers between devices with their start and end apart: 10 -> 10, of which waited for: 9 -> 9; matrix products, arithmetic and copies ran while one was open for 0% -> 0% of each run, Pallas kernels for 7% -> 5%
where the time goes in v5:
time: 44.8 us; the launch traced here: 44.6 us
  waiting for transfers between devices  21.7 us (48%)
  starting transfers between devices  12.7 us (28%)
  Pallas kernels  9.26 us (21%)
  other arithmetic  0.91 us (2%)
    ppermute x10, waiting for transfers between devices, shards(): swap = lambda a, p: lax.ppermute(a, ('dp', 'grp'), p)  21.7 us
    ppermute x10, starting transfers between devices, shards(): swap = lambda a, p: lax.ppermute(a, ('dp', 'grp'), p)  12.7 us
    pallas_call x2, Pallas kernels, local_sums(): pl.pallas_call(functools.partial(local_kernel, height, width, own), out_s...  5.19 us
    pallas_call x1, Pallas kernels, precondition(): pl.pallas_call(functools.partial(final_kernel, float(total_rows)), out_sh...  4.07 us
  transfers between devices with their start and end apart: 10, of which 9 were waited for; matrix products, arithmetic and copies ran while one was open for 0% of the time, Pallas kernels for 5%

profile of v5, /device:TPU:25, one launch (start us, length us, event | category | flops | bytes accessed | tf_op | source)
XLA Modules:
  0.0 44.6 jit_solution(14700700170794361305)
XLA Ops:
  0.0 3.2 %shard_map.28 = (f32[4,280,128]{2,1,0:T(8,128)S(1)}, bf16[56,3584]{1,0:T(8,128)(2,1)S(1)}, bf16[56,3584]{1,0:T(8,128)(2,1)S(1)}) custom-call(bf16[2,1,56,3584]{3,2,1,0:T(8,128)(2,1)} %refs_0_.1, bf16[2,1,56,3584]{3,2,1,0:T(8,128)(2,1)} %refs_1_.1), custom_call_target="tpu_custom_call" | custom-call | tf_op jit(solution)/shard_map/pallas_call | solution.py:220
  3.2 0.7 %collective-permute-start = (f32[4,280,128]{2,1,0:T(8,128)S(1)}, f32[4,280,128]{2,1,0:T(8,128)S(1)}, u32[]{:S(2)}, u32[]{:S(2)}) collective-permute-start(f32[4,280,128]{2,1,0:T(8,128)S(1)} %get-tuple-element.10), channel_id=1, source_target_pairs={{0,2},{1,3},{2,0},{3,1},{4,6},{5,7},{6,4},{7,5},{8,10},{9,11},{10,... | collective-permute-start | bytes 1720328 | tf_op jit(solution)/shard_map/ppermute | solution.py:412
  3.9 2.0 %shard_map.29 = f32[4,280,128]{2,1,0:T(8,128)S(1)} custom-call(bf16[56,3584]{1,0:T(8,128)(2,1)S(1)} %get-tuple-element.8.refs_0_, bf16[56,3584]{1,0:T(8,128)(2,1)S(1)} %get-tuple-element.9.refs_1_), custom_call_target="tpu_custom_call" | custom-call | tf_op jit(solution)/shard_map/pallas_call | solution.py:220
  6.0 0.0 collective-permute-done
  6.0 1.3 %collective-permute-start.2 = (f32[280,128]{1,0:T(8,128)S(1)}, f32[280,128]{1,0:T(8,128)S(1)}, u32[]{:S(2)}, u32[]{:S(2)}) collective-permute-start(f32[280,128]{1,0:T(8,128)S(1)} %get-tuple-element.12), channel_id=1, source_target_pairs={{0,1},{1,0},{2,6},{3,7},{4,5},{5,4},{6,2},{7,3},{8,9},{9,8},{10,14... | collective-permute-start | bytes 430088 | tf_op jit(solution)/shard_map/ppermute | solution.py:412
  7.3 0.2 collective-permute-start.1
  7.5 2.8 %collective-permute-done.2 = f32[280,128]{1,0:T(8,128)S(1)} collective-permute-done((f32[280,128]{1,0:T(8,128)S(1)}, f32[280,128]{1,0:T(8,128)S(1)}, u32[]{:S(2)}, u32[]{:S(2)}) %collective-permute-start.2) | collective-permute-done | bytes 143392 | tf_op jit(solution)/shard_map/ppermute | solution.py:412
  10.3 1.3 %collective-permute-start.3 = (f32[280,128]{1,0:T(8,128)S(1)}, f32[280,128]{1,0:T(8,128)S(1)}, u32[]{:S(2)}, u32[]{:S(2)}) collective-permute-start(f32[280,128]{1,0:T(8,128)S(1)} %fusion.2), channel_id=1, source_target_pairs={{0,4},{1,5},{2,3},{3,2},{4,0},{5,1},{6,7},{7,6},{8,12},{9,13},{10,... | collective-permute-start | bytes 430088 | tf_op jit(solution)/shard_map/ppermute | solution.py:412
  11.6 0.2 collective-permute-done.1
  11.8 2.8 %collective-permute-done.3 = f32[280,128]{1,0:T(8,128)S(1)} collective-permute-done((f32[280,128]{1,0:T(8,128)S(1)}, f32[280,128]{1,0:T(8,128)S(1)}, u32[]{:S(2)}, u32[]{:S(2)}) %collective-permute-start.3) | collective-permute-done | bytes 143392 | tf_op jit(solution)/shard_map/ppermute | solution.py:412
  14.7 0.1 fusion.6
  14.7 0.1 collective-permute-start.4
  14.8 6.3 %collective-permute-done.4 = f32[280,128]{1,0:T(8,128)S(1)} collective-permute-done((f32[280,128]{1,0:T(8,128)S(1)}, f32[280,128]{1,0:T(8,128)S(1)}, u32[]{:S(2)}, u32[]{:S(2)}) %collective-permute-start.4) | collective-permute-done | bytes 143392 | tf_op jit(solution)/shard_map/ppermute | solution.py:412
  21.2 0.1 collective-permute-start.5
  21.3 3.9 %collective-permute-done.5 = f32[280,128]{1,0:T(8,128)S(1)} collective-permute-done((f32[280,128]{1,0:T(8,128)S(1)}, f32[280,128]{1,0:T(8,128)S(1)}, u32[]{:S(2)}, u32[]{:S(2)}) %collective-permute-start.5) | collective-permute-done | bytes 143392 | tf_op jit(solution)/shard_map/ppermute | solution.py:412
  25.2 1.3 %collective-permute-start.6 = (f32[280,128]{1,0:T(8,128)S(1)}, f32[280,128]{1,0:T(8,128)S(1)}, u32[]{:S(2)}, u32[]{:S(2)}) collective-permute-start(f32[280,128]{1,0:T(8,128)S(1)} %add.51.own_ref), channel_id=1, source_target_pairs={{0,1},{1,0},{2,3},{3,2},{4,5},{5,4},{6,7},{7,6},{8,9},{9,8},{10,11... | collective-permute-start | bytes 430088 | tf_op jit(solution)/shard_map/ppermute | solution.py:412
  26.5 1.2 %collective-permute-start.7 = (f32[280,128]{1,0:T(8,128)S(1)}, f32[280,128]{1,0:T(8,128)S(1)}, u32[]{:S(2)}, u32[]{:S(2)}) collective-permute-start(f32[280,128]{1,0:T(8,128)S(1)} %add.51.own_ref), channel_id=1, source_target_pairs={{0,4},{1,5},{2,6},{3,7},{4,0},{5,1},{6,2},{7,3},{8,12},{9,13},{10,... | collective-permute-start | bytes 430088 | tf_op jit(solution)/shard_map/ppermute | solution.py:412
  27.7 0.2 collective-permute-start.8
  27.9 1.3 %collective-permute-done.6.beside_ref = f32[280,128]{1,0:T(8,128)S(1)} collective-permute-done((f32[280,128]{1,0:T(8,128)S(1)}, f32[280,128]{1,0:T(8,128)S(1)}, u32[]{:S(2)}, u32[]{:S(2)}) %collective-permute-start.6) | collective-permute-done | bytes 143392 | tf_op jit(solution)/shard_map/ppermute | solution.py:412
  29.2 2.1 %collective-permute-done.7.below_ref = f32[280,128]{1,0:T(8,128)S(1)} collective-permute-done((f32[280,128]{1,0:T(8,128)S(1)}, f32[280,128]{1,0:T(8,128)S(1)}, u32[]{:S(2)}, u32[]{:S(2)}) %collective-permute-start.7) | collective-permute-done | bytes 143392 | tf_op jit(solution)/shard_map/ppermute | solution.py:412
  31.3 1.3 %collective-permute-done.8.across_ref = f32[280,128]{1,0:T(8,128)S(1)} collective-permute-done((f32[280,128]{1,0:T(8,128)S(1)}, f32[280,128]{1,0:T(8,128)S(1)}, u32[]{:S(2)}, u32[]{:S(2)}) %collective-permute-start.8) | collective-permute-done | bytes 143392 | tf_op jit(solution)/shard_map/ppermute | solution.py:412
  32.6 4.1 %shard_map.30 = f32[64,576]{1,0:T(8,128)S(1)} custom-call(f32[280,128]{1,0:T(8,128)S(1)} %add.51.own_ref, f32[280,128]{1,0:T(8,128)S(1)} %collective-permute-done.6.beside_ref, f32[280,128]{1,0:T(8,128)S(1)} %collective-permute-done.7.below_ref, f32[280,128]{1,0:T(8,128)S(1)} %collective-permute-done.8.across_ref), custom_call_target="tpu_custom_call" | custom-call | tf_op jit(solution)/shard_map/pallas_call | solution.py:380
  36.6 6.2 %collective-permute-start.9 = (f32[64,576]{1,0:T(8,128)S(1)}, f32[64,576]{1,0:T(8,128)S(1)}, u32[]{:S(2)}, u32[]{:S(2)}) collective-permute-start(f32[64,576]{1,0:T(8,128)S(1)} %shard_map.30), channel_id=1, source_target_pairs={{0,2},{1,3},{2,0},{3,1},{4,6},{5,7},{6,4},{7,5},{8,10},{9,11},{10,... | collective-permute-start | bytes 442376 | tf_op jit(solution)/shard_map/ppermute | solution.py:412
  42.9 1.0 %collective-permute-done.9 = f32[64,576]{1,0:T(8,128)S(1)} collective-permute-done((f32[64,576]{1,0:T(8,128)S(1)}, f32[64,576]{1,0:T(8,128)S(1)}, u32[]{:S(2)}, u32[]{:S(2)}) %collective-permute-start.9) | collective-permute-done | bytes 147488 | tf_op jit(solution)/shard_map/ppermute | solution.py:412
  43.9 0.7 %maximum_select_fusion = f32[2,64,576]{2,1,0:T(8,128)} fusion(f32[1,64,576]{2,1,0:T(8,128)S(1)} %bitcast.17, f32[1,64,576]{2,1,0:T(8,128)S(1)} %bitcast.16, pred[]{:T(512)S(6)} %eq.3), kind=kLoop, calls=%fused_computation | loop fusion | flops 221184 | bytes 589825 | tf_op jit(solution)/shard_map/jit(_where)/select_n | solution.py:431
  (4 shorter events, 0.1 us)
Async XLA Ops:
  3.2 2.8 %collective-permute-start = (f32[4,280,128]{2,1,0:T(8,128)S(1)}, f32[4,280,128]{2,1,0:T(8,128)S(1)}, u32[]{:S(2)}, u32[]{:S(2)}) collective-permute-start(f32[4,280,128]{2,1,0:T(8,128)S(1)} %get-tuple-element.10), channel_id=1, source_target_pairs={{0,2},{1,3},{2,0},{3,1},{4,6},{5,7},{6,4},{7,5},{8,10},{9,11},{10,... | collective-permute-start | bytes 1720328 | tf_op jit(solution)/shard_map/ppermute | solution.py:412
  6.0 4.3 %collective-permute-start.2 = (f32[280,128]{1,0:T(8,128)S(1)}, f32[280,128]{1,0:T(8,128)S(1)}, u32[]{:S(2)}, u32[]{:S(2)}) collective-permute-start(f32[280,128]{1,0:T(8,128)S(1)} %get-tuple-element.12), channel_id=1, source_target_pairs={{0,1},{1,0},{2,6},{3,7},{4,5},{5,4},{6,2},{7,3},{8,9},{9,8},{10,14... | collective-permute-start | bytes 430088 | tf_op jit(solution)/shard_map/ppermute | solution.py:412
  7.3 4.5 %collective-permute-start.1 = (f32[280,128]{1,0:T(8,128)S(1)}, f32[280,128]{1,0:T(8,128)S(1)}, u32[]{:S(2)}, u32[]{:S(2)}) collective-permute-start(f32[280,128]{1,0:T(8,128)S(1)} %get-tuple-element.11), channel_id=1, source_target_pairs={{0,1},{1,0},{2,6},{3,7},{4,5},{5,4},{6,2},{7,3},{8,9},{9,8},{10,14... | collective-permute-start | bytes 430088 | tf_op jit(solution)/shard_map/ppermute | solution.py:412
  10.3 4.3 %collective-permute-start.3 = (f32[280,128]{1,0:T(8,128)S(1)}, f32[280,128]{1,0:T(8,128)S(1)}, u32[]{:S(2)}, u32[]{:S(2)}) collective-permute-start(f32[280,128]{1,0:T(8,128)S(1)} %fusion.2), channel_id=1, source_target_pairs={{0,4},{1,5},{2,3},{3,2},{4,0},{5,1},{6,7},{7,6},{8,12},{9,13},{10,... | collective-permute-start | bytes 430088 | tf_op jit(solution)/shard_map/ppermute | solution.py:412
  14.7 6.4 %collective-permute-start.4 = (f32[280,128]{1,0:T(8,128)S(1)}, f32[280,128]{1,0:T(8,128)S(1)}, u32[]{:S(2)}, u32[]{:S(2)}) collective-permute-start(f32[280,128]{1,0:T(8,128)S(1)} %fusion.6), channel_id=1, source_target_pairs={{0,8},{1,9},{2,18},{3,19},{4,12},{5,13},{6,22},{7,23},{8,0},{9,1},... | collective-permute-start | bytes 430088 | tf_op jit(solution)/shard_map/ppermute | solution.py:412
  21.2 4.0 %collective-permute-start.5 = (f32[280,128]{1,0:T(8,128)S(1)}, f32[280,128]{1,0:T(8,128)S(1)}, u32[]{:S(2)}, u32[]{:S(2)}) collective-permute-start(f32[280,128]{1,0:T(8,128)S(1)} %add.50), channel_id=1, source_target_pairs={{0,16},{1,17},{2,10},{3,11},{4,20},{5,21},{6,14},{7,15},{8,24},{9,... | collective-permute-start | bytes 430088 | tf_op jit(solution)/shard_map/ppermute | solution.py:412
  25.2 4.0 %collective-permute-start.6 = (f32[280,128]{1,0:T(8,128)S(1)}, f32[280,128]{1,0:T(8,128)S(1)}, u32[]{:S(2)}, u32[]{:S(2)}) collective-permute-start(f32[280,128]{1,0:T(8,128)S(1)} %add.51.own_ref), channel_id=1, source_target_pairs={{0,1},{1,0},{2,3},{3,2},{4,5},{5,4},{6,7},{7,6},{8,9},{9,8},{10,11... | collective-permute-start | bytes 430088 | tf_op jit(solution)/shard_map/ppermute | solution.py:412
  26.5 4.8 %collective-permute-start.7 = (f32[280,128]{1,0:T(8,128)S(1)}, f32[280,128]{1,0:T(8,128)S(1)}, u32[]{:S(2)}, u32[]{:S(2)}) collective-permute-start(f32[280,128]{1,0:T(8,128)S(1)} %add.51.own_ref), channel_id=1, source_target_pairs={{0,4},{1,5},{2,6},{3,7},{4,0},{5,1},{6,2},{7,3},{8,12},{9,13},{10,... | collective-permute-start | bytes 430088 | tf_op jit(solution)/shard_map/ppermute | solution.py:412
  27.7 4.8 %collective-permute-start.8 = (f32[280,128]{1,0:T(8,128)S(1)}, f32[280,128]{1,0:T(8,128)S(1)}, u32[]{:S(2)}, u32[]{:S(2)}) collective-permute-start(f32[280,128]{1,0:T(8,128)S(1)} %add.51.own_ref), channel_id=1, source_target_pairs={{0,5},{1,4},{2,7},{3,6},{4,1},{5,0},{6,3},{7,2},{8,13},{9,12},{10,... | collective-permute-start | bytes 430088 | tf_op jit(solution)/shard_map/ppermute | solution.py:412
  36.6 7.2 %collective-permute-start.9 = (f32[64,576]{1,0:T(8,128)S(1)}, f32[64,576]{1,0:T(8,128)S(1)}, u32[]{:S(2)}, u32[]{:S(2)}) collective-permute-start(f32[64,576]{1,0:T(8,128)S(1)} %shard_map.30), channel_id=1, source_target_pairs={{0,2},{1,3},{2,0},{3,1},{4,6},{5,7},{6,4},{7,5},{8,10},{9,11},{10,... | collective-permute-start | bytes 442376 | tf_op jit(solution)/shard_map/ppermute | solution.py:412

commit v6 on v5

--- a/solution.py
+++ b/solution.py
@@ -103,12 +103,11 @@
         lhs_t[0:PAIR, lanes] = jnp.concatenate(tiles_x, axis=0).T.astype(BF16)
         lhs_t[PAIR : 2 * PAIR, lanes] = jnp.concatenate(tiles_g, axis=0).T.astype(BF16)
 
-    def product(d, s, part):
+    def product(wanted, part):
         left = lhs_t[...] if part is None else lhs_t[part * PAIR : (part + 1) * PAIR, :]
-        right = [shifted[d, (1 + one) * ROW : (1 + one) * ROW + rows, :] for one in s]
-        right = right[0] if len(right) == 1 else jnp.concatenate(right, axis=1)
-        full = jnp.dot(left, right, preferred_element_type=F32)
-        return [full[:, k * PAIR : (k + 1) * PAIR] for k in range(len(s))]
+        right = [shifted[d, (1 + s) * ROW : (1 + s) * ROW + rows, :] for d, s in wanted]
+        full = jnp.dot(left, right[0] if len(right) == 1 else jnp.concatenate(right, axis=1), preferred_element_type=F32)
+        return [full[:, k * PAIR : (k + 1) * PAIR] for k in range(len(right))]
 
     def table(at_s, base, s):
         upper = at_s[s][base : base + C, :]
@@ -132,24 +131,25 @@
     pack = lambda a, b: jnp.where(row >= col, a, b)
     diagonal = lambda a: jnp.sum(jnp.where(row == col, a, 0.0), axis=0, keepdims=True)
 
-    p = product(0, (-1, 0), 1) + product(0, (1,), 1)
+    p = product(((0, -1), (0, 0)), 1) + product(((0, 1),), 1)
     at_s = dict(zip((-1, 0, 1), p))
     store("w0z", table(at_s, 0, 0))
     w0 = odd(at_s, 0, -1)
-    p = product(1, (-1, 0), None) + product(1, (1,), None)
-    at_s = dict(zip((-1, 0, 1), p))
+    same, under = product(((1, 1), (2, 1)), None)
+    p = product(((1, -1), (1, 0)), None)
+    at_s = dict(zip((-1, 0, 1), p + [same]))
     x0z = table(at_s, 0, 0)
     store("h0", jnp.where(low, table(at_s, 0, 1), w0))
     store("w1z", table(at_s, PAIR, 0))
     w1 = odd(at_s, PAIR, -1)
-    p = product(2, (-1, 0), None) + product(2, (1,), None)
-    at_s = dict(zip((-1, 0, 1), p))
+    p = product(((2, -1), (2, 0)), None)
+    at_s = dict(zip((-1, 0, 1), p + [under]))
     store("x1m", table(at_s, 0, -1))
     store("x1z", table(at_s, 0, 0))
     x12 = table(at_s, 0, 1)
     store("w2z", table(at_s, PAIR, 0))
     w2 = odd(at_s, PAIR, -1)
-    p = product(3, (-1, 0), 0) + product(3, (1,), 0)
+    p = product(((3, -1), (3, 0)), 0) + product(((3, 1),), 0)
     at_s = dict(zip((-1, 0, 1), p))
     store("x2m", table(at_s, 0, -1))
     store("x2z", table(at_s, 0, 0))

time: 44.8 us -> 44.5 us (level)
  Pallas kernels: 9.26 us -> 8.79 us
    pallas_call x2, Pallas kernels: 5.19 us -> 4.72 us  [local_sums(): pl.pallas_call(functools.partial(local_kernel, height, width, own), out_s...]
  transfers between devices with their start and end apart: 10 -> 10, of which waited for: 9 -> 9; matrix products, arithmetic and copies ran while one was open for 0% -> 0% of each run, Pallas kernels for 5% -> 4%
where the time goes in v6:
time: 44.5 us; the launch traced here: 44.3 us
  waiting for transfers between devices  21.7 us (49%)
  starting transfers between devices  12.8 us (29%)
  Pallas kernels  8.79 us (20%)
  other arithmetic  0.91 us (2%)
    ppermute x10, waiting for transfers between devices, shards(): swap = lambda a, p: lax.ppermute(a, ('dp', 'grp'), p)  21.7 us
    ppermute x10, starting transfers between devices, shards(): swap = lambda a, p: lax.ppermute(a, ('dp', 'grp'), p)  12.8 us
    pallas_call x2, Pallas kernels, local_sums(): pl.pallas_call(functools.partial(local_kernel, height, width, own), out_s...  4.72 us
    pallas_call x1, Pallas kernels, precondition(): pl.pallas_call(functools.partial(final_kernel, float(total_rows)), out_sh...  4.07 us
  transfers between devices with their start and end apart: 10, of which 9 were waited for; matrix products, arithmetic and copies ran while one was open for 0% of the time, Pallas kernels for 4%

profile of v6, /device:TPU:25, one launch (start us, length us, event | category | flops | bytes accessed | tf_op | source)
XLA Modules:
  0.0 44.3 jit_solution(4918007303731837795)
XLA Ops:
  0.0 2.9 %shard_map.28 = (f32[4,280,128]{2,1,0:T(8,128)S(1)}, bf16[56,3584]{1,0:T(8,128)(2,1)S(1)}, bf16[56,3584]{1,0:T(8,128)(2,1)S(1)}) custom-call(bf16[2,1,56,3584]{3,2,1,0:T(8,128)(2,1)} %refs_0_.1, bf16[2,1,56,3584]{3,2,1,0:T(8,128)(2,1)} %refs_1_.1), custom_call_target="tpu_custom_call" | custom-call | tf_op jit(solution)/shard_map/pallas_call | solution.py:220
  2.9 0.7 %collective-permute-start = (f32[4,280,128]{2,1,0:T(8,128)S(1)}, f32[4,280,128]{2,1,0:T(8,128)S(1)}, u32[]{:S(2)}, u32[]{:S(2)}) collective-permute-start(f32[4,280,128]{2,1,0:T(8,128)S(1)} %get-tuple-element.10), channel_id=1, source_target_pairs={{0,2},{1,3},{2,0},{3,1},{4,6},{5,7},{6,4},{7,5},{8,10},{9,11},{10,... | collective-permute-start | bytes 1720328 | tf_op jit(solution)/shard_map/ppermute | solution.py:412
  3.7 1.8 %shard_map.29 = f32[4,280,128]{2,1,0:T(8,128)S(1)} custom-call(bf16[56,3584]{1,0:T(8,128)(2,1)S(1)} %get-tuple-element.8.refs_0_, bf16[56,3584]{1,0:T(8,128)(2,1)S(1)} %get-tuple-element.9.refs_1_), custom_call_target="tpu_custom_call" | custom-call | tf_op jit(solution)/shard_map/pallas_call | solution.py:220
  5.5 0.0 collective-permute-done
  5.5 1.3 %collective-permute-start.2 = (f32[280,128]{1,0:T(8,128)S(1)}, f32[280,128]{1,0:T(8,128)S(1)}, u32[]{:S(2)}, u32[]{:S(2)}) collective-permute-start(f32[280,128]{1,0:T(8,128)S(1)} %get-tuple-element.12), channel_id=1, source_target_pairs={{0,1},{1,0},{2,6},{3,7},{4,5},{5,4},{6,2},{7,3},{8,9},{9,8},{10,14... | collective-permute-start | bytes 430088 | tf_op jit(solution)/shard_map/ppermute | solution.py:412
  6.8 0.2 collective-permute-start.1
  7.1 2.8 %collective-permute-done.2 = f32[280,128]{1,0:T(8,128)S(1)} collective-permute-done((f32[280,128]{1,0:T(8,128)S(1)}, f32[280,128]{1,0:T(8,128)S(1)}, u32[]{:S(2)}, u32[]{:S(2)}) %collective-permute-start.2) | collective-permute-done | bytes 143392 | tf_op jit(solution)/shard_map/ppermute | solution.py:412
  9.9 1.3 %collective-permute-start.3 = (f32[280,128]{1,0:T(8,128)S(1)}, f32[280,128]{1,0:T(8,128)S(1)}, u32[]{:S(2)}, u32[]{:S(2)}) collective-permute-start(f32[280,128]{1,0:T(8,128)S(1)} %fusion.2), channel_id=1, source_target_pairs={{0,4},{1,5},{2,3},{3,2},{4,0},{5,1},{6,7},{7,6},{8,12},{9,13},{10,... | collective-permute-start | bytes 430088 | tf_op jit(solution)/shard_map/ppermute | solution.py:412
  11.1 0.2 collective-permute-done.1
  11.4 2.8 %collective-permute-done.3 = f32[280,128]{1,0:T(8,128)S(1)} collective-permute-done((f32[280,128]{1,0:T(8,128)S(1)}, f32[280,128]{1,0:T(8,128)S(1)}, u32[]{:S(2)}, u32[]{:S(2)}) %collective-permute-start.3) | collective-permute-done | bytes 143392 | tf_op jit(solution)/shard_map/ppermute | solution.py:412
  14.2 0.1 fusion.6
  14.2 0.1 collective-permute-start.4
  14.4 6.3 %collective-permute-done.4 = f32[280,128]{1,0:T(8,128)S(1)} collective-permute-done((f32[280,128]{1,0:T(8,128)S(1)}, f32[280,128]{1,0:T(8,128)S(1)}, u32[]{:S(2)}, u32[]{:S(2)}) %collective-permute-start.4) | collective-permute-done | bytes 143392 | tf_op jit(solution)/shard_map/ppermute | solution.py:412
  20.7 0.1 collective-permute-start.5
  20.8 3.9 %collective-permute-done.5 = f32[280,128]{1,0:T(8,128)S(1)} collective-permute-done((f32[280,128]{1,0:T(8,128)S(1)}, f32[280,128]{1,0:T(8,128)S(1)}, u32[]{:S(2)}, u32[]{:S(2)}) %collective-permute-start.5) | collective-permute-done | bytes 143392 | tf_op jit(solution)/shard_map/ppermute | solution.py:412
  24.7 1.3 %collective-permute-start.6 = (f32[280,128]{1,0:T(8,128)S(1)}, f32[280,128]{1,0:T(8,128)S(1)}, u32[]{:S(2)}, u32[]{:S(2)}) collective-permute-start(f32[280,128]{1,0:T(8,128)S(1)} %add.51.own_ref), channel_id=1, source_target_pairs={{0,1},{1,0},{2,3},{3,2},{4,5},{5,4},{6,7},{7,6},{8,9},{9,8},{10,11... | collective-permute-start | bytes 430088 | tf_op jit(solution)/shard_map/ppermute | solution.py:412
  26.0 1.2 %collective-permute-start.7 = (f32[280,128]{1,0:T(8,128)S(1)}, f32[280,128]{1,0:T(8,128)S(1)}, u32[]{:S(2)}, u32[]{:S(2)}) collective-permute-start(f32[280,128]{1,0:T(8,128)S(1)} %add.51.own_ref), channel_id=1, source_target_pairs={{0,4},{1,5},{2,6},{3,7},{4,0},{5,1},{6,2},{7,3},{8,12},{9,13},{10,... | collective-permute-start | bytes 430088 | tf_op jit(solution)/shard_map/ppermute | solution.py:412
  27.3 0.2 collective-permute-start.8
  27.4 1.5 %collective-permute-done.6.beside_ref = f32[280,128]{1,0:T(8,128)S(1)} collective-permute-done((f32[280,128]{1,0:T(8,128)S(1)}, f32[280,128]{1,0:T(8,128)S(1)}, u32[]{:S(2)}, u32[]{:S(2)}) %collective-permute-start.6) | collective-permute-done | bytes 143392 | tf_op jit(solution)/shard_map/ppermute | solution.py:412
  28.9 1.9 %collective-permute-done.7.below_ref = f32[280,128]{1,0:T(8,128)S(1)} collective-permute-done((f32[280,128]{1,0:T(8,128)S(1)}, f32[280,128]{1,0:T(8,128)S(1)}, u32[]{:S(2)}, u32[]{:S(2)}) %collective-permute-start.7) | collective-permute-done | bytes 143392 | tf_op jit(solution)/shard_map/ppermute | solution.py:412
  30.8 1.3 %collective-permute-done.8.across_ref = f32[280,128]{1,0:T(8,128)S(1)} collective-permute-done((f32[280,128]{1,0:T(8,128)S(1)}, f32[280,128]{1,0:T(8,128)S(1)}, u32[]{:S(2)}, u32[]{:S(2)}) %collective-permute-start.8) | collective-permute-done | bytes 143392 | tf_op jit(solution)/shard_map/ppermute | solution.py:412
  32.1 4.1 %shard_map.30 = f32[64,576]{1,0:T(8,128)S(1)} custom-call(f32[280,128]{1,0:T(8,128)S(1)} %add.51.own_ref, f32[280,128]{1,0:T(8,128)S(1)} %collective-permute-done.6.beside_ref, f32[280,128]{1,0:T(8,128)S(1)} %collective-permute-done.7.below_ref, f32[280,128]{1,0:T(8,128)S(1)} %collective-permute-done.8.across_ref), custom_call_target="tpu_custom_call" | custom-call | tf_op jit(solution)/shard_map/pallas_call | solution.py:380
  36.2 6.4 %collective-permute-start.9 = (f32[64,576]{1,0:T(8,128)S(1)}, f32[64,576]{1,0:T(8,128)S(1)}, u32[]{:S(2)}, u32[]{:S(2)}) collective-permute-start(f32[64,576]{1,0:T(8,128)S(1)} %shard_map.30), channel_id=1, source_target_pairs={{0,2},{1,3},{2,0},{3,1},{4,6},{5,7},{6,4},{7,5},{8,10},{9,11},{10,... | collective-permute-start | bytes 442376 | tf_op jit(solution)/shard_map/ppermute | solution.py:412
  42.5 1.0 %collective-permute-done.9 = f32[64,576]{1,0:T(8,128)S(1)} collective-permute-done((f32[64,576]{1,0:T(8,128)S(1)}, f32[64,576]{1,0:T(8,128)S(1)}, u32[]{:S(2)}, u32[]{:S(2)}) %collective-permute-start.9) | collective-permute-done | bytes 147488 | tf_op jit(solution)/shard_map/ppermute | solution.py:412
  43.6 0.7 %maximum_select_fusion = f32[2,64,576]{2,1,0:T(8,128)} fusion(f32[1,64,576]{2,1,0:T(8,128)S(1)} %bitcast.17, f32[1,64,576]{2,1,0:T(8,128)S(1)} %bitcast.16, pred[]{:T(512)S(6)} %eq.3), kind=kLoop, calls=%fused_computation | loop fusion | flops 221184 | bytes 589825 | tf_op jit(solution)/shard_map/jit(_where)/select_n | solution.py:431
  (4 shorter events, 0.1 us)
Async XLA Ops:
  2.9 2.5 %collective-permute-start = (f32[4,280,128]{2,1,0:T(8,128)S(1)}, f32[4,280,128]{2,1,0:T(8,128)S(1)}, u32[]{:S(2)}, u32[]{:S(2)}) collective-permute-start(f32[4,280,128]{2,1,0:T(8,128)S(1)} %get-tuple-element.10), channel_id=1, source_target_pairs={{0,2},{1,3},{2,0},{3,1},{4,6},{5,7},{6,4},{7,5},{8,10},{9,11},{10,... | collective-permute-start | bytes 1720328 | tf_op jit(solution)/shard_map/ppermute | solution.py:412
  5.5 4.3 %collective-permute-start.2 = (f32[280,128]{1,0:T(8,128)S(1)}, f32[280,128]{1,0:T(8,128)S(1)}, u32[]{:S(2)}, u32[]{:S(2)}) collective-permute-start(f32[280,128]{1,0:T(8,128)S(1)} %get-tuple-element.12), channel_id=1, source_target_pairs={{0,1},{1,0},{2,6},{3,7},{4,5},{5,4},{6,2},{7,3},{8,9},{9,8},{10,14... | collective-permute-start | bytes 430088 | tf_op jit(solution)/shard_map/ppermute | solution.py:412
  6.8 4.5 %collective-permute-start.1 = (f32[280,128]{1,0:T(8,128)S(1)}, f32[280,128]{1,0:T(8,128)S(1)}, u32[]{:S(2)}, u32[]{:S(2)}) collective-permute-start(f32[280,128]{1,0:T(8,128)S(1)} %get-tuple-element.11), channel_id=1, source_target_pairs={{0,1},{1,0},{2,6},{3,7},{4,5},{5,4},{6,2},{7,3},{8,9},{9,8},{10,14... | collective-permute-start | bytes 430088 | tf_op jit(solution)/shard_map/ppermute | solution.py:412
  9.9 4.3 %collective-permute-start.3 = (f32[280,128]{1,0:T(8,128)S(1)}, f32[280,128]{1,0:T(8,128)S(1)}, u32[]{:S(2)}, u32[]{:S(2)}) collective-permute-start(f32[280,128]{1,0:T(8,128)S(1)} %fusion.2), channel_id=1, source_target_pairs={{0,4},{1,5},{2,3},{3,2},{4,0},{5,1},{6,7},{7,6},{8,12},{9,13},{10,... | collective-permute-start | bytes 430088 | tf_op jit(solution)/shard_map/ppermute | solution.py:412
  14.2 6.4 %collective-permute-start.4 = (f32[280,128]{1,0:T(8,128)S(1)}, f32[280,128]{1,0:T(8,128)S(1)}, u32[]{:S(2)}, u32[]{:S(2)}) collective-permute-start(f32[280,128]{1,0:T(8,128)S(1)} %fusion.6), channel_id=1, source_target_pairs={{0,8},{1,9},{2,18},{3,19},{4,12},{5,13},{6,22},{7,23},{8,0},{9,1},... | collective-permute-start | bytes 430088 | tf_op jit(solution)/shard_map/ppermute | solution.py:412
  20.7 4.0 %collective-permute-start.5 = (f32[280,128]{1,0:T(8,128)S(1)}, f32[280,128]{1,0:T(8,128)S(1)}, u32[]{:S(2)}, u32[]{:S(2)}) collective-permute-start(f32[280,128]{1,0:T(8,128)S(1)} %add.50), channel_id=1, source_target_pairs={{0,16},{1,17},{2,10},{3,11},{4,20},{5,21},{6,14},{7,15},{8,24},{9,... | collective-permute-start | bytes 430088 | tf_op jit(solution)/shard_map/ppermute | solution.py:412
  24.7 4.2 %collective-permute-start.6 = (f32[280,128]{1,0:T(8,128)S(1)}, f32[280,128]{1,0:T(8,128)S(1)}, u32[]{:S(2)}, u32[]{:S(2)}) collective-permute-start(f32[280,128]{1,0:T(8,128)S(1)} %add.51.own_ref), channel_id=1, source_target_pairs={{0,1},{1,0},{2,3},{3,2},{4,5},{5,4},{6,7},{7,6},{8,9},{9,8},{10,11... | collective-permute-start | bytes 430088 | tf_op jit(solution)/shard_map/ppermute | solution.py:412
  26.0 4.8 %collective-permute-start.7 = (f32[280,128]{1,0:T(8,128)S(1)}, f32[280,128]{1,0:T(8,128)S(1)}, u32[]{:S(2)}, u32[]{:S(2)}) collective-permute-start(f32[280,128]{1,0:T(8,128)S(1)} %add.51.own_ref), channel_id=1, source_target_pairs={{0,4},{1,5},{2,6},{3,7},{4,0},{5,1},{6,2},{7,3},{8,12},{9,13},{10,... | collective-permute-start | bytes 430088 | tf_op jit(solution)/shard_map/ppermute | solution.py:412
  27.3 4.8 %collective-permute-start.8 = (f32[280,128]{1,0:T(8,128)S(1)}, f32[280,128]{1,0:T(8,128)S(1)}, u32[]{:S(2)}, u32[]{:S(2)}) collective-permute-start(f32[280,128]{1,0:T(8,128)S(1)} %add.51.own_ref), channel_id=1, source_target_pairs={{0,5},{1,4},{2,7},{3,6},{4,1},{5,0},{6,3},{7,2},{8,13},{9,12},{10,... | collective-permute-start | bytes 430088 | tf_op jit(solution)/shard_map/ppermute | solution.py:412
  36.2 7.4 %collective-permute-start.9 = (f32[64,576]{1,0:T(8,128)S(1)}, f32[64,576]{1,0:T(8,128)S(1)}, u32[]{:S(2)}, u32[]{:S(2)}) collective-permute-start(f32[64,576]{1,0:T(8,128)S(1)} %shard_map.30), channel_id=1, source_target_pairs={{0,2},{1,3},{2,0},{3,1},{4,6},{5,7},{6,4},{7,5},{8,10},{9,11},{10,... | collective-permute-start | bytes 442376 | tf_op jit(solution)/shard_map/ppermute | solution.py:412

commit v7 on v6

--- a/solution.py
+++ b/solution.py
@@ -297,6 +297,15 @@
         col0[dr], col1[dr] = load("cc%d" % dr)
     down[1, 2], down[2, 2] = load("x22")
 
+    eg, inv_g = normalized(g)
+    eg2 = dot3(eg, eg)
+    pg = eg + dot3(eg, eg2) + eg2
+    w0 = load("w0z")
+    w1 = load("w1z")
+    w2 = load("w2z")
+    w = jnp.concatenate([w00, w0[0], w0[1], w10, w1[0], w1[1], w20, w2[0], w2[1]], axis=1)
+    w = w + dot3(pg, w)
+    w = w.T
     squares = []
 
     def put(t, u, block):
@@ -354,15 +363,7 @@
     shift = DAMP * trace / n
     inv_a = lax.rsqrt(jnp.sum(sum(squares)) + shift * (2.0 * trace + n * shift))
     keep = 1.0 - inv_a * shift
-    eg, inv_g = normalized(g)
-    eg2 = dot3(eg, eg)
-    pg = eg + dot3(eg, eg2) + eg2
-    w0 = load("w0z")
-    w1 = load("w1z")
-    w2 = load("w2z")
-    w = jnp.concatenate([w00, w0[0], w0[1], w10, w1[0], w1[1], w20, w2[0], w2[1]], axis=1)
-    w = w + dot3(pg, w)
-    v = w.T * (inv_a * inv_g * total_rows)
+    v = w * (inv_a * inv_g * total_rows)
 
     def apply(v):
         vh, vl = split(v)
@@ -428,7 +429,9 @@
     mine = precondition((own, beside, below, across), total_rows)
     other = swap(mine, cores)
     core = lax.rem(lax.axis_index("dp"), 2)
-    return jnp.where(core == 0, jnp.stack([mine, other]), jnp.stack([other, mine]))
+    result = jnp.zeros((2,) + mine.shape, F32)
+    result = lax.dynamic_update_slice(result, mine[None], (core, 0, 0))
+    return lax.dynamic_update_slice(result, other[None], (1 - core, 0, 0))
 
 
 def solution(mesh):

time: 44.5 us -> 44.3 us (level)
  other arithmetic: 0.91 us -> 0.16 us
  local copies, waits for them, and re-layouts: 0 us -> 0.72 us
    select_n x1 -> x0, other arithmetic: 0.75 us -> none  [shards(): jnp.where(core == 0, jnp.stack([mine, other]), jnp.stack([other, mine]))]
    dynamic_update_slice x0 -> x2, local copies, waits for them, and re-layouts: none -> 0.7 us  [the longest x1 0.68 us: shards(): return lax.dynamic_update_slice(result, other[None], (1 - core, 0, 0))]
where the time goes in v7:
time: 44.3 us; the launch traced here: 44.2 us
  waiting for transfers between devices  21.7 us (49%)
  starting transfers between devices  12.8 us (29%)
  Pallas kernels  8.68 us (20%)
  local copies, waits for them, and re-layouts  0.72 us (2%)
    ppermute x10, waiting for transfers between devices, shards(): swap = lambda a, p: lax.ppermute(a, ('dp', 'grp'), p)  21.7 us
    ppermute x10, starting transfers between devices, shards(): swap = lambda a, p: lax.ppermute(a, ('dp', 'grp'), p)  12.8 us
    pallas_call x2, Pallas kernels, local_sums(): pl.pallas_call(functools.partial(local_kernel, height, width, own), out_s...  4.72 us
    pallas_call x1, Pallas kernels, precondition(): pl.pallas_call(functools.partial(final_kernel, float(total_rows)), out_sh...  3.96 us
  transfers between devices with their start and end apart: 10, of which 9 were waited for; matrix products, arithmetic and copies ran while one was open for 0% of the time, Pallas kernels for 4%

profile of v7, /device:TPU:25, one launch (start us, length us, event | category | flops | bytes accessed | tf_op | source)
XLA Modules:
  0.0 44.2 jit_solution(8249932123232698138)
XLA Ops:
  0.0 2.9 %shard_map.28 = (f32[4,280,128]{2,1,0:T(8,128)S(1)}, bf16[56,3584]{1,0:T(8,128)(2,1)S(1)}, bf16[56,3584]{1,0:T(8,128)(2,1)S(1)}) custom-call(bf16[2,1,56,3584]{3,2,1,0:T(8,128)(2,1)} %refs_0_.1, bf16[2,1,56,3584]{3,2,1,0:T(8,128)(2,1)} %refs_1_.1), custom_call_target="tpu_custom_call" | custom-call | tf_op jit(solution)/shard_map/pallas_call | solution.py:220
  2.9 0.7 %collective-permute-start = (f32[4,280,128]{2,1,0:T(8,128)S(1)}, f32[4,280,128]{2,1,0:T(8,128)S(1)}, u32[]{:S(2)}, u32[]{:S(2)}) collective-permute-start(f32[4,280,128]{2,1,0:T(8,128)S(1)} %get-tuple-element.10), channel_id=1, source_target_pairs={{0,2},{1,3},{2,0},{3,1},{4,6},{5,7},{6,4},{7,5},{8,10},{9,11},{10,... | collective-permute-start | bytes 1720328 | tf_op jit(solution)/shard_map/ppermute | solution.py:413
  3.7 1.8 %shard_map.29 = f32[4,280,128]{2,1,0:T(8,128)S(1)} custom-call(bf16[56,3584]{1,0:T(8,128)(2,1)S(1)} %get-tuple-element.8.refs_0_, bf16[56,3584]{1,0:T(8,128)(2,1)S(1)} %get-tuple-element.9.refs_1_), custom_call_target="tpu_custom_call" | custom-call | tf_op jit(solution)/shard_map/pallas_call | solution.py:220
  5.5 0.0 collective-permute-done
  5.5 1.3 %collective-permute-start.2 = (f32[280,128]{1,0:T(8,128)S(1)}, f32[280,128]{1,0:T(8,128)S(1)}, u32[]{:S(2)}, u32[]{:S(2)}) collective-permute-start(f32[280,128]{1,0:T(8,128)S(1)} %get-tuple-element.12), channel_id=1, source_target_pairs={{0,1},{1,0},{2,6},{3,7},{4,5},{5,4},{6,2},{7,3},{8,9},{9,8},{10,14... | collective-permute-start | bytes 430088 | tf_op jit(solution)/shard_map/ppermute | solution.py:413
  6.8 0.2 collective-permute-start.1
  7.1 2.8 %collective-permute-done.2 = f32[280,128]{1,0:T(8,128)S(1)} collective-permute-done((f32[280,128]{1,0:T(8,128)S(1)}, f32[280,128]{1,0:T(8,128)S(1)}, u32[]{:S(2)}, u32[]{:S(2)}) %collective-permute-start.2) | collective-permute-done | bytes 143392 | tf_op jit(solution)/shard_map/ppermute | solution.py:413
  9.9 1.3 %collective-permute-start.3 = (f32[280,128]{1,0:T(8,128)S(1)}, f32[280,128]{1,0:T(8,128)S(1)}, u32[]{:S(2)}, u32[]{:S(2)}) collective-permute-start(f32[280,128]{1,0:T(8,128)S(1)} %fusion.2), channel_id=1, source_target_pairs={{0,4},{1,5},{2,3},{3,2},{4,0},{5,1},{6,7},{7,6},{8,12},{9,13},{10,... | collective-permute-start | bytes 430088 | tf_op jit(solution)/shard_map/ppermute | solution.py:413
  11.1 0.2 collective-permute-done.1
  11.4 2.8 %collective-permute-done.3 = f32[280,128]{1,0:T(8,128)S(1)} collective-permute-done((f32[280,128]{1,0:T(8,128)S(1)}, f32[280,128]{1,0:T(8,128)S(1)}, u32[]{:S(2)}, u32[]{:S(2)}) %collective-permute-start.3) | collective-permute-done | bytes 143392 | tf_op jit(solution)/shard_map/ppermute | solution.py:413
  14.2 0.1 fusion.6
  14.2 0.1 collective-permute-start.4
  14.4 6.3 %collective-permute-done.4 = f32[280,128]{1,0:T(8,128)S(1)} collective-permute-done((f32[280,128]{1,0:T(8,128)S(1)}, f32[280,128]{1,0:T(8,128)S(1)}, u32[]{:S(2)}, u32[]{:S(2)}) %collective-permute-start.4) | collective-permute-done | bytes 143392 | tf_op jit(solution)/shard_map/ppermute | solution.py:413
  20.7 0.1 collective-permute-start.5
  20.8 3.9 %collective-permute-done.5 = f32[280,128]{1,0:T(8,128)S(1)} collective-permute-done((f32[280,128]{1,0:T(8,128)S(1)}, f32[280,128]{1,0:T(8,128)S(1)}, u32[]{:S(2)}, u32[]{:S(2)}) %collective-permute-start.5) | collective-permute-done | bytes 143392 | tf_op jit(solution)/shard_map/ppermute | solution.py:413
  24.7 1.3 %collective-permute-start.6 = (f32[280,128]{1,0:T(8,128)S(1)}, f32[280,128]{1,0:T(8,128)S(1)}, u32[]{:S(2)}, u32[]{:S(2)}) collective-permute-start(f32[280,128]{1,0:T(8,128)S(1)} %add.58.own_ref), channel_id=1, source_target_pairs={{0,1},{1,0},{2,3},{3,2},{4,5},{5,4},{6,7},{7,6},{8,9},{9,8},{10,11... | collective-permute-start | bytes 430088 | tf_op jit(solution)/shard_map/ppermute | solution.py:413
  26.0 1.2 %collective-permute-start.7 = (f32[280,128]{1,0:T(8,128)S(1)}, f32[280,128]{1,0:T(8,128)S(1)}, u32[]{:S(2)}, u32[]{:S(2)}) collective-permute-start(f32[280,128]{1,0:T(8,128)S(1)} %add.58.own_ref), channel_id=1, source_target_pairs={{0,4},{1,5},{2,6},{3,7},{4,0},{5,1},{6,2},{7,3},{8,12},{9,13},{10,... | collective-permute-start | bytes 430088 | tf_op jit(solution)/shard_map/ppermute | solution.py:413
  27.3 0.2 collective-permute-start.8
  27.4 1.5 %collective-permute-done.6.beside_ref = f32[280,128]{1,0:T(8,128)S(1)} collective-permute-done((f32[280,128]{1,0:T(8,128)S(1)}, f32[280,128]{1,0:T(8,128)S(1)}, u32[]{:S(2)}, u32[]{:S(2)}) %collective-permute-start.6) | collective-permute-done | bytes 143392 | tf_op jit(solution)/shard_map/ppermute | solution.py:413
  28.9 1.9 %collective-permute-done.7.below_ref = f32[280,128]{1,0:T(8,128)S(1)} collective-permute-done((f32[280,128]{1,0:T(8,128)S(1)}, f32[280,128]{1,0:T(8,128)S(1)}, u32[]{:S(2)}, u32[]{:S(2)}) %collective-permute-start.7) | collective-permute-done | bytes 143392 | tf_op jit(solution)/shard_map/ppermute | solution.py:413
  30.8 1.3 %collective-permute-done.8.across_ref = f32[280,128]{1,0:T(8,128)S(1)} collective-permute-done((f32[280,128]{1,0:T(8,128)S(1)}, f32[280,128]{1,0:T(8,128)S(1)}, u32[]{:S(2)}, u32[]{:S(2)}) %collective-permute-start.8) | collective-permute-done | bytes 143392 | tf_op jit(solution)/shard_map/ppermute | solution.py:413
  32.1 4.0 %shard_map.30 = f32[64,576]{1,0:T(8,128)S(1)} custom-call(f32[280,128]{1,0:T(8,128)S(1)} %add.58.own_ref, f32[280,128]{1,0:T(8,128)S(1)} %collective-permute-done.6.beside_ref, f32[280,128]{1,0:T(8,128)S(1)} %collective-permute-done.7.below_ref, f32[280,128]{1,0:T(8,128)S(1)} %collective-permute-done.8.across_ref), custom_call_target="tpu_custom_call" | custom-call | tf_op jit(solution)/shard_map/pallas_call | solution.py:381
  36.1 6.4 %collective-permute-start.9 = (f32[64,576]{1,0:T(8,128)S(1)}, f32[64,576]{1,0:T(8,128)S(1)}, u32[]{:S(2)}, u32[]{:S(2)}) collective-permute-start(f32[64,576]{1,0:T(8,128)S(1)} %shard_map.30), channel_id=1, source_target_pairs={{0,2},{1,3},{2,0},{3,1},{4,6},{5,7},{6,4},{7,5},{8,10},{9,11},{10,... | collective-permute-start | bytes 442376 | tf_op jit(solution)/shard_map/ppermute | solution.py:413
  42.5 0.0 copy-start
  42.5 1.0 %collective-permute-done.9 = f32[64,576]{1,0:T(8,128)S(1)} collective-permute-done((f32[64,576]{1,0:T(8,128)S(1)}, f32[64,576]{1,0:T(8,128)S(1)}, u32[]{:S(2)}, u32[]{:S(2)}) %collective-permute-start.9) | collective-permute-done | bytes 147488 | tf_op jit(solution)/shard_map/ppermute | solution.py:413
  43.5 0.0 copy-done
  43.5 0.7 %bitcast_dynamic-update-slice_fusion = f32[2,64,576]{2,1,0:T(8,128)} fusion(f32[2,64,576]{2,1,0:T(8,128)} %copy-done, s32[]{:T(128)S(6)} %select_n.7, f32[64,576]{1,0:T(8,128)S(1)} %collective-permute-done.9), kind=kLoop, calls=%fused_computation | loop fusion | bytes 311300 | tf_op jit(solution)/shard_map/dynamic_update_slice | solution.py:434
  (6 shorter events, 0.1 us)
Async XLA Ops:
  2.9 2.5 %collective-permute-start = (f32[4,280,128]{2,1,0:T(8,128)S(1)}, f32[4,280,128]{2,1,0:T(8,128)S(1)}, u32[]{:S(2)}, u32[]{:S(2)}) collective-permute-start(f32[4,280,128]{2,1,0:T(8,128)S(1)} %get-tuple-element.10), channel_id=1, source_target_pairs={{0,2},{1,3},{2,0},{3,1},{4,6},{5,7},{6,4},{7,5},{8,10},{9,11},{10,... | collective-permute-start | bytes 1720328 | tf_op jit(solution)/shard_map/ppermute | solution.py:413
  5.5 4.3 %collective-permute-start.2 = (f32[280,128]{1,0:T(8,128)S(1)}, f32[280,128]{1,0:T(8,128)S(1)}, u32[]{:S(2)}, u32[]{:S(2)}) collective-permute-start(f32[280,128]{1,0:T(8,128)S(1)} %get-tuple-element.12), channel_id=1, source_target_pairs={{0,1},{1,0},{2,6},{3,7},{4,5},{5,4},{6,2},{7,3},{8,9},{9,8},{10,14... | collective-permute-start | bytes 430088 | tf_op jit(solution)/shard_map/ppermute | solution.py:413
  6.8 4.5 %collective-permute-start.1 = (f32[280,128]{1,0:T(8,128)S(1)}, f32[280,128]{1,0:T(8,128)S(1)}, u32[]{:S(2)}, u32[]{:S(2)}) collective-permute-start(f32[280,128]{1,0:T(8,128)S(1)} %get-tuple-element.11), channel_id=1, source_target_pairs={{0,1},{1,0},{2,6},{3,7},{4,5},{5,4},{6,2},{7,3},{8,9},{9,8},{10,14... | collective-permute-start | bytes 430088 | tf_op jit(solution)/shard_map/ppermute | solution.py:413
  9.9 4.3 %collective-permute-start.3 = (f32[280,128]{1,0:T(8,128)S(1)}, f32[280,128]{1,0:T(8,128)S(1)}, u32[]{:S(2)}, u32[]{:S(2)}) collective-permute-start(f32[280,128]{1,0:T(8,128)S(1)} %fusion.2), channel_id=1, source_target_pairs={{0,4},{1,5},{2,3},{3,2},{4,0},{5,1},{6,7},{7,6},{8,12},{9,13},{10,... | collective-permute-start | bytes 430088 | tf_op jit(solution)/shard_map/ppermute | solution.py:413
  14.2 6.4 %collective-permute-start.4 = (f32[280,128]{1,0:T(8,128)S(1)}, f32[280,128]{1,0:T(8,128)S(1)}, u32[]{:S(2)}, u32[]{:S(2)}) collective-permute-start(f32[280,128]{1,0:T(8,128)S(1)} %fusion.6), channel_id=1, source_target_pairs={{0,8},{1,9},{2,18},{3,19},{4,12},{5,13},{6,22},{7,23},{8,0},{9,1},... | collective-permute-start | bytes 430088 | tf_op jit(solution)/shard_map/ppermute | solution.py:413
  20.7 4.0 %collective-permute-start.5 = (f32[280,128]{1,0:T(8,128)S(1)}, f32[280,128]{1,0:T(8,128)S(1)}, u32[]{:S(2)}, u32[]{:S(2)}) collective-permute-start(f32[280,128]{1,0:T(8,128)S(1)} %add.57), channel_id=1, source_target_pairs={{0,16},{1,17},{2,10},{3,11},{4,20},{5,21},{6,14},{7,15},{8,24},{9,... | collective-permute-start | bytes 430088 | tf_op jit(solution)/shard_map/ppermute | solution.py:413
  24.7 4.2 %collective-permute-start.6 = (f32[280,128]{1,0:T(8,128)S(1)}, f32[280,128]{1,0:T(8,128)S(1)}, u32[]{:S(2)}, u32[]{:S(2)}) collective-permute-start(f32[280,128]{1,0:T(8,128)S(1)} %add.58.own_ref), channel_id=1, source_target_pairs={{0,1},{1,0},{2,3},{3,2},{4,5},{5,4},{6,7},{7,6},{8,9},{9,8},{10,11... | collective-permute-start | bytes 430088 | tf_op jit(solution)/shard_map/ppermute | solution.py:413
  26.0 4.8 %collective-permute-start.7 = (f32[280,128]{1,0:T(8,128)S(1)}, f32[280,128]{1,0:T(8,128)S(1)}, u32[]{:S(2)}, u32[]{:S(2)}) collective-permute-start(f32[280,128]{1,0:T(8,128)S(1)} %add.58.own_ref), channel_id=1, source_target_pairs={{0,4},{1,5},{2,6},{3,7},{4,0},{5,1},{6,2},{7,3},{8,12},{9,13},{10,... | collective-permute-start | bytes 430088 | tf_op jit(solution)/shard_map/ppermute | solution.py:413
  27.3 4.8 %collective-permute-start.8 = (f32[280,128]{1,0:T(8,128)S(1)}, f32[280,128]{1,0:T(8,128)S(1)}, u32[]{:S(2)}, u32[]{:S(2)}) collective-permute-start(f32[280,128]{1,0:T(8,128)S(1)} %add.58.own_ref), channel_id=1, source_target_pairs={{0,5},{1,4},{2,7},{3,6},{4,1},{5,0},{6,3},{7,2},{8,13},{9,12},{10,... | collective-permute-start | bytes 430088 | tf_op jit(solution)/shard_map/ppermute | solution.py:413
  36.1 7.4 %collective-permute-start.9 = (f32[64,576]{1,0:T(8,128)S(1)}, f32[64,576]{1,0:T(8,128)S(1)}, u32[]{:S(2)}, u32[]{:S(2)}) collective-permute-start(f32[64,576]{1,0:T(8,128)S(1)} %shard_map.30), channel_id=1, source_target_pairs={{0,2},{1,3},{2,0},{3,1},{4,6},{5,7},{6,4},{7,5},{8,10},{9,11},{10,... | collective-permute-start | bytes 442376 | tf_op jit(solution)/shard_map/ppermute | solution.py:413
  42.5 1.0 %copy-start = (f32[2,64,576]{2,1,0:T(8,128)}, f32[2,64,576]{2,1,0:T(8,128)S(1)}, u32[]{:S(2)}) copy-start(f32[2,64,576]{2,1,0:T(8,128)S(1)} %bitcast_dynamic-update-slice_fusion.1) | copy-start | bytes 884740

commit v8 on v7

--- a/solution.py
+++ b/solution.py
@@ -83,10 +83,8 @@
     n_edge = edges.shape[1] - 16
     if not own:
         copies[0].wait()
-        copies[1].wait()
     for pair in range(wp // 2):
         tiles_x = []
-        tiles_g = []
         for half in range(2):
             j = 2 * pair + half
             block = jnp.concatenate([xbuf[:, j * PAIR : (j + 1) * PAIR].astype(F32), pad], axis=0)
@@ -98,9 +96,15 @@
             shifted[2, at : at + ROW, :] = pltpu.roll(block, ROW - 1, 0).astype(BF16)
             shifted[3, at : at + ROW, :] = pltpu.roll(block, ROW - 2, 0).astype(BF16)
             tiles_x.append(block)
+        lanes = slice(pair * PAIR, (pair + 1) * PAIR)
+        lhs_t[0:PAIR, lanes] = jnp.concatenate(tiles_x, axis=0).T.astype(BF16)
+    if not own:
+        copies[1].wait()
+    for pair in range(wp // 2):
+        tiles_g = []
+        for j in (2 * pair, 2 * pair + 1):
             tiles_g.append(jnp.concatenate([gbuf[:, j * PAIR : (j + 1) * PAIR].astype(F32), pad], axis=0))
         lanes = slice(pair * PAIR, (pair + 1) * PAIR)
-        lhs_t[0:PAIR, lanes] = jnp.concatenate(tiles_x, axis=0).T.astype(BF16)
         lhs_t[PAIR : 2 * PAIR, lanes] = jnp.concatenate(tiles_g, axis=0).T.astype(BF16)
 
     def product(wanted, part):

time: 44.3 us -> 44.5 us (level)
  no operation moved by 1% of the time
where the time goes in v8:
time: 44.5 us; the launch traced here: 44.4 us
  waiting for transfers between devices  21.7 us (49%)
  starting transfers between devices  12.8 us (29%)
  Pallas kernels  8.89 us (20%)
  local copies, waits for them, and re-layouts  0.72 us (2%)
    ppermute x10, waiting for transfers between devices, shards(): swap = lambda a, p: lax.ppermute(a, ('dp', 'grp'), p)  21.7 us
    ppermute x10, starting transfers between devices, shards(): swap = lambda a, p: lax.ppermute(a, ('dp', 'grp'), p)  12.8 us
    pallas_call x2, Pallas kernels, local_sums(): pl.pallas_call(functools.partial(local_kernel, height, width, own), out_s...  4.93 us
    pallas_call x1, Pallas kernels, precondition(): pl.pallas_call(functools.partial(final_kernel, float(total_rows)), out_sh...  3.96 us
  transfers between devices with their start and end apart: 10, of which 9 were waited for; matrix products, arithmetic and copies ran while one was open for 0% of the time, Pallas kernels for 4%

profile of v8, /device:TPU:25, one launch (start us, length us, event | category | flops | bytes accessed | tf_op | source)
XLA Modules:
  0.0 44.4 jit_solution(13850277062524902625)
XLA Ops:
  0.0 3.2 %shard_map.28 = (f32[4,280,128]{2,1,0:T(8,128)S(1)}, bf16[56,3584]{1,0:T(8,128)(2,1)S(1)}, bf16[56,3584]{1,0:T(8,128)(2,1)S(1)}) custom-call(bf16[2,1,56,3584]{3,2,1,0:T(8,128)(2,1)} %refs_0_.1, bf16[2,1,56,3584]{3,2,1,0:T(8,128)(2,1)} %refs_1_.1), custom_call_target="tpu_custom_call" | custom-call | tf_op jit(solution)/shard_map/pallas_call | solution.py:224
  3.2 0.7 %collective-permute-start = (f32[4,280,128]{2,1,0:T(8,128)S(1)}, f32[4,280,128]{2,1,0:T(8,128)S(1)}, u32[]{:S(2)}, u32[]{:S(2)}) collective-permute-start(f32[4,280,128]{2,1,0:T(8,128)S(1)} %get-tuple-element.10), channel_id=1, source_target_pairs={{0,2},{1,3},{2,0},{3,1},{4,6},{5,7},{6,4},{7,5},{8,10},{9,11},{10,... | collective-permute-start | bytes 1720328 | tf_op jit(solution)/shard_map/ppermute | solution.py:417
  3.9 1.8 %shard_map.29 = f32[4,280,128]{2,1,0:T(8,128)S(1)} custom-call(bf16[56,3584]{1,0:T(8,128)(2,1)S(1)} %get-tuple-element.8.refs_0_, bf16[56,3584]{1,0:T(8,128)(2,1)S(1)} %get-tuple-element.9.refs_1_), custom_call_target="tpu_custom_call" | custom-call | tf_op jit(solution)/shard_map/pallas_call | solution.py:224
  5.7 0.0 collective-permute-done
  5.7 1.3 %collective-permute-start.2 = (f32[280,128]{1,0:T(8,128)S(1)}, f32[280,128]{1,0:T(8,128)S(1)}, u32[]{:S(2)}, u32[]{:S(2)}) collective-permute-start(f32[280,128]{1,0:T(8,128)S(1)} %get-tuple-element.12), channel_id=1, source_target_pairs={{0,1},{1,0},{2,6},{3,7},{4,5},{5,4},{6,2},{7,3},{8,9},{9,8},{10,14... | collective-permute-start | bytes 430088 | tf_op jit(solution)/shard_map/ppermute | solution.py:417
  7.0 0.2 collective-permute-start.1
  7.3 2.8 %collective-permute-done.2 = f32[280,128]{1,0:T(8,128)S(1)} collective-permute-done((f32[280,128]{1,0:T(8,128)S(1)}, f32[280,128]{1,0:T(8,128)S(1)}, u32[]{:S(2)}, u32[]{:S(2)}) %collective-permute-start.2) | collective-permute-done | bytes 143392 | tf_op jit(solution)/shard_map/ppermute | solution.py:417
  10.1 1.3 %collective-permute-start.3 = (f32[280,128]{1,0:T(8,128)S(1)}, f32[280,128]{1,0:T(8,128)S(1)}, u32[]{:S(2)}, u32[]{:S(2)}) collective-permute-start(f32[280,128]{1,0:T(8,128)S(1)} %fusion.2), channel_id=1, source_target_pairs={{0,4},{1,5},{2,3},{3,2},{4,0},{5,1},{6,7},{7,6},{8,12},{9,13},{10,... | collective-permute-start | bytes 430088 | tf_op jit(solution)/shard_map/ppermute | solution.py:417
  11.4 0.2 collective-permute-done.1
  11.6 2.8 %collective-permute-done.3 = f32[280,128]{1,0:T(8,128)S(1)} collective-permute-done((f32[280,128]{1,0:T(8,128)S(1)}, f32[280,128]{1,0:T(8,128)S(1)}, u32[]{:S(2)}, u32[]{:S(2)}) %collective-permute-start.3) | collective-permute-done | bytes 143392 | tf_op jit(solution)/shard_map/ppermute | solution.py:417
  14.4 0.1 fusion.6
  14.5 0.1 collective-permute-start.4
  14.6 6.3 %collective-permute-done.4 = f32[280,128]{1,0:T(8,128)S(1)} collective-permute-done((f32[280,128]{1,0:T(8,128)S(1)}, f32[280,128]{1,0:T(8,128)S(1)}, u32[]{:S(2)}, u32[]{:S(2)}) %collective-permute-start.4) | collective-permute-done | bytes 143392 | tf_op jit(solution)/shard_map/ppermute | solution.py:417
  20.9 0.1 collective-permute-start.5
  21.0 3.9 %collective-permute-done.5 = f32[280,128]{1,0:T(8,128)S(1)} collective-permute-done((f32[280,128]{1,0:T(8,128)S(1)}, f32[280,128]{1,0:T(8,128)S(1)}, u32[]{:S(2)}, u32[]{:S(2)}) %collective-permute-start.5) | collective-permute-done | bytes 143392 | tf_op jit(solution)/shard_map/ppermute | solution.py:417
  24.9 1.3 %collective-permute-start.6 = (f32[280,128]{1,0:T(8,128)S(1)}, f32[280,128]{1,0:T(8,128)S(1)}, u32[]{:S(2)}, u32[]{:S(2)}) collective-permute-start(f32[280,128]{1,0:T(8,128)S(1)} %add.58.own_ref), channel_id=1, source_target_pairs={{0,1},{1,0},{2,3},{3,2},{4,5},{5,4},{6,7},{7,6},{8,9},{9,8},{10,11... | collective-permute-start | bytes 430088 | tf_op jit(solution)/shard_map/ppermute | solution.py:417
  26.2 1.2 %collective-permute-start.7 = (f32[280,128]{1,0:T(8,128)S(1)}, f32[280,128]{1,0:T(8,128)S(1)}, u32[]{:S(2)}, u32[]{:S(2)}) collective-permute-start(f32[280,128]{1,0:T(8,128)S(1)} %add.58.own_ref), channel_id=1, source_target_pairs={{0,4},{1,5},{2,6},{3,7},{4,0},{5,1},{6,2},{7,3},{8,12},{9,13},{10,... | collective-permute-start | bytes 430088 | tf_op jit(solution)/shard_map/ppermute | solution.py:417
  27.5 0.2 collective-permute-start.8
  27.7 1.5 %collective-permute-done.6.beside_ref = f32[280,128]{1,0:T(8,128)S(1)} collective-permute-done((f32[280,128]{1,0:T(8,128)S(1)}, f32[280,128]{1,0:T(8,128)S(1)}, u32[]{:S(2)}, u32[]{:S(2)}) %collective-permute-start.6) | collective-permute-done | bytes 143392 | tf_op jit(solution)/shard_map/ppermute | solution.py:417
  29.1 1.9 %collective-permute-done.7.below_ref = f32[280,128]{1,0:T(8,128)S(1)} collective-permute-done((f32[280,128]{1,0:T(8,128)S(1)}, f32[280,128]{1,0:T(8,128)S(1)}, u32[]{:S(2)}, u32[]{:S(2)}) %collective-permute-start.7) | collective-permute-done | bytes 143392 | tf_op jit(solution)/shard_map/ppermute | solution.py:417
  31.0 1.3 %collective-permute-done.8.across_ref = f32[280,128]{1,0:T(8,128)S(1)} collective-permute-done((f32[280,128]{1,0:T(8,128)S(1)}, f32[280,128]{1,0:T(8,128)S(1)}, u32[]{:S(2)}, u32[]{:S(2)}) %collective-permute-start.8) | collective-permute-done | bytes 143392 | tf_op jit(solution)/shard_map/ppermute | solution.py:417
  32.3 4.0 %shard_map.30 = f32[64,576]{1,0:T(8,128)S(1)} custom-call(f32[280,128]{1,0:T(8,128)S(1)} %add.58.own_ref, f32[280,128]{1,0:T(8,128)S(1)} %collective-permute-done.6.beside_ref, f32[280,128]{1,0:T(8,128)S(1)} %collective-permute-done.7.below_ref, f32[280,128]{1,0:T(8,128)S(1)} %collective-permute-done.8.across_ref), custom_call_target="tpu_custom_call" | custom-call | tf_op jit(solution)/shard_map/pallas_call | solution.py:385
  36.3 6.4 %collective-permute-start.9 = (f32[64,576]{1,0:T(8,128)S(1)}, f32[64,576]{1,0:T(8,128)S(1)}, u32[]{:S(2)}, u32[]{:S(2)}) collective-permute-start(f32[64,576]{1,0:T(8,128)S(1)} %shard_map.30), channel_id=1, source_target_pairs={{0,2},{1,3},{2,0},{3,1},{4,6},{5,7},{6,4},{7,5},{8,10},{9,11},{10,... | collective-permute-start | bytes 442376 | tf_op jit(solution)/shard_map/ppermute | solution.py:417
  42.7 0.0 copy-start
  42.7 1.0 %collective-permute-done.9 = f32[64,576]{1,0:T(8,128)S(1)} collective-permute-done((f32[64,576]{1,0:T(8,128)S(1)}, f32[64,576]{1,0:T(8,128)S(1)}, u32[]{:S(2)}, u32[]{:S(2)}) %collective-permute-start.9) | collective-permute-done | bytes 147488 | tf_op jit(solution)/shard_map/ppermute | solution.py:417
  43.7 0.0 copy-done
  43.7 0.7 %bitcast_dynamic-update-slice_fusion = f32[2,64,576]{2,1,0:T(8,128)} fusion(f32[2,64,576]{2,1,0:T(8,128)} %copy-done, s32[]{:T(128)S(6)} %select_n.7, f32[64,576]{1,0:T(8,128)S(1)} %collective-permute-done.9), kind=kLoop, calls=%fused_computation | loop fusion | bytes 311300 | tf_op jit(solution)/shard_map/dynamic_update_slice | solution.py:438
  (6 shorter events, 0.1 us)
Async XLA Ops:
  3.2 2.5 %collective-permute-start = (f32[4,280,128]{2,1,0:T(8,128)S(1)}, f32[4,280,128]{2,1,0:T(8,128)S(1)}, u32[]{:S(2)}, u32[]{:S(2)}) collective-permute-start(f32[4,280,128]{2,1,0:T(8,128)S(1)} %get-tuple-element.10), channel_id=1, source_target_pairs={{0,2},{1,3},{2,0},{3,1},{4,6},{5,7},{6,4},{7,5},{8,10},{9,11},{10,... | collective-permute-start | bytes 1720328 | tf_op jit(solution)/shard_map/ppermute | solution.py:417
  5.7 4.3 %collective-permute-start.2 = (f32[280,128]{1,0:T(8,128)S(1)}, f32[280,128]{1,0:T(8,128)S(1)}, u32[]{:S(2)}, u32[]{:S(2)}) collective-permute-start(f32[280,128]{1,0:T(8,128)S(1)} %get-tuple-element.12), channel_id=1, source_target_pairs={{0,1},{1,0},{2,6},{3,7},{4,5},{5,4},{6,2},{7,3},{8,9},{9,8},{10,14... | collective-permute-start | bytes 430088 | tf_op jit(solution)/shard_map/ppermute | solution.py:417
  7.0 4.5 %collective-permute-start.1 = (f32[280,128]{1,0:T(8,128)S(1)}, f32[280,128]{1,0:T(8,128)S(1)}, u32[]{:S(2)}, u32[]{:S(2)}) collective-permute-start(f32[280,128]{1,0:T(8,128)S(1)} %get-tuple-element.11), channel_id=1, source_target_pairs={{0,1},{1,0},{2,6},{3,7},{4,5},{5,4},{6,2},{7,3},{8,9},{9,8},{10,14... | collective-permute-start | bytes 430088 | tf_op jit(solution)/shard_map/ppermute | solution.py:417
  10.1 4.3 %collective-permute-start.3 = (f32[280,128]{1,0:T(8,128)S(1)}, f32[280,128]{1,0:T(8,128)S(1)}, u32[]{:S(2)}, u32[]{:S(2)}) collective-permute-start(f32[280,128]{1,0:T(8,128)S(1)} %fusion.2), channel_id=1, source_target_pairs={{0,4},{1,5},{2,3},{3,2},{4,0},{5,1},{6,7},{7,6},{8,12},{9,13},{10,... | collective-permute-start | bytes 430088 | tf_op jit(solution)/shard_map/ppermute | solution.py:417
  14.5 6.4 %collective-permute-start.4 = (f32[280,128]{1,0:T(8,128)S(1)}, f32[280,128]{1,0:T(8,128)S(1)}, u32[]{:S(2)}, u32[]{:S(2)}) collective-permute-start(f32[280,128]{1,0:T(8,128)S(1)} %fusion.6), channel_id=1, source_target_pairs={{0,8},{1,9},{2,18},{3,19},{4,12},{5,13},{6,22},{7,23},{8,0},{9,1},... | collective-permute-start | bytes 430088 | tf_op jit(solution)/shard_map/ppermute | solution.py:417
  20.9 4.0 %collective-permute-start.5 = (f32[280,128]{1,0:T(8,128)S(1)}, f32[280,128]{1,0:T(8,128)S(1)}, u32[]{:S(2)}, u32[]{:S(2)}) collective-permute-start(f32[280,128]{1,0:T(8,128)S(1)} %add.57), channel_id=1, source_target_pairs={{0,16},{1,17},{2,10},{3,11},{4,20},{5,21},{6,14},{7,15},{8,24},{9,... | collective-permute-start | bytes 430088 | tf_op jit(solution)/shard_map/ppermute | solution.py:417
  24.9 4.2 %collective-permute-start.6 = (f32[280,128]{1,0:T(8,128)S(1)}, f32[280,128]{1,0:T(8,128)S(1)}, u32[]{:S(2)}, u32[]{:S(2)}) collective-permute-start(f32[280,128]{1,0:T(8,128)S(1)} %add.58.own_ref), channel_id=1, source_target_pairs={{0,1},{1,0},{2,3},{3,2},{4,5},{5,4},{6,7},{7,6},{8,9},{9,8},{10,11... | collective-permute-start | bytes 430088 | tf_op jit(solution)/shard_map/ppermute | solution.py:417
  26.2 4.8 %collective-permute-start.7 = (f32[280,128]{1,0:T(8,128)S(1)}, f32[280,128]{1,0:T(8,128)S(1)}, u32[]{:S(2)}, u32[]{:S(2)}) collective-permute-start(f32[280,128]{1,0:T(8,128)S(1)} %add.58.own_ref), channel_id=1, source_target_pairs={{0,4},{1,5},{2,6},{3,7},{4,0},{5,1},{6,2},{7,3},{8,12},{9,13},{10,... | collective-permute-start | bytes 430088 | tf_op jit(solution)/shard_map/ppermute | solution.py:417
  27.5 4.8 %collective-permute-start.8 = (f32[280,128]{1,0:T(8,128)S(1)}, f32[280,128]{1,0:T(8,128)S(1)}, u32[]{:S(2)}, u32[]{:S(2)}) collective-permute-start(f32[280,128]{1,0:T(8,128)S(1)} %add.58.own_ref), channel_id=1, source_target_pairs={{0,5},{1,4},{2,7},{3,6},{4,1},{5,0},{6,3},{7,2},{8,13},{9,12},{10,... | collective-permute-start | bytes 430088 | tf_op jit(solution)/shard_map/ppermute | solution.py:417
  36.3 7.4 %collective-permute-start.9 = (f32[64,576]{1,0:T(8,128)S(1)}, f32[64,576]{1,0:T(8,128)S(1)}, u32[]{:S(2)}, u32[]{:S(2)}) collective-permute-start(f32[64,576]{1,0:T(8,128)S(1)} %shard_map.30), channel_id=1, source_target_pairs={{0,2},{1,3},{2,0},{3,1},{4,6},{5,7},{6,4},{7,5},{8,10},{9,11},{10,... | collective-permute-start | bytes 442376 | tf_op jit(solution)/shard_map/ppermute | solution.py:417
  42.7 1.0 %copy-start = (f32[2,64,576]{2,1,0:T(8,128)}, f32[2,64,576]{2,1,0:T(8,128)S(1)}, u32[]{:S(2)}) copy-start(f32[2,64,576]{2,1,0:T(8,128)S(1)} %bitcast_dynamic-update-slice_fusion.1) | copy-start | bytes 884740
